TPU v7x, 512 devices: a whole 4x8x8 slice. The times are simulated.
512 devices in a mesh: blk: 64 (over x, z_hi, y), head: 8 (over z_lo, core).
Axes of the slice: x: 4, y: 8, z: 8 (z_hi: 2, z_lo: 4; z = z_hi * 4 + z_lo), core: 2. Of those that a mesh axis runs over, the one named last changes fastest.
Arguments:
- queries: bfloat16 [65536, 2048], P(('blk', 'head')), may hold values from -4.7 to 4.7
- keys: bfloat16 [65536, 2048], P(('blk', 'head')), may hold values from -4.7 to 4.7
- values: bfloat16 [65536, 2048], P(('blk', 'head')), may hold values from -5 to 5
- w_out: bfloat16 [2048, 1600], P('head', 'blk'), may hold values from -1.5 to 1.5
Outputs:
- projected: bfloat16 [65536, 1600], P(('blk', 'head'))
All inputs are finite; a program needn't handle non-finite values.
Results may differ from a plain program's by a relative error of at most 0.0075.
Values may be sent and summed in bfloat16 or wider, within the bound.
No kernel may reach another device: no remote copies, remote signals or barrier semaphores. Data moves between devices by JAX's collectives and lax.ppermute only.
A program may use at most 64 MiB of HBM per device.

v0:
```python
import math

import jax
import jax.numpy as jnp
from jax import lax
from jax.sharding import PartitionSpec as P

HDIM = 128


def extended(value, sides, width):
    for axis, dim in sides:
        count, length = (lax.axis_size(axis), value.shape[dim])
        up = [(i, (i + 1) % count) for i in range(count - 1)]
        down = [(j, i) for i, j in up]
        last = lax.slice_in_dim(value, length - width, length, axis=dim)
        initial = lax.slice_in_dim(value, 0, width, axis=dim)
        before = lax.ppermute(last, axis, up)
        after = lax.ppermute(initial, axis, down)
        value = jnp.concatenate([before, value, after], axis=dim)
    return value


def attend_rows(query_rows, near_keys, near_values, key_ok):
    scores = jnp.einsum(
        "qhd,khd->hqk", query_rows, near_keys, preferred_element_type=jnp.float32
    ) * HDIM ** (-0.5)
    scores = jnp.where(key_ok[None, None, :], scores, -1e30)
    largest = jnp.max(scores, axis=2, keepdims=True)
    raised = jnp.exp(scores - largest)
    totals = jnp.sum(raised, axis=2)
    weighted = jnp.einsum(
        "hqk,khd->qhd", raised.astype(jnp.bfloat16), near_values, preferred_element_type=jnp.float32
    )
    return (weighted / jnp.transpose(totals)[:, :, None]).astype(jnp.bfloat16)


def local(queries, keys, values, w_out):
    moved_q, moved_k, moved_v = (
        lax.all_to_all(queries, "head", split_axis=1, concat_axis=0, tiled=True),
        lax.all_to_all(keys, "head", split_axis=1, concat_axis=0, tiled=True),
        lax.all_to_all(values, "head", split_axis=1, concat_axis=0, tiled=True),
    )
    block_len, width = moved_q.shape
    group_heads = width // HDIM
    stacked = jnp.stack((moved_k, moved_v))
    nearby = extended(stacked, (("blk", 1),), block_len)
    span = 3 * block_len
    near_keys = nearby[0].reshape(span, group_heads, HDIM)
    near_values = nearby[1].reshape(span, group_heads, HDIM)
    position = lax.axis_index("blk")
    count = lax.axis_size("blk")
    owner = position - 1 + jnp.arange(span, dtype=jnp.int32) // block_len
    key_ok = (owner >= 0) & (owner < count)
    step_rows = math.gcd(block_len, 512)
    grouped = moved_q.reshape(block_len // step_rows, step_rows, group_heads, HDIM)

    def attend_step(query_rows):
        return attend_rows(query_rows, near_keys, near_values, key_ok)

    context = lax.map(attend_step, grouped).reshape(block_len, width)
    own_rows = lax.all_to_all(context, "head", split_axis=0, concat_axis=1, tiled=True)
    full_rows = lax.all_gather(w_out, "head", axis=0, tiled=True)
    head_groups = lax.axis_size("head")
    tok_rows = own_rows.shape[0]
    split_context = own_rows.reshape(tok_rows, head_groups, width)
    weight_cols = lax.all_gather(full_rows, "blk", axis=1, tiled=True)
    split_weight = weight_cols.reshape(head_groups, width, weight_cols.shape[1])
    partials = jnp.einsum(
        "tgw,gwc->gtc", split_context, split_weight, preferred_element_type=jnp.float32
    )
    rounded = lax.optimization_barrier(partials.astype(jnp.bfloat16))
    summed = jnp.sum(rounded.astype(jnp.float32), axis=0)
    return summed.astype(jnp.bfloat16)


def solution(mesh):
    return jax.shard_map(
        local,
        mesh=mesh,
        in_specs=(
            P(("blk", "head"), None),
            P(("blk", "head"), None),
            P(("blk", "head"), None),
            P("head", "blk"),
        ),
        out_specs=P(("blk", "head"), None),
        check_vma=False,
    )
```

profile of v0, /device:TPU:6, one launch (start us, length us, event | category | flops | bytes accessed | tf_op | source)
XLA Modules:
  0.0 307.0 jit_solution(12091563614848608013)
XLA Ops:
  6.5 17.6 %all_gather.6 = bf16[2048,25]{0,1:T(8,128)(2,1)} all-gather(bf16[256,25]{0,1:T(8,128)(2,1)} %param.9), channel_id=1, replica_groups=mesh['blk'=64,'head'=8] {'head'}, dimensions={0}, use_global_device_ids=true | all-gather | bytes 115200 | tf_op jit(solution)/shard_map/all_gather | solution.py:63
  24.1 2.1 copy.27
  26.2 5.0 %all-to-all-start.1 = ((bf16[128,8,256]{0,2,1:T(8,128)(2,1)}), bf16[128,8,256]{0,2,1:T(8,128)(2,1)S(1)}, u32[]{:S(2)}, u32[]{:S(2)}) async-start(bf16[128,8,256]{0,2,1:T(8,128)(2,1)} %bitcast.1), calls=%async_computation.1 | async-start | bytes 1048576 | tf_op jit(solution)/shard_map/all_to_all | solution.py:41
  31.3 2.1 copy.29
  33.4 13.4 %all-to-all-done.1 = bf16[128,8,256]{0,2,1:T(8,128)(2,1)S(1)} async-done(((bf16[128,8,256]{0,2,1:T(8,128)(2,1)}), bf16[128,8,256]{0,2,1:T(8,128)(2,1)S(1)}, u32[]{:S(2)}, u32[]{:S(2)}) %all-to-all-start.1) | async-done | bytes 524320 | tf_op jit(solution)/shard_map/all_to_all | solution.py:41
  46.7 3.5 %all-to-all-start.2 = ((bf16[128,8,256]{0,2,1:T(8,128)(2,1)}), bf16[128,8,256]{0,2,1:T(8,128)(2,1)S(1)}, u32[]{:S(2)}, u32[]{:S(2)}) async-start(bf16[128,8,256]{0,2,1:T(8,128)(2,1)} %bitcast.4), calls=%async_computation.2 | async-start | bytes 1048576 | tf_op jit(solution)/shard_map/all_to_all | solution.py:42
  50.4 15.1 %all-to-all-done.2 = bf16[128,8,256]{0,2,1:T(8,128)(2,1)S(1)} async-done(((bf16[128,8,256]{0,2,1:T(8,128)(2,1)}), bf16[128,8,256]{0,2,1:T(8,128)(2,1)S(1)}, u32[]{:S(2)}, u32[]{:S(2)}) %all-to-all-start.2) | async-done | bytes 524320 | tf_op jit(solution)/shard_map/all_to_all | solution.py:42
  65.8 3.5 %collective-permute-start = (bf16[2,1024,256]{2,1,0:T(8,128)(2,1)S(1)}, bf16[2,1024,256]{2,1,0:T(8,128)(2,1)}, u32[]{:S(2)}, u32[]{:S(2)}) collective-permute-start(bf16[2,1024,256]{2,1,0:T(8,128)(2,1)S(1)} %pad_maximum_fusion.1), channel_id=1, source_target_pairs={{0,8},{8,16},{16,24},{24,32},{32,40},{40,48},{48,56},{56,64},{64,7... | collective-permute-start | bytes 3145736 | tf_op jit(solution)/shard_map/ppermute | solution.py:18
  69.4 11.5 %collective-permute-start.1 = (bf16[2,1024,256]{2,1,0:T(8,128)(2,1)S(1)}, bf16[2,1024,256]{2,1,0:T(8,128)(2,1)}, u32[]{:S(2)}, u32[]{:S(2)}) collective-permute-start(bf16[2,1024,256]{2,1,0:T(8,128)(2,1)S(1)} %pad_maximum_fusion.1), channel_id=1, source_target_pairs={{8,0},{16,8},{24,16},{32,24},{40,32},{48,40},{56,48},{64,56},{72,6... | collective-permute-start | bytes 3145736 | tf_op jit(solution)/shard_map/ppermute | solution.py:19
  80.9 1.9 copy.56
  82.8 3.7 %all-to-all-start = ((bf16[128,8,256]{2,0,1:T(8,128)(2,1)}), bf16[128,8,256]{2,0,1:T(8,128)(2,1)S(1)}, u32[]{:S(2)}, u32[]{:S(2)}) async-start(bf16[128,8,256]{2,0,1:T(8,128)(2,1)} %bitcast.43), calls=%async_computation | async-start | bytes 1048576 | tf_op jit(solution)/shard_map/all_to_all | solution.py:40
  86.5 54.4 %all-to-all-done = bf16[128,8,256]{2,0,1:T(8,128)(2,1)S(1)} async-done(((bf16[128,8,256]{2,0,1:T(8,128)(2,1)}), bf16[128,8,256]{2,0,1:T(8,128)(2,1)S(1)}, u32[]{:S(2)}, u32[]{:S(2)}) %all-to-all-start) | async-done | bytes 524320 | tf_op jit(solution)/shard_map/all_to_all | solution.py:40
  141.0 1.8 pad_maximum_fusion
  142.9 1.4 fusion.37
  144.3 1.7 copy.31
  146.0 1.9 copy.34
  147.9 2.6 copy.32
  150.5 2.6 copy.35
  153.2 19.2 %while.11 = (s32[]{:T(128)}, bf16[2,512,2,128]{3,2,1,0:T(2,128)(2,1)S(1)}, bf16[2,512,2,128]{3,2,1,0:T(2,128)(2,1)S(1)}, bf16[3072,2,128]{2,0,1:T(8,128)(2,1)S(1...) while((s32[]{:T(128)}, bf16[2,512,2,128]{3,2,1,0:T(2,128)(2,1)S(1)}, ...), condition=%wide.region_3.4_spmd.clone, body=%wide.region_0.3_spmd.clone.sunk | while | flops 1645512704 | bytes 42500184 | solution.py:61
  153.4 2.2 fusion.51
  155.6 2.7 fusion.52
  158.3 4.1 %fusion.53 = bf16[1,512,2,128]{3,1,2,0:T(8,128)(2,1)S(1)} fusion(bf16[3072,2,128]{2,0,1:T(8,128)(2,1)} %get-tuple-element.146, f32[2,512,3072]{2,1,0:T(8,128)S(1)} %get-tuple-element.126, f32[2,512]{1,0:T(2,128)S(1)} %get-tuple-element.127, pred[3072]{0:T(1024)(128)(4,1)S(1)} %fusion.50, f32[512,2]{0,1:T(2,128)S(1)} %bitcast.68), kind=kOutput, calls=%fused_computation.11.clone.1 | convolution fusion | flops 818151424 | bytes 14429184 | tf_op jit(solution)/shard_map/while/body/eval_jaxpr/hqk,khd->qhd/dot_general | solution.py:32
  163.0 2.2 fusion.51
  165.2 2.7 fusion.52
  167.9 4.1 %fusion.53 = bf16[1,512,2,128]{3,1,2,0:T(8,128)(2,1)S(1)} fusion(bf16[3072,2,128]{2,0,1:T(8,128)(2,1)} %get-tuple-element.146, f32[2,512,3072]{2,1,0:T(8,128)S(1)} %get-tuple-element.126, f32[2,512]{1,0:T(2,128)S(1)} %get-tuple-element.127, pred[3072]{0:T(1024)(128)(4,1)S(1)} %fusion.50, f32[512,2]{0,1:T(2,128)S(1)} %bitcast.68), kind=kOutput, calls=%fused_computation.11.clone.1 | convolution fusion | flops 818151424 | bytes 14429184 | tf_op jit(solution)/shard_map/while/body/eval_jaxpr/hqk,khd->qhd/dot_general | solution.py:32
  172.3 1.1 all_to_all.57
  173.5 3.7 %all-to-all-start.3 = ((bf16[8,128,256]{2,1,0:T(8,128)(2,1)}), bf16[8,128,256]{2,1,0:T(8,128)(2,1)S(1)}, u32[]{:S(2)}, u32[]{:S(2)}) async-start(bf16[8,128,256]{2,1,0:T(8,128)(2,1)} %all_to_all.57), calls=%async_computation.3 | async-start | bytes 1048576 | tf_op jit(solution)/shard_map/all_to_all | solution.py:62
  177.2 106.7 %all-gather.3.cloned.1.call-done = bf16[64,25,2048]{2,1,0:T(8,128)(2,1)} async-done(((bf16[1,25,2048]{2,1,0:T(8,128)(2,1)}), bf16[64,25,2048]{2,1,0:T(8,128)(2,1)}) %all-gather.3.cloned.1.call-update) | async-done | bytes 6553616 | tf_op jit(solution)/shard_map/all_gather | solution.py:67
  283.9 9.2 %reshape.31 = bf16[1600,2048]{1,0:T(8,128)(2,1)} reshape(bf16[64,25,2048]{2,1,0:T(8,128)(2,1)} %all-gather.3.cloned.1.call-done) | data formatting | bytes 13107200
  293.1 0.8 copy-done.1
  293.9 4.9 %fusion.33 = bf16[8,128,1600]{1,2,0:T(8,128)(2,1)S(1)} fusion(bf16[200,8,8,256]{3,2,1,0:T(8,128)(2,1)} %bitcast.56, bf16[8,128,256]{2,1,0:T(8,128)(2,1)} %copy-done.1), kind=kOutput, calls=%fused_computation.32 | convolution fusion | flops 840499200 | bytes 10354688 | tf_op jit(solution)/shard_map/tgw,gwc->gtc/dot_general | solution.py:69
  298.8 1.3 reduce_sum.21
  (19 shorter events, 1.7 us)
Async XLA Ops:
  6.5 277.4 %all-gather.3.cloned.1.call-start = ((), (), s32[]{:S(2)}) async-start(), calls=%async_computation.4 | async-start | bytes 8519680 | tf_op jit(solution)/shard_map/all_gather | solution.py:67
  26.2 20.5 %all-to-all-start.1 = ((bf16[128,8,256]{0,2,1:T(8,128)(2,1)}), bf16[128,8,256]{0,2,1:T(8,128)(2,1)S(1)}, u32[]{:S(2)}, u32[]{:S(2)}) async-start(bf16[128,8,256]{0,2,1:T(8,128)(2,1)} %bitcast.1), calls=%async_computation.1 | async-start | bytes 1048576 | tf_op jit(solution)/shard_map/all_to_all | solution.py:41
  46.7 18.8 %all-to-all-start.2 = ((bf16[128,8,256]{0,2,1:T(8,128)(2,1)}), bf16[128,8,256]{0,2,1:T(8,128)(2,1)S(1)}, u32[]{:S(2)}, u32[]{:S(2)}) async-start(bf16[128,8,256]{0,2,1:T(8,128)(2,1)} %bitcast.4), calls=%async_computation.2 | async-start | bytes 1048576 | tf_op jit(solution)/shard_map/all_to_all | solution.py:42
  65.8 75.2 %collective-permute-start = (bf16[2,1024,256]{2,1,0:T(8,128)(2,1)S(1)}, bf16[2,1024,256]{2,1,0:T(8,128)(2,1)}, u32[]{:S(2)}, u32[]{:S(2)}) collective-permute-start(bf16[2,1024,256]{2,1,0:T(8,128)(2,1)S(1)} %pad_maximum_fusion.1), channel_id=1, source_target_pairs={{0,8},{8,16},{16,24},{24,32},{32,40},{40,48},{48,56},{56,64},{64,7... | collective-permute-start | bytes 3145736 | tf_op jit(solution)/shard_map/ppermute | solution.py:18
  69.4 71.7 %collective-permute-start.1 = (bf16[2,1024,256]{2,1,0:T(8,128)(2,1)S(1)}, bf16[2,1024,256]{2,1,0:T(8,128)(2,1)}, u32[]{:S(2)}, u32[]{:S(2)}) collective-permute-start(bf16[2,1024,256]{2,1,0:T(8,128)(2,1)S(1)} %pad_maximum_fusion.1), channel_id=1, source_target_pairs={{8,0},{16,8},{24,16},{32,24},{40,32},{48,40},{56,48},{64,56},{72,6... | collective-permute-start | bytes 3145736 | tf_op jit(solution)/shard_map/ppermute | solution.py:19
  82.8 58.1 %all-to-all-start = ((bf16[128,8,256]{2,0,1:T(8,128)(2,1)}), bf16[128,8,256]{2,0,1:T(8,128)(2,1)S(1)}, u32[]{:S(2)}, u32[]{:S(2)}) async-start(bf16[128,8,256]{2,0,1:T(8,128)(2,1)} %bitcast.43), calls=%async_computation | async-start | bytes 1048576 | tf_op jit(solution)/shard_map/all_to_all | solution.py:40
  144.3 8.9 %copy-start = (bf16[2,512,2,128]{3,2,1,0:T(2,128)(2,1)S(1)}, bf16[2,512,2,128]{3,2,1,0:T(2,128)(2,1)}, u32[]{:S(2)}) copy-start(bf16[2,512,2,128]{3,2,1,0:T(2,128)(2,1)} %custom-call) | copy-start | bytes 1572868
  173.5 119.6 %all-to-all-start.3 = ((bf16[8,128,256]{2,1,0:T(8,128)(2,1)}), bf16[8,128,256]{2,1,0:T(8,128)(2,1)S(1)}, u32[]{:S(2)}, u32[]{:S(2)}) async-start(bf16[8,128,256]{2,1,0:T(8,128)(2,1)} %all_to_all.57), calls=%async_computation.3 | async-start | bytes 1048576 | tf_op jit(solution)/shard_map/all_to_all | solution.py:62
  293.1 0.8 copy-start.1
Sparse Core Ops, SparseCore 0:
  24.3 259.6 all-gather.2
where the time goes:
time: 308 us; the launch traced here: 307 us
  waiting for transfers between devices  190 us (62%)
  starting transfers between devices  30.9 us (10%)
  local copies, waits for them, and re-layouts  28.9 us (9%)
  blocking collectives  17.6 us (6%)
  matrix products  17.6 us (6%)
  between operations  13.5 us (4%)
  other arithmetic  8.75 us (3%)
    all_gather x1, waiting for transfers between devices, local(): weight_cols = lax.all_gather(full_rows, 'blk', axis=1, tiled=True)  107 us
    all_to_all x1, waiting for transfers between devices, local(): lax.all_to_all(queries, 'head', split_axis=1, concat_axis=0, tiled=True)  54.4 us
    unnamed x9, local copies, waits for them, and re-layouts  18.7 us
    all_gather x1, blocking collectives, local(): full_rows = lax.all_gather(w_out, 'head', axis=0, tiled=True)  17.6 us
    all_to_all x1, waiting for transfers between devices, local(): lax.all_to_all(values, 'head', split_axis=1, concat_axis=0, tiled=True)  15.1 us
    all_to_all x1, waiting for transfers between devices, local(): lax.all_to_all(keys, 'head', split_axis=1, concat_axis=0, tiled=True)  13.4 us
    ppermute x1, starting transfers between devices, extended(): after = lax.ppermute(initial, axis, down)  11.5 us
    dot_general x2, matrix products, attend_rows(): jnp.einsum('hqk,khd->qhd', raised.astype(jnp.bfloat16), near_values, pref...  8.25 us
  transfers between devices with their start and end apart: 7, of which 4 were waited for; matrix products, arithmetic and copies ran while one was open for 15% of the time, Pallas kernels for 0%

commit v1 on v0

v1 whole, which is shorter than its diff:
```python
import functools
import math

import jax
import jax.numpy as jnp
from jax import lax
from jax.experimental import pallas as pl
from jax.experimental.pallas import tpu as pltpu
from jax.sharding import Mesh, PartitionSpec as P

HDIM = 128
LOG2E = 1.4426950408889634
FACTOR = LOG2E / math.sqrt(HDIM)
AXES = ("x", "zh", "y", "zl", "c")
SIZES = (4, 2, 8, 4, 2)
BLK = ("x", "zh", "y")
HEAD = ("zl", "c")
TILE = 256
DIMS_NT = (((1,), (1,)), ((), ()))
DIMS_TN = (((0,), (0,)), ((), ()))
VMEM = 48 * 1024 * 1024


def own_kernel(q_ref, k_ref, v_ref, acc_ref, m_ref, l_ref):
    scores = lax.dot_general(k_ref[...], q_ref[...], DIMS_NT, preferred_element_type=jnp.float32)
    largest = jnp.max(scores, axis=0, keepdims=True) * FACTOR
    raised = jnp.exp2(scores * FACTOR - largest)
    m_ref[0] = jnp.broadcast_to(largest, m_ref.shape[1:])
    l_ref[0] = jnp.broadcast_to(jnp.sum(raised, axis=0, keepdims=True), l_ref.shape[1:])
    acc_ref[0] = lax.dot_general(
        v_ref[...], raised.astype(jnp.bfloat16), DIMS_TN, preferred_element_type=jnp.float32
    )


def own_attention(q, k, v):
    rows, width = q.shape
    heads = width // HDIM
    return pl.pallas_call(
        own_kernel,
        grid=(heads, rows // TILE),
        in_specs=[
            pl.BlockSpec((TILE, HDIM), lambda h, i: (i, h)),
            pl.BlockSpec((rows, HDIM), lambda h, i: (0, h)),
            pl.BlockSpec((rows, HDIM), lambda h, i: (0, h)),
        ],
        out_specs=[
            pl.BlockSpec((1, HDIM, TILE), lambda h, i: (h, 0, i)),
            pl.BlockSpec((1, 8, TILE), lambda h, i: (h, 0, i)),
            pl.BlockSpec((1, 8, TILE), lambda h, i: (h, 0, i)),
        ],
        out_shape=[
            jax.ShapeDtypeStruct((heads, HDIM, rows), jnp.float32),
            jax.ShapeDtypeStruct((heads, 8, rows), jnp.float32),
            jax.ShapeDtypeStruct((heads, 8, rows), jnp.float32),
        ],
        compiler_params=pltpu.CompilerParams(vmem_limit_bytes=VMEM),
        cost_estimate=pl.CostEstimate(
            flops=4 * rows * rows * width, bytes_accessed=6 * rows * width, transcendentals=rows * rows * heads
        ),
        name="own_attention",
    )(q, k, v)


def near_kernel(ok_ref, q_ref, kp_ref, vp_ref, kn_ref, vn_ref, acc_ref, m_ref, l_ref, out_ref):
    far = jnp.float32(1e30)
    q = q_ref[...]
    m = m_ref[0][:1]
    sides = ((kp_ref, vp_ref, ok_ref[0] > 0), (kn_ref, vn_ref, ok_ref[1] > 0))
    scores = []
    for k_ref, _, ok in sides:
        s = lax.dot_general(k_ref[...], q, DIMS_NT, preferred_element_type=jnp.float32)
        scores.append(s)
        m = jnp.maximum(m, jnp.where(ok, jnp.max(s, axis=0, keepdims=True) * FACTOR, -far))
    alpha = jnp.exp2(m_ref[0][:1] - m)
    total = l_ref[0][:1] * alpha
    acc = acc_ref[0] * alpha
    for s, (_, v_ref, ok) in zip(scores, sides):
        raised = jnp.exp2(s * FACTOR - jnp.where(ok, m, far))
        total += jnp.sum(raised, axis=0, keepdims=True)
        acc += lax.dot_general(
            v_ref[...], raised.astype(jnp.bfloat16), DIMS_TN, preferred_element_type=jnp.float32
        )
    result = (acc / total).astype(jnp.bfloat16)
    tok = out_ref.shape[2]
    for part in range(out_ref.shape[0]):
        out_ref[part] = result[:, part * tok : (part + 1) * tok]


def near_attention(ok, q, kp, vp, kn, vn, acc, m, l, tok):
    rows, width = q.shape
    heads = width // HDIM
    side = pl.BlockSpec((rows, HDIM), lambda h, i: (0, h))
    row = pl.BlockSpec((1, 8, TILE), lambda h, i: (h, 0, i))
    return pl.pallas_call(
        near_kernel,
        grid=(heads, rows // TILE),
        in_specs=[
            pl.BlockSpec(memory_space=pltpu.SMEM),
            pl.BlockSpec((TILE, HDIM), lambda h, i: (i, h)),
            side,
            side,
            side,
            side,
            pl.BlockSpec((1, HDIM, TILE), lambda h, i: (h, 0, i)),
            row,
            row,
        ],
        out_specs=pl.BlockSpec((TILE // tok, HDIM, tok), lambda h, i: (i, h, 0)),
        out_shape=jax.ShapeDtypeStruct((rows // tok, width, tok), jnp.bfloat16),
        compiler_params=pltpu.CompilerParams(vmem_limit_bytes=VMEM),
        cost_estimate=pl.CostEstimate(
            flops=8 * rows * rows * width, bytes_accessed=14 * rows * width, transcendentals=2 * rows * rows * heads
        ),
        name="near_attention",
    )(ok, q, kp, vp, kn, vn, acc, m, l)


def project_kernel(w_ref, ctx_ref, out_ref):
    total = None
    for c in range(w_ref.shape[1]):
        part = jnp.dot(w_ref[0, c], ctx_ref[c], preferred_element_type=jnp.float32)
        total = part if total is None else total + part
    out_ref[...] = total.astype(jnp.bfloat16)


def project(w, ctx):
    parts, cores, rows, depth = w.shape
    tok = ctx.shape[2]
    return pl.pallas_call(
        project_kernel,
        grid=(parts,),
        in_specs=[
            pl.BlockSpec((1, cores, rows, depth), lambda i: (i, 0, 0, 0)),
            pl.BlockSpec((cores, depth, tok), lambda i: (0, 0, 0)),
        ],
        out_specs=pl.BlockSpec((rows, tok), lambda i: (i, 0)),
        out_shape=jax.ShapeDtypeStruct((parts * rows, tok), jnp.bfloat16),
        compiler_params=pltpu.CompilerParams(vmem_limit_bytes=VMEM),
        cost_estimate=pl.CostEstimate(
            flops=2 * parts * rows * depth * cores * tok, bytes_accessed=2 * parts * rows * depth * cores, transcendentals=0
        ),
        name="project",
    )(w, ctx)


def head_split(value):
    tok = value.shape[0]
    chunks = value.reshape(tok, 8, -1).transpose(1, 0, 2)
    moved = lax.all_to_all(chunks, HEAD, split_axis=0, concat_axis=0)
    return moved.reshape(8 * tok, -1)


def gather_w(w):
    wt = w.T
    cols, depth = wt.shape
    a = lax.all_gather(wt, ("zh", "zl"))
    a = a.reshape(2, 4, cols, depth).transpose(0, 2, 1, 3).reshape(2 * cols, 4 * depth)
    b = lax.all_gather(a, "y")
    b = b.reshape(8, 2, cols, 4 * depth).transpose(1, 0, 2, 3).reshape(16 * cols, 4 * depth)
    return lax.all_gather(b, ("x", "c")).reshape(4, 2, 16 * cols, 4 * depth)


def local(queries, keys, values, w_out):
    tok = queries.shape[0]
    weight = gather_w(w_out)
    k = head_split(keys)
    v = head_split(values)
    q = head_split(queries)
    n_blk = 64
    up = [(i, i + 1) for i in range(n_blk - 1)]
    down = [(i + 1, i) for i in range(n_blk - 1)]
    kp, kn = lax.ppermute(k, BLK, up), lax.ppermute(k, BLK, down)
    vp, vn = lax.ppermute(v, BLK, up), lax.ppermute(v, BLK, down)
    here = lax.axis_index(BLK)
    ok = jnp.stack([here > 0, here < n_blk - 1]).astype(jnp.int32)
    acc, m, l = own_attention(q, k, v)
    ctx = near_attention(ok, q, kp, vp, kn, vn, acc, m, l, tok)
    moved = lax.all_to_all(ctx, HEAD, split_axis=0, concat_axis=0)
    width = moved.shape[1]
    by_core = moved.reshape(4, 2, width, tok).transpose(1, 0, 2, 3).reshape(2, 4 * width, tok)
    return project(weight, by_core).T


def solution(mesh):
    cut = Mesh(mesh.devices.reshape(SIZES), AXES)
    return jax.shard_map(
        local,
        mesh=cut,
        in_specs=(P(AXES, None), P(AXES, None), P(AXES, None), P(HEAD, BLK)),
        out_specs=P(AXES, None),
        check_vma=False,
    )
```

time: 308 us -> 223 us (0.72)
  the two profiles are of different devices: /device:TPU:6 before, /device:TPU:1 now
where the time goes in v1:
time: 223 us; the launch traced here: 222 us
  waiting for transfers between devices  79.3 us (36%)
  blocking collectives  68 us (30%)
  starting transfers between devices  32.1 us (14%)
  Pallas kernels  24.6 us (11%)
  between operations  13.5 us (6%)
  local copies, waits for them, and re-layouts  4.84 us (2%)
    all_to_all x3, waiting for transfers between devices, head_split(): moved = lax.all_to_all(chunks, HEAD, split_axis=0, concat_axis=0)  79.3 us
    all_gather x1, blocking collectives, gather_w(): a = lax.all_gather(wt, ('zh', 'zl'))  26 us
    all_to_all x3, starting transfers between devices, head_split(): moved = lax.all_to_all(chunks, HEAD, split_axis=0, concat_axis=0)  23.9 us
    all_gather x1, blocking collectives, gather_w(): b = lax.all_gather(a, 'y')  22.5 us
    all_to_all x1, blocking collectives, local(): moved = lax.all_to_all(ctx, HEAD, split_axis=0, concat_axis=0)  19.4 us
    pallas_call x1, Pallas kernels, near_attention(): pl.pallas_call(near_kernel, grid=(heads, rows // TILE), in_specs=[pl.Bloc...  12 us
    pallas_call x1, Pallas kernels, own_attention(): pl.pallas_call(own_kernel, grid=(heads, rows // TILE), in_specs=[pl.Block...  7.09 us
    pallas_call x1, Pallas kernels, project(): pl.pallas_call(project_kernel, grid=(parts,), in_specs=[pl.BlockSpec((1,...  5.48 us
  transfers between devices with their start and end apart: 8, of which 3 were waited for; matrix products, arithmetic and copies ran while one was open for 1% of the time, Pallas kernels for 9%

profile of v1, /device:TPU:1, one launch (start us, length us, event | category | flops | bytes accessed | tf_op | source)
XLA Modules:
  0.0 222.5 jit_solution(13592680866276120643)
XLA Ops:
  6.5 0.0 all-gather.4.cloned.1.call-start
  6.5 26.0 %all-gather.1 = bf16[8,25,256]{2,1,0:T(8,128)(2,1)S(1)} all-gather(bf16[1,25,256]{2,1,0:T(8,128)(2,1)} %bitcast.59), channel_id=2, replica_groups=mesh['x'=4,'zh'=2,'y'=8,'zl'=4,'c'=2] {'zh','zl'}, dimensions={0}, use_global_device_ids=true | all-gather | bytes 115200 | tf_op jit(solution)/shard_map/all_gather | solution.py:156
  32.6 0.1 copy.33
  32.7 22.5 %all_gather.14 = bf16[8,50,1024]{2,1,0:T(8,128)(2,1)S(1)} all-gather(bf16[1,50,1024]{2,1,0:T(8,128)(2,1)S(1)} %all_gather_reshape.6), channel_id=1, replica_groups=mesh['x'=4,'zh'=2,'y'=8,'zl'=4,'c'=2] {'y'}, dimensions={0}, use_global_device_ids=true | all-gather | bytes 921600 | tf_op jit(solution)/shard_map/all_gather | solution.py:158
  55.2 0.5 copy.17
  55.7 0.5 copy.18
  56.1 1.2 all_gather_reshape.7
  57.3 0.0 all-gather.4.cloned.1.call-update
  57.3 0.8 copy.31
  58.2 15.6 %all-to-all-start.1 = ((bf16[8,128,256]{2,1,0:T(8,128)(2,1)}), bf16[8,128,256]{2,1,0:T(8,128)(2,1)S(1)}, u32[]{:S(2)}, u32[]{:S(2)}) async-start(bf16[8,128,256]{2,1,0:T(8,128)(2,1)} %bitcast.38), calls=%async_computation.1 | async-start | bytes 1048576 | tf_op jit(solution)/shard_map/all_to_all | solution.py:149
  73.8 0.9 copy.30
  74.7 13.7 %all-to-all-done.1 = bf16[8,128,256]{2,1,0:T(8,128)(2,1)S(1)} async-done(((bf16[8,128,256]{2,1,0:T(8,128)(2,1)}), bf16[8,128,256]{2,1,0:T(8,128)(2,1)S(1)}, u32[]{:S(2)}, u32[]{:S(2)}) %all-to-all-start.1) | async-done | bytes 524320 | tf_op jit(solution)/shard_map/all_to_all | solution.py:149
  88.4 4.2 %all-to-all-start.2 = ((bf16[8,128,256]{2,1,0:T(8,128)(2,1)}), bf16[8,128,256]{2,1,0:T(8,128)(2,1)S(1)}, u32[]{:S(2)}, u32[]{:S(2)}) async-start(bf16[8,128,256]{2,1,0:T(8,128)(2,1)} %bitcast.36), calls=%async_computation.2 | async-start | bytes 1048576 | tf_op jit(solution)/shard_map/all_to_all | solution.py:149
  92.6 0.0 copy-done.2
  92.6 0.8 copy.32
  93.4 13.8 %all-to-all-done.2 = bf16[8,128,256]{2,1,0:T(8,128)(2,1)S(1)} async-done(((bf16[8,128,256]{2,1,0:T(8,128)(2,1)}), bf16[8,128,256]{2,1,0:T(8,128)(2,1)S(1)}, u32[]{:S(2)}, u32[]{:S(2)}) %all-to-all-start.2) | async-done | bytes 524320 | tf_op jit(solution)/shard_map/all_to_all | solution.py:149
  107.2 4.2 %all-to-all-start = ((bf16[8,128,256]{2,1,0:T(8,128)(2,1)}), bf16[8,128,256]{2,1,0:T(8,128)(2,1)S(1)}, u32[]{:S(2)}, u32[]{:S(2)}) async-start(bf16[8,128,256]{2,1,0:T(8,128)(2,1)} %bitcast.40), calls=%async_computation | async-start | bytes 1048576 | tf_op jit(solution)/shard_map/all_to_all | solution.py:149
  111.4 2.4 %collective-permute-start = (bf16[1024,256]{1,0:T(8,128)(2,1)S(1)}, bf16[1024,256]{1,0:T(8,128)(2,1)S(1)}, u32[]{:S(2)}, u32[]{:S(2)}) collective-permute-start(bf16[1024,256]{1,0:T(8,128)(2,1)S(1)} %bitcast.43), channel_id=1, source_target_pairs={{0,8},{8,16},{16,24},{24,32},{32,40},{40,48},{48,56},{56,64},{64,7... | collective-permute-start | bytes 1572872 | tf_op jit(solution)/shard_map/ppermute | solution.py:172
  113.8 3.2 %collective-permute-start.1 = (bf16[1024,256]{1,0:T(8,128)(2,1)S(1)}, bf16[1024,256]{1,0:T(8,128)(2,1)S(1)}, u32[]{:S(2)}, u32[]{:S(2)}) collective-permute-start(bf16[1024,256]{1,0:T(8,128)(2,1)S(1)} %bitcast.46), channel_id=1, source_target_pairs={{0,8},{8,16},{16,24},{24,32},{32,40},{40,48},{48,56},{56,64},{64,7... | collective-permute-start | bytes 1572872 | tf_op jit(solution)/shard_map/ppermute | solution.py:173
  117.0 1.3 collective-permute-start.2
  118.3 1.3 collective-permute-start.3
  119.6 0.1 add_convert_fusion.ok_ref
  119.6 51.8 %all-to-all-done = bf16[8,128,256]{2,1,0:T(8,128)(2,1)S(1)} async-done(((bf16[8,128,256]{2,1,0:T(8,128)(2,1)}), bf16[8,128,256]{2,1,0:T(8,128)(2,1)S(1)}, u32[]{:S(2)}, u32[]{:S(2)}) %all-to-all-start) | async-done | bytes 524320 | tf_op jit(solution)/shard_map/all_to_all | solution.py:149
  171.4 7.1 %own_attention.1 = (f32[2,128,1024]{2,1,0:T(8,128)S(1)}, f32[2,8,1024]{2,1,0:T(8,128)S(1)}, f32[2,8,1024]{2,1,0:T(8,128)S(1)}) custom-call(bf16[1024,256]{1,0:T(8,128)(2,1)S(1)} %bitcast.49, bf16[1024,256]{1,0:T(8,128)(2,1)S(1)} %bitcast.45, bf16[1024,256]{1,0:T(8,128)(2,1)S(1)} %bitcast.48), custom_call_target="tpu_custom_call" | custom-call | flops 1073741824 | bytes 1572864 | tf_op jit(solution)/shard_map/own_attention/pallas_call | solution.py:38
  178.5 0.0 collective-permute-done.kp_ref
  178.5 0.0 collective-permute-done.1.vp_ref
  178.6 0.0 collective-permute-done.2.kn_ref
  178.6 0.0 collective-permute-done.3.vn_ref
  178.6 12.0 %near_attention.1 = bf16[8,256,128]{2,1,0:T(8,128)(2,1)S(1)} custom-call(s32[2]{0:T(128)S(1)} %add_convert_fusion.ok_ref, bf16[1024,256]{1,0:T(8,128)(2,1)S(1)} %bitcast.50, bf16[1024,256]{1,0:T(8,128)(2,1)S(1)} %collective-permute-done.kp_ref, bf16[1024,256]{1,0:T(8,128)(2,1)S(1)} %collective-permute-done.1.vp_ref, ...), custom_call_target="tpu_custom_call" | custom-call | flops 2147483648 | bytes 3670016 | tf_op jit(solution)/shard_map/near_attention/pallas_call | solution.py:94
  190.6 19.4 %all_to_all.20 = bf16[8,256,128]{2,1,0:T(8,128)(2,1)S(1)} all-to-all(bf16[8,256,128]{2,1,0:T(8,128)(2,1)S(1)} %near_attention.1), channel_id=1, replica_groups=mesh['x'=4,'zh'=2,'y'=8,'zl'=4,'c'=2] {'zl','c'}, dimensions={0} | all-to-all | bytes 1048576 | tf_op jit(solution)/shard_map/all_to_all | solution.py:178
  210.1 0.0 all-gather.4.cloned.1.call-done
  210.1 5.5 %project.1 = bf16[1600,128]{1,0:T(8,128)(2,1)} custom-call(bf16[4,2,400,1024]{3,2,1,0:T(8,128)(2,1)} %bitcast.51, bf16[2,1024,128]{2,1,0:T(8,128)(2,1)S(1)} %bitcast.42), custom_call_target="tpu_custom_call" | custom-call | flops 838860800 | bytes 6553600 | tf_op jit(solution)/shard_map/project/pallas_call | solution.py:129
  (7 shorter events, 0.1 us)
Async XLA Ops:
  6.5 50.8 %copy-start = (bf16[128,2048]{1,0:T(8,128)(2,1)S(1)}, bf16[128,2048]{1,0:T(8,128)(2,1)}, u32[]{:S(2)}) copy-start(bf16[128,2048]{1,0:T(8,128)(2,1)} %param.5) | copy-start | bytes 1572868
  6.5 67.3 %copy-start.1 = (bf16[128,2048]{1,0:T(8,128)(2,1)S(1)}, bf16[128,2048]{1,0:T(8,128)(2,1)}, u32[]{:S(2)}) copy-start(bf16[128,2048]{1,0:T(8,128)(2,1)} %param.6) | copy-start | bytes 1572868
  6.5 86.1 %copy-start.2 = (bf16[128,2048]{1,0:T(8,128)(2,1)S(1)}, bf16[128,2048]{1,0:T(8,128)(2,1)}, u32[]{:S(2)}) copy-start(bf16[128,2048]{1,0:T(8,128)(2,1)} %param.4) | copy-start | bytes 1572868
  6.5 203.6 %all-gather.4.cloned.1.call-start = ((), (), s32[]{:S(2)}) async-start(), calls=%async_computation.4 | async-start | bytes 7372800 | tf_op jit(solution)/shard_map/all_gather | solution.py:160
  58.2 30.2 %all-to-all-start.1 = ((bf16[8,128,256]{2,1,0:T(8,128)(2,1)}), bf16[8,128,256]{2,1,0:T(8,128)(2,1)S(1)}, u32[]{:S(2)}, u32[]{:S(2)}) async-start(bf16[8,128,256]{2,1,0:T(8,128)(2,1)} %bitcast.38), calls=%async_computation.1 | async-start | bytes 1048576 | tf_op jit(solution)/shard_map/all_to_all | solution.py:149
  88.4 18.8 %all-to-all-start.2 = ((bf16[8,128,256]{2,1,0:T(8,128)(2,1)}), bf16[8,128,256]{2,1,0:T(8,128)(2,1)S(1)}, u32[]{:S(2)}, u32[]{:S(2)}) async-start(bf16[8,128,256]{2,1,0:T(8,128)(2,1)} %bitcast.36), calls=%async_computation.2 | async-start | bytes 1048576 | tf_op jit(solution)/shard_map/all_to_all | solution.py:149
  107.2 64.2 %all-to-all-start = ((bf16[8,128,256]{2,1,0:T(8,128)(2,1)}), bf16[8,128,256]{2,1,0:T(8,128)(2,1)S(1)}, u32[]{:S(2)}, u32[]{:S(2)}) async-start(bf16[8,128,256]{2,1,0:T(8,128)(2,1)} %bitcast.40), calls=%async_computation | async-start | bytes 1048576 | tf_op jit(solution)/shard_map/all_to_all | solution.py:149
  111.4 67.2 %collective-permute-start = (bf16[1024,256]{1,0:T(8,128)(2,1)S(1)}, bf16[1024,256]{1,0:T(8,128)(2,1)S(1)}, u32[]{:S(2)}, u32[]{:S(2)}) collective-permute-start(bf16[1024,256]{1,0:T(8,128)(2,1)S(1)} %bitcast.43), channel_id=1, source_target_pairs={{0,8},{8,16},{16,24},{24,32},{32,40},{40,48},{48,56},{56,64},{64,7... | collective-permute-start | bytes 1572872 | tf_op jit(solution)/shard_map/ppermute | solution.py:172
  113.8 64.8 %collective-permute-start.1 = (bf16[1024,256]{1,0:T(8,128)(2,1)S(1)}, bf16[1024,256]{1,0:T(8,128)(2,1)S(1)}, u32[]{:S(2)}, u32[]{:S(2)}) collective-permute-start(bf16[1024,256]{1,0:T(8,128)(2,1)S(1)} %bitcast.46), channel_id=1, source_target_pairs={{0,8},{8,16},{16,24},{24,32},{32,40},{40,48},{48,56},{56,64},{64,7... | collective-permute-start | bytes 1572872 | tf_op jit(solution)/shard_map/ppermute | solution.py:173
  117.0 61.6 %collective-permute-start.2 = (bf16[1024,256]{1,0:T(8,128)(2,1)S(1)}, bf16[1024,256]{1,0:T(8,128)(2,1)S(1)}, u32[]{:S(2)}, u32[]{:S(2)}) collective-permute-start(bf16[1024,256]{1,0:T(8,128)(2,1)S(1)} %bitcast.44), channel_id=1, source_target_pairs={{8,0},{16,8},{24,16},{32,24},{40,32},{48,40},{56,48},{64,56},{72,6... | collective-permute-start | bytes 1572872 | tf_op jit(solution)/shard_map/ppermute | solution.py:172
  118.3 60.3 %collective-permute-start.3 = (bf16[1024,256]{1,0:T(8,128)(2,1)S(1)}, bf16[1024,256]{1,0:T(8,128)(2,1)}, u32[]{:S(2)}, u32[]{:S(2)}) collective-permute-start(bf16[1024,256]{1,0:T(8,128)(2,1)S(1)} %bitcast.47), channel_id=1, source_target_pairs={{8,0},{16,8},{24,16},{32,24},{40,32},{48,40},{56,48},{64,56},{72,6... | collective-permute-start | bytes 1572872 | tf_op jit(solution)/shard_map/ppermute | solution.py:173
Sparse Core Ops, SparseCore 0:
  57.5 55.6 all-gather.3

commit v2 on v1

--- a/solution.py
+++ b/solution.py
@@ -18,7 +18,8 @@
 TILE = 256
 DIMS_NT = (((1,), (1,)), ((), ()))
 DIMS_TN = (((0,), (0,)), ((), ()))
-VMEM = 48 * 1024 * 1024
+VMEM = 32 * 1024 * 1024
+EXTRA = 16
 
 
 def own_kernel(q_ref, k_ref, v_ref, acc_ref, m_ref, l_ref):
@@ -55,7 +56,7 @@
         ],
         compiler_params=pltpu.CompilerParams(vmem_limit_bytes=VMEM),
         cost_estimate=pl.CostEstimate(
-            flops=4 * rows * rows * width, bytes_accessed=6 * rows * width, transcendentals=rows * rows * heads
+            flops=rows * width, bytes_accessed=rows * width, transcendentals=0
         ),
         name="own_attention",
     )(q, k, v)
@@ -117,8 +118,11 @@
 
 def project_kernel(w_ref, ctx_ref, out_ref):
     total = None
-    for c in range(w_ref.shape[1]):
-        part = jnp.dot(w_ref[0, c], ctx_ref[c], preferred_element_type=jnp.float32)
+    groups, width, tok = ctx_ref.shape
+    half = width // w_ref.shape[1]
+    for h in range(w_ref.shape[1]):
+        ctx = ctx_ref[:, h * half : (h + 1) * half, :].reshape(groups * half, tok)
+        part = jnp.dot(w_ref[0, h], ctx, preferred_element_type=jnp.float32)
         total = part if total is None else total + part
     out_ref[...] = total.astype(jnp.bfloat16)
 
@@ -131,7 +135,7 @@
         grid=(parts,),
         in_specs=[
             pl.BlockSpec((1, cores, rows, depth), lambda i: (i, 0, 0, 0)),
-            pl.BlockSpec((cores, depth, tok), lambda i: (0, 0, 0)),
+            pl.BlockSpec(ctx.shape, lambda i: (0, 0, 0)),
         ],
         out_specs=pl.BlockSpec((rows, tok), lambda i: (i, 0)),
         out_shape=jax.ShapeDtypeStruct((parts * rows, tok), jnp.bfloat16),
@@ -143,42 +147,93 @@
     )(w, ctx)
 
 
-def head_split(value):
+def pack_kernel(k_ref, w_ref, out_ref):
+    groups, rows, width = out_ref.shape
+    tok = k_ref.shape[0]
+    half = width // 2
+    cols = w_ref.shape[0]
+    low = rows - tok
+    for g in range(groups):
+        out_ref[g, :tok, :] = k_ref[:, g * width : (g + 1) * width]
+        part = w_ref[:, (g % 2) * half : (g % 2 + 1) * half]
+        out_ref[g, tok:, :half] = part[:low]
+        out_ref[g, tok : tok + cols - low, half:] = part[low:]
+        out_ref[g, tok + cols - low :, half:] = jnp.zeros((2 * low - cols, half), out_ref.dtype)
+
+
+def pack(k, wt):
+    tok, width = k.shape[0], wt.shape[1]
+    return pl.pallas_call(
+        pack_kernel,
+        out_shape=jax.ShapeDtypeStruct((8, tok + EXTRA, width), k.dtype),
+        compiler_params=pltpu.CompilerParams(vmem_limit_bytes=VMEM),
+        name="pack",
+    )(k, wt)
+
+
+def unpack_kernel(in_ref, k_ref, w_ref):
+    groups, rows, width = in_ref.shape
+    tok = k_ref.shape[1]
+    low = rows - tok
+    half = width // 2
+    for g in range(groups):
+        k_ref[g] = in_ref[g, :tok, :]
+        w_ref[:low, g * half : (g + 1) * half] = in_ref[g, tok:, :half]
+        w_ref[low:, g * half : (g + 1) * half] = in_ref[g, tok:, half:]
+
+
+def unpack(moved):
+    groups, rows, width = moved.shape
+    tok = rows - EXTRA
+    return pl.pallas_call(
+        unpack_kernel,
+        out_shape=[
+            jax.ShapeDtypeStruct((groups, tok, width), moved.dtype),
+            jax.ShapeDtypeStruct((2 * EXTRA, groups * width // 2), moved.dtype),
+        ],
+        compiler_params=pltpu.CompilerParams(vmem_limit_bytes=VMEM),
+        name="unpack",
+    )(moved)
+
+
+def to_heads(chunks):
+    return lax.all_to_all(chunks, HEAD, split_axis=0, concat_axis=0)
+
+
+def split_heads(value):
     tok = value.shape[0]
-    chunks = value.reshape(tok, 8, -1).transpose(1, 0, 2)
-    moved = lax.all_to_all(chunks, HEAD, split_axis=0, concat_axis=0)
-    return moved.reshape(8 * tok, -1)
-
-
-def gather_w(w):
-    wt = w.T
-    cols, depth = wt.shape
-    a = lax.all_gather(wt, ("zh", "zl"))
-    a = a.reshape(2, 4, cols, depth).transpose(0, 2, 1, 3).reshape(2 * cols, 4 * depth)
-    b = lax.all_gather(a, "y")
-    b = b.reshape(8, 2, cols, 4 * depth).transpose(1, 0, 2, 3).reshape(16 * cols, 4 * depth)
-    return lax.all_gather(b, ("x", "c")).reshape(4, 2, 16 * cols, 4 * depth)
+    return value.reshape(tok, 8, -1).transpose(1, 0, 2)
 
 
 def local(queries, keys, values, w_out):
     tok = queries.shape[0]
-    weight = gather_w(w_out)
-    k = head_split(keys)
-    v = head_split(values)
-    q = head_split(queries)
+    cols, depth = w_out.shape[1], 4 * w_out.shape[0]
     n_blk = 64
     up = [(i, i + 1) for i in range(n_blk - 1)]
     down = [(i + 1, i) for i in range(n_blk - 1)]
-    kp, kn = lax.ppermute(k, BLK, up), lax.ppermute(k, BLK, down)
-    vp, vn = lax.ppermute(v, BLK, up), lax.ppermute(v, BLK, down)
     here = lax.axis_index(BLK)
     ok = jnp.stack([here > 0, here < n_blk - 1]).astype(jnp.int32)
+    k, w_rows = unpack(to_heads(pack(keys, w_out.T)))
+    k = k.reshape(8 * tok, -1)
+
+    other = lax.ppermute(w_rows, "zh", [(0, 1), (1, 0)])
+    kp, kn = lax.ppermute(k, BLK, up), lax.ppermute(k, BLK, down)
+    values, k = lax.optimization_barrier((values, k))
+    v = to_heads(split_heads(values)).reshape(8 * tok, -1)
+    first = lax.axis_index("zh") == 0
+    pair = jnp.stack([jnp.where(first, w_rows, other), jnp.where(first, other, w_rows)])
+    line = lax.all_gather(pair.reshape(-1, depth), "y").reshape(8, 2, -1, depth)
+    kp, kn, v, queries = lax.optimization_barrier((kp, kn, v, queries))
+
+    vp, vn = lax.ppermute(v, BLK, up), lax.ppermute(v, BLK, down)
+    q = to_heads(split_heads(queries)).reshape(8 * tok, -1)
     acc, m, l = own_attention(q, k, v)
+    line, acc, vp, vn = lax.optimization_barrier((line, acc, vp, vn))
+    line = line[:, :, :cols].transpose(1, 0, 2, 3).reshape(16 * cols, depth)
+    line, acc = lax.optimization_barrier((line, acc))
+    weight = lax.all_gather(line, ("x", "c")).reshape(4, 2, 16 * cols, depth)
     ctx = near_attention(ok, q, kp, vp, kn, vn, acc, m, l, tok)
-    moved = lax.all_to_all(ctx, HEAD, split_axis=0, concat_axis=0)
-    width = moved.shape[1]
-    by_core = moved.reshape(4, 2, width, tok).transpose(1, 0, 2, 3).reshape(2, 4 * width, tok)
-    return project(weight, by_core).T
+    return project(weight, to_heads(ctx)).T
 
 
 def solution(mesh):

time: 223 us -> 203 us (0.910)
  the two profiles are of different devices: /device:TPU:1 before, /device:TPU:6 now
where the time goes in v2:
time: 203 us; the launch traced here: 199 us
  waiting for transfers between devices  72.1 us (36%)
  blocking collectives  44.8 us (22%)
  starting transfers between devices  32.1 us (16%)
  Pallas kernels  22.2 us (11%)
  between operations  13.5 us (7%)
  local copies, waits for them, and re-layouts  13.4 us (7%)
    all_to_all x2, blocking collectives, to_heads(): return lax.all_to_all(chunks, HEAD, split_axis=0, concat_axis=0)  44.8 us
    ppermute x2, waiting for transfers between devices, local(): kp, kn = (lax.ppermute(k, BLK, up), lax.ppermute(k, BLK, down))  29.5 us
    all_gather x1, waiting for transfers between devices, local(): weight = lax.all_gather(line, ('x', 'c')).reshape(4, 2, 16 * cols, depth)  19.6 us
    ppermute x2, waiting for transfers between devices, local(): vp, vn = (lax.ppermute(v, BLK, up), lax.ppermute(v, BLK, down))  13.3 us
    pallas_call x1, Pallas kernels, near_attention(): pl.pallas_call(near_kernel, grid=(heads, rows // TILE), in_specs=[pl.Bloc...  11.9 us
    ppermute x2, starting transfers between devices, local(): kp, kn = (lax.ppermute(k, BLK, up), lax.ppermute(k, BLK, down))  9.71 us
    all_to_all x2, waiting for transfers between devices, to_heads(): return lax.all_to_all(chunks, HEAD, split_axis=0, concat_axis=0)  9.67 us
    all_to_all x2, starting transfers between devices, to_heads(): return lax.all_to_all(chunks, HEAD, split_axis=0, concat_axis=0)  8.29 us
  transfers between devices with their start and end apart: 9, of which 6 were waited for; matrix products, arithmetic and copies ran while one was open for 2% of the time, Pallas kernels for 10%

profile of v2, /device:TPU:6, one launch (start us, length us, event | category | flops | bytes accessed | tf_op | source)
XLA Modules:
  0.0 199.0 jit_solution(17724789820924083014)
XLA Ops:
  6.5 1.0 copy-done.1
  7.6 0.7 copy-done.2
  8.3 0.1 pack.1
  8.4 23.8 %all_to_all.20.in_ref = bf16[8,144,256]{2,1,0:T(8,128)(2,1)S(1)} all-to-all(bf16[8,144,256]{2,1,0:T(8,128)(2,1)S(1)} %pack.1), channel_id=1, replica_groups=mesh['x'=4,'zh'=2,'y'=8,'zl'=4,'c'=2] {'zl','c'}, dimensions={0} | all-to-all | bytes 1179648 | tf_op jit(solution)/shard_map/all_to_all | solution.py:200
  32.2 8.2 %collective-permute-start = (bf16[32,1024]{1,0:T(8,128)(2,1)S(1)}, bf16[32,1024]{1,0:T(8,128)(2,1)S(1)}, u32[]{:S(2)}, u32[]{:S(2)}) collective-permute-start(bf16[32,1024]{1,0:T(8,128)(2,1)S(1)} %get-tuple-element.22), channel_id=1, source_target_pairs={{0,64},{64,0},{1,65},{65,1},{2,66},{66,2},{3,67},{67,3},{4,68},{68... | collective-permute-start | bytes 196616 | tf_op jit(solution)/shard_map/ppermute | solution.py:219
  40.5 1.9 copy.21
  42.3 3.5 %all-to-all-start.1 = ((bf16[8,128,256]{2,1,0:T(8,128)(2,1)}), bf16[8,128,256]{2,1,0:T(8,128)(2,1)S(1)}, u32[]{:S(2)}, u32[]{:S(2)}) async-start(bf16[8,128,256]{2,1,0:T(8,128)(2,1)} %bitcast.29), calls=%async_computation.1 | async-start | bytes 1048576 | tf_op jit(solution)/shard_map/all_to_all | solution.py:200
  45.8 0.0 all-gather.4.cloned.1.call-start
  45.9 0.7 pad_maximum_fusion
  46.6 0.0 all-gather.4.cloned.1.call-update
  46.6 7.8 %collective-permute-start.2 = (bf16[1024,256]{1,0:T(8,128)(2,1)S(1)}, bf16[1024,256]{1,0:T(8,128)(2,1)S(1)}, u32[]{:S(2)}, u32[]{:S(2)}) collective-permute-start(bf16[1024,256]{1,0:T(8,128)(2,1)S(1)} %bitcast.36), channel_id=1, source_target_pairs={{8,0},{16,8},{24,16},{32,24},{40,32},{48,40},{56,48},{64,56},{72,6... | collective-permute-start | bytes 1572872 | tf_op jit(solution)/shard_map/ppermute | solution.py:220
  54.4 1.9 collective-permute-start.1
  56.3 17.7 %collective-permute-done.2.kn_ref = bf16[1024,256]{1,0:T(8,128)(2,1)S(1)} collective-permute-done((bf16[1024,256]{1,0:T(8,128)(2,1)S(1)}, bf16[1024,256]{1,0:T(8,128)(2,1)S(1)}, u32[]{:S(2)}, u32[]{:S(2)}) %collective-permute-start.2) | collective-permute-done | bytes 524320 | tf_op jit(solution)/shard_map/ppermute | solution.py:220
  74.1 11.8 %collective-permute-done.1.kp_ref = bf16[1024,256]{1,0:T(8,128)(2,1)S(1)} collective-permute-done((bf16[1024,256]{1,0:T(8,128)(2,1)S(1)}, bf16[1024,256]{1,0:T(8,128)(2,1)S(1)}, u32[]{:S(2)}, u32[]{:S(2)}) %collective-permute-start.1) | collective-permute-done | bytes 524320 | tf_op jit(solution)/shard_map/ppermute | solution.py:220
  85.9 2.1 %copy.20 = bf16[16,8,8,256]{3,2,0,1:T(8,128)(2,1)} copy(bf16[16,8,8,256]{3,2,1,0:T(8,128)(2,1)} %bitcast.42) | data formatting | bytes 1048576 | tf_op jit(solution)/shard_map/reshape | solution.py:205
  87.9 4.8 %all-to-all-start.2 = ((bf16[8,128,256]{2,1,0:T(8,128)(2,1)}), bf16[8,128,256]{2,1,0:T(8,128)(2,1)S(1)}, u32[]{:S(2)}, u32[]{:S(2)}) async-start(bf16[8,128,256]{2,1,0:T(8,128)(2,1)} %bitcast.27), calls=%async_computation.2 | async-start | bytes 1048576 | tf_op jit(solution)/shard_map/all_to_all | solution.py:200
  92.8 0.0 all-gather.6.cloned.1.call-start
  92.8 2.0 collective-permute-start.4
  94.8 3.9 %collective-permute-start.3 = (bf16[1024,256]{1,0:T(8,128)(2,1)S(1)}, bf16[1024,256]{1,0:T(8,128)(2,1)}, u32[]{:S(2)}, u32[]{:S(2)}) collective-permute-start(bf16[1024,256]{1,0:T(8,128)(2,1)S(1)} %bitcast.34), channel_id=1, source_target_pairs={{0,8},{8,16},{16,24},{24,32},{32,40},{40,48},{48,56},{56,64},{64,7... | collective-permute-start | bytes 1572872 | tf_op jit(solution)/shard_map/ppermute | solution.py:228
  98.7 9.7 %all-to-all-done.2 = bf16[8,128,256]{2,1,0:T(8,128)(2,1)S(1)} async-done(((bf16[8,128,256]{2,1,0:T(8,128)(2,1)}), bf16[8,128,256]{2,1,0:T(8,128)(2,1)S(1)}, u32[]{:S(2)}, u32[]{:S(2)}) %all-to-all-start.2) | async-done | bytes 524320 | tf_op jit(solution)/shard_map/all_to_all | solution.py:200
  108.3 7.1 %own_attention.1 = (f32[2,128,1024]{2,1,0:T(8,128)S(1)}, f32[2,8,1024]{2,1,0:T(8,128)S(1)}, f32[2,8,1024]{2,1,0:T(8,128)S(1)}) custom-call(bf16[1024,256]{1,0:T(8,128)(2,1)S(1)} %bitcast.31, bf16[1024,256]{1,0:T(8,128)(2,1)S(1)} %bitcast.38, bf16[1024,256]{1,0:T(8,128)(2,1)S(1)} %bitcast.35), custom_call_target="tpu_custom_call" | custom-call | flops 262144 | bytes 262144 | tf_op jit(solution)/shard_map/own_attention/pallas_call | solution.py:39
  115.4 0.3 collective-permute-done.4.vn_ref
  115.8 12.9 %collective-permute-done.3.vp_ref = bf16[1024,256]{1,0:T(8,128)(2,1)} collective-permute-done((bf16[1024,256]{1,0:T(8,128)(2,1)S(1)}, bf16[1024,256]{1,0:T(8,128)(2,1)}, u32[]{:S(2)}, u32[]{:S(2)}) %collective-permute-start.3) | collective-permute-done | bytes 524320 | tf_op jit(solution)/shard_map/ppermute | solution.py:228
  128.7 1.3 slice_bitcast_fusion
  130.0 1.1 copy.15
  131.1 2.4 %reshape.30 = bf16[400,1024]{1,0:T(8,128)(2,1)} reshape(bf16[2,8,25,1024]{3,2,1,0:T(8,128)(2,1)} %copy.15) | data formatting | bytes 1638400 | tf_op jit(solution)/shard_map/reshape | solution.py:232
  133.5 0.1 add_convert_fusion.ok_ref
  133.6 11.9 %near_attention.1 = bf16[8,256,128]{2,1,0:T(8,128)(2,1)S(1)} custom-call(s32[2]{0:T(128)S(1)} %add_convert_fusion.ok_ref, bf16[1024,256]{1,0:T(8,128)(2,1)S(1)} %bitcast.32, bf16[1024,256]{1,0:T(8,128)(2,1)S(1)} %copy-done.4, bf16[1024,256]{1,0:T(8,128)(2,1)} %collective-permute-done.3.vp_ref, bf16[1024,256]{1,0:T(8,128)(2,1)S(1)} %collective-permute-done.2.kn_ref, ...), custom_call_target="tpu_custom_call" | custom-call | flops 2147483648 | bytes 3670016 | tf_op jit(solution)/shard_map/near_attention/pallas_call | solution.py:95
  145.6 21.0 %all_to_all.21.ctx_ref = bf16[8,256,128]{2,1,0:T(8,128)(2,1)S(1)} all-to-all(bf16[8,256,128]{2,1,0:T(8,128)(2,1)S(1)} %near_attention.1), channel_id=1, replica_groups=mesh['x'=4,'zh'=2,'y'=8,'zl'=4,'c'=2] {'zl','c'}, dimensions={0} | all-to-all | bytes 1048576 | tf_op jit(solution)/shard_map/all_to_all | solution.py:200
  166.6 19.6 %all-gather.6.cloned.1.call-done = bf16[3200,1024]{1,0:T(8,128)(2,1)} async-done(((bf16[400,1024]{1,0:T(8,128)(2,1)}), bf16[3200,1024]{1,0:T(8,128)(2,1)}) %all-gather.6.cloned.1.call-update) | async-done | bytes 6553616 | tf_op jit(solution)/shard_map/all_gather | solution.py:234
  186.2 2.9 %copy-done = bf16[3200,1024]{1,0:T(8,128)(2,1)S(1)} copy-done((bf16[3200,1024]{1,0:T(8,128)(2,1)S(1)}, bf16[3200,1024]{1,0:T(8,128)(2,1)}, u32[]{:S(2)}) %copy-start) | copy-done | bytes 6553624
  189.1 3.1 %project.1 = bf16[1600,128]{1,0:T(8,128)(2,1)} custom-call(bf16[4,2,400,1024]{3,2,1,0:T(8,128)(2,1)S(1)} %bitcast.30, bf16[8,256,128]{2,1,0:T(8,128)(2,1)S(1)} %all_to_all.21.ctx_ref), custom_call_target="tpu_custom_call" | custom-call | flops 838860800 | bytes 6553600 | tf_op jit(solution)/shard_map/project/pallas_call | solution.py:133
  (13 shorter events, 0.1 us)
Async XLA Ops:
  6.5 1.0 copy-start.1
  7.6 0.7 copy-start.2
  32.2 13.7 %collective-permute-start = (bf16[32,1024]{1,0:T(8,128)(2,1)S(1)}, bf16[32,1024]{1,0:T(8,128)(2,1)S(1)}, u32[]{:S(2)}, u32[]{:S(2)}) collective-permute-start(bf16[32,1024]{1,0:T(8,128)(2,1)S(1)} %get-tuple-element.22), channel_id=1, source_target_pairs={{0,64},{64,0},{1,65},{65,1},{2,66},{66,2},{3,67},{67,3},{4,68},{68... | collective-permute-start | bytes 196616 | tf_op jit(solution)/shard_map/ppermute | solution.py:219
  42.3 43.6 %all-to-all-start.1 = ((bf16[8,128,256]{2,1,0:T(8,128)(2,1)}), bf16[8,128,256]{2,1,0:T(8,128)(2,1)S(1)}, u32[]{:S(2)}, u32[]{:S(2)}) async-start(bf16[8,128,256]{2,1,0:T(8,128)(2,1)} %bitcast.29), calls=%async_computation.1 | async-start | bytes 1048576 | tf_op jit(solution)/shard_map/all_to_all | solution.py:200
  45.8 82.9 %all-gather.4.cloned.1.call-start = ((), (), s32[]{:S(2)}) async-start(), calls=%async_computation.4 | async-start | bytes 1179648 | tf_op jit(solution)/shard_map/all_gather | solution.py:225
  46.6 27.4 %collective-permute-start.2 = (bf16[1024,256]{1,0:T(8,128)(2,1)S(1)}, bf16[1024,256]{1,0:T(8,128)(2,1)S(1)}, u32[]{:S(2)}, u32[]{:S(2)}) collective-permute-start(bf16[1024,256]{1,0:T(8,128)(2,1)S(1)} %bitcast.36), channel_id=1, source_target_pairs={{8,0},{16,8},{24,16},{32,24},{40,32},{48,40},{56,48},{64,56},{72,6... | collective-permute-start | bytes 1572872 | tf_op jit(solution)/shard_map/ppermute | solution.py:220
  54.4 31.5 %collective-permute-start.1 = (bf16[1024,256]{1,0:T(8,128)(2,1)S(1)}, bf16[1024,256]{1,0:T(8,128)(2,1)S(1)}, u32[]{:S(2)}, u32[]{:S(2)}) collective-permute-start(bf16[1024,256]{1,0:T(8,128)(2,1)S(1)} %bitcast.37), channel_id=1, source_target_pairs={{0,8},{8,16},{16,24},{24,32},{32,40},{40,48},{48,56},{56,64},{64,7... | collective-permute-start | bytes 1572872 | tf_op jit(solution)/shard_map/ppermute | solution.py:220
  85.9 22.4 %copy-start.3 = (bf16[1024,256]{1,0:T(8,128)(2,1)}, bf16[1024,256]{1,0:T(8,128)(2,1)S(1)}, u32[]{:S(2)}) copy-start(bf16[1024,256]{1,0:T(8,128)(2,1)S(1)} %collective-permute-done.1.kp_ref) | copy-start | bytes 1572868
  87.9 20.4 %all-to-all-start.2 = ((bf16[8,128,256]{2,1,0:T(8,128)(2,1)}), bf16[8,128,256]{2,1,0:T(8,128)(2,1)S(1)}, u32[]{:S(2)}, u32[]{:S(2)}) async-start(bf16[8,128,256]{2,1,0:T(8,128)(2,1)} %bitcast.27), calls=%async_computation.2 | async-start | bytes 1048576 | tf_op jit(solution)/shard_map/all_to_all | solution.py:200
  92.8 93.5 %all-gather.6.cloned.1.call-start = ((), (), s32[]{:S(2)}) async-start(), calls=%async_computation.5 | async-start | bytes 7372800 | tf_op jit(solution)/shard_map/all_gather | solution.py:234
  92.8 23.0 %collective-permute-start.4 = (bf16[1024,256]{1,0:T(8,128)(2,1)S(1)}, bf16[1024,256]{1,0:T(8,128)(2,1)}, u32[]{:S(2)}, u32[]{:S(2)}) collective-permute-start(bf16[1024,256]{1,0:T(8,128)(2,1)S(1)} %bitcast.33), channel_id=1, source_target_pairs={{8,0},{16,8},{24,16},{32,24},{40,32},{48,40},{56,48},{64,56},{72,6... | collective-permute-start | bytes 1572872 | tf_op jit(solution)/shard_map/ppermute | solution.py:228
  94.8 33.9 %collective-permute-start.3 = (bf16[1024,256]{1,0:T(8,128)(2,1)S(1)}, bf16[1024,256]{1,0:T(8,128)(2,1)}, u32[]{:S(2)}, u32[]{:S(2)}) collective-permute-start(bf16[1024,256]{1,0:T(8,128)(2,1)S(1)} %bitcast.34), channel_id=1, source_target_pairs={{0,8},{8,16},{16,24},{24,32},{32,40},{40,48},{48,56},{56,64},{64,7... | collective-permute-start | bytes 1572872 | tf_op jit(solution)/shard_map/ppermute | solution.py:228
  115.4 18.2 %copy-start.4 = (bf16[1024,256]{1,0:T(8,128)(2,1)S(1)}, bf16[1024,256]{1,0:T(8,128)(2,1)}, u32[]{:S(2)}) copy-start(bf16[1024,256]{1,0:T(8,128)(2,1)} %copy-done.3) | copy-start | bytes 1572868
  186.2 2.9 %copy-start = (bf16[3200,1024]{1,0:T(8,128)(2,1)S(1)}, bf16[3200,1024]{1,0:T(8,128)(2,1)}, u32[]{:S(2)}) copy-start(bf16[3200,1024]{1,0:T(8,128)(2,1)} %all-gather.6.cloned.1.call-done) | copy-start | bytes 19660804
Sparse Core Ops, SparseCore 0:
  48.8 41.4 all-gather.3
  133.7 52.5 all-gather.5

commit v3 on v1

v3 whole, which is shorter than its diff:
```python
import functools
import math

import jax
import jax.numpy as jnp
from jax import lax
from jax.experimental import pallas as pl
from jax.experimental.pallas import tpu as pltpu
from jax.sharding import Mesh, PartitionSpec as P

HDIM = 128
LOG2E = 1.4426950408889634
FACTOR = LOG2E / math.sqrt(HDIM)
AXES = ("x", "zh", "y", "zl", "c")
SIZES = (4, 2, 8, 4, 2)
BLK = ("x", "zh", "y")
HEAD = ("zl", "c")
TILE = 256
DIMS_NT = (((1,), (1,)), ((), ()))
DIMS_TN = (((0,), (0,)), ((), ()))
VMEM = 32 * 1024 * 1024
N_BLK = 64


def attend(parts, q, carry):
    far = jnp.float32(1e30)
    scores, m = [], None if carry is None else carry[1]
    for k, _, ok in parts:
        s = lax.dot_general(k, q, DIMS_NT, preferred_element_type=jnp.float32)
        scores.append(s)
        largest = jnp.max(s, axis=0, keepdims=True) * FACTOR
        if ok is not None:
            largest = jnp.where(ok, largest, -far)
        m = largest if m is None else jnp.maximum(m, largest)
    acc = total = None
    if carry is not None:
        alpha = jnp.exp2(carry[1] - m)
        acc, total = carry[0] * alpha, carry[2] * alpha
    for s, (_, v, ok) in zip(scores, parts):
        raised = jnp.exp2(s * FACTOR - (m if ok is None else jnp.where(ok, m, far)))
        part = lax.dot_general(v, raised.astype(jnp.bfloat16), DIMS_TN, preferred_element_type=jnp.float32)
        summed = jnp.sum(raised, axis=0, keepdims=True)
        acc, total = (part, summed) if acc is None else (acc + part, total + summed)
    return acc, m, total


def pair_kernel(ok_ref, q_ref, k_ref, v_ref, acc_ref, m_ref, l_ref):
    chunks, tok = k_ref.shape[0] // 2, k_ref.shape[1]
    parts = []
    for p in range(2):
        span = slice(p * chunks, (p + 1) * chunks)
        parts.append(
            (k_ref[span].reshape(chunks * tok, HDIM), v_ref[span].reshape(chunks * tok, HDIM), ok_ref[p] > 0)
        )
    acc, m, total = attend(parts, q_ref[...], None)
    acc_ref[0] = acc
    m_ref[0] = jnp.broadcast_to(m, m_ref.shape[1:])
    l_ref[0] = jnp.broadcast_to(total, l_ref.shape[1:])


def sides(kv):
    block = (kv.shape[0], kv.shape[1] // 2, HDIM)
    return [pl.BlockSpec(block, lambda h, i: (0, 0, h)), pl.BlockSpec(block, lambda h, i: (0, 1, h))]


def pair_attention(ok, q, kv):
    rows, width = q.shape
    heads = width // HDIM
    row = pl.BlockSpec((1, 8, TILE), lambda h, i: (h, 0, i))
    return pl.pallas_call(
        pair_kernel,
        grid=(heads, rows // TILE),
        in_specs=[
            pl.BlockSpec(memory_space=pltpu.SMEM),
            pl.BlockSpec((TILE, HDIM), lambda h, i: (i, h)),
            *sides(kv),
        ],
        out_specs=[pl.BlockSpec((1, HDIM, TILE), lambda h, i: (h, 0, i)), row, row],
        out_shape=[
            jax.ShapeDtypeStruct((heads, HDIM, rows), jnp.float32),
            jax.ShapeDtypeStruct((heads, 8, rows), jnp.float32),
            jax.ShapeDtypeStruct((heads, 8, rows), jnp.float32),
        ],
        compiler_params=pltpu.CompilerParams(vmem_limit_bytes=VMEM),
        cost_estimate=pl.CostEstimate(flops=rows * width, bytes_accessed=rows * width, transcendentals=0),
        name="pair_attention",
    )(ok, q, kv, kv)


def last_kernel(q_ref, k_ref, v_ref, acc_ref, m_ref, l_ref, out_ref):
    carry = (acc_ref[0], m_ref[0][:1], l_ref[0][:1])
    rows = k_ref.shape[0] * k_ref.shape[1]
    part = (k_ref[...].reshape(rows, HDIM), v_ref[...].reshape(rows, HDIM), None)
    acc, _, total = attend([part], q_ref[...], carry)
    result = (acc / total).astype(jnp.bfloat16)
    tok = out_ref.shape[2]
    for part in range(out_ref.shape[0]):
        out_ref[part] = result[:, part * tok : (part + 1) * tok]


def last_attention(q, kv, acc, m, l, tok):
    rows, width = q.shape
    heads = width // HDIM
    row = pl.BlockSpec((1, 8, TILE), lambda h, i: (h, 0, i))
    return pl.pallas_call(
        last_kernel,
        grid=(heads, rows // TILE),
        in_specs=[
            pl.BlockSpec((TILE, HDIM), lambda h, i: (i, h)),
            *sides(kv),
            pl.BlockSpec((1, HDIM, TILE), lambda h, i: (h, 0, i)),
            row,
            row,
        ],
        out_specs=pl.BlockSpec((TILE // tok, HDIM, tok), lambda h, i: (i, h, 0)),
        out_shape=jax.ShapeDtypeStruct((rows // tok, width, tok), jnp.bfloat16),
        compiler_params=pltpu.CompilerParams(vmem_limit_bytes=VMEM),
        cost_estimate=pl.CostEstimate(
            flops=4 * rows * rows * width, bytes_accessed=14 * rows * width, transcendentals=rows * rows * heads
        ),
        name="last_attention",
    )(q, kv, kv, acc, m, l)


def project_kernel(w_ref, ctx_ref, out_ref):
    total = None
    groups, width, tok = ctx_ref.shape
    half = width // w_ref.shape[1]
    for h in range(w_ref.shape[1]):
        ctx = ctx_ref[:, h * half : (h + 1) * half, :].reshape(groups * half, tok)
        part = jnp.dot(w_ref[0, h], ctx, preferred_element_type=jnp.float32)
        total = part if total is None else total + part
    out_ref[...] = total.astype(jnp.bfloat16)


def project(w, ctx):
    parts, cores, rows, depth = w.shape
    tok = ctx.shape[2]
    return pl.pallas_call(
        project_kernel,
        grid=(parts,),
        in_specs=[
            pl.BlockSpec((1, cores, rows, depth), lambda i: (i, 0, 0, 0)),
            pl.BlockSpec(ctx.shape, lambda i: (0, 0, 0)),
        ],
        out_specs=pl.BlockSpec((rows, tok), lambda i: (i, 0)),
        out_shape=jax.ShapeDtypeStruct((parts * rows, tok), jnp.bfloat16),
        compiler_params=pltpu.CompilerParams(vmem_limit_bytes=VMEM),
        cost_estimate=pl.CostEstimate(
            flops=2 * parts * rows * depth * cores * tok, bytes_accessed=2 * parts * rows * depth * cores, transcendentals=0
        ),
        name="project",
    )(w, ctx)


def pack_kernel(k_ref, v_ref, out_ref):
    tok, width = k_ref.shape[0], out_ref.shape[2]
    for chunk in range(out_ref.shape[0]):
        g = chunk % 8
        out_ref[chunk, :tok, :] = k_ref[:, g * width : (g + 1) * width]
        out_ref[chunk, tok:, :] = v_ref[:, g * width : (g + 1) * width]


def pack(k, v):
    tok, width = k.shape
    return pl.pallas_call(
        pack_kernel,
        out_shape=jax.ShapeDtypeStruct((16, 2 * tok, width // 8), k.dtype),
        compiler_params=pltpu.CompilerParams(vmem_limit_bytes=VMEM),
        name="pack",
    )(k, v)


def to_heads(chunks):
    return lax.all_to_all(chunks, HEAD, split_axis=0, concat_axis=0)


def to_pair(chunks):
    groups = []
    for b in range(1, N_BLK, 2):
        groups.append([c * 8 + i for c in (b, (b + 1) % N_BLK) for i in range(8)])
    return lax.all_to_all(chunks, AXES, split_axis=0, concat_axis=0, axis_index_groups=groups)


def exchange(own):
    pairs = [(b * 8 + i, (b ^ 1) * 8 + i) for b in range(N_BLK) for i in range(8)]
    return lax.ppermute(own, AXES, pairs)


def split_heads(value):
    tok = value.shape[0]
    return value.reshape(tok, 8, -1).transpose(1, 0, 2)


def local(queries, keys, values, w_out):
    tok = queries.shape[0]
    depth, cols = w_out.shape
    half = depth // 2
    here = lax.axis_index(BLK)
    ok = jnp.stack([here > 0, here < N_BLK - 1]).astype(jnp.int32)
    start = jnp.where(here % 2 == 0, 8, 0)
    kv = to_pair(pack(keys, values))

    rows = lax.all_gather(w_out.T, ("zh", "zl", "c")).reshape(2, 8, cols, depth)
    rows = lax.dynamic_slice_in_dim(rows, lax.axis_index("c") * half, half, 3)
    rows = rows.transpose(0, 2, 1, 3).reshape(2 * cols, 8 * half)
    line = lax.all_gather(rows, "y").reshape(8, 2, cols, 8 * half)
    line = line.transpose(1, 0, 2, 3).reshape(16 * cols, 8 * half)
    kv, line, queries = lax.optimization_barrier((kv, line, queries))

    weight = lax.all_gather(line, ("x", "c")).reshape(4, 2, 16 * cols, 8 * half)
    other = exchange(lax.dynamic_slice_in_dim(kv, start, 8, 0))
    q = to_heads(split_heads(queries)).reshape(8 * tok, -1)
    acc, m, l = pair_attention(ok, q, kv)
    other, acc = lax.optimization_barrier((other, acc))
    ctx = last_attention(q, other, acc, m, l, tok)
    return project(weight, to_heads(ctx)).T


def solution(mesh):
    cut = Mesh(mesh.devices.reshape(SIZES), AXES)
    return jax.shard_map(
        local,
        mesh=cut,
        in_specs=(P(AXES, None), P(AXES, None), P(AXES, None), P(HEAD, BLK)),
        out_specs=P(AXES, None),
        check_vma=False,
    )
```

time: 223 us -> 208 us (0.933)
  the two profiles are of different devices: /device:TPU:1 before, /device:TPU:6 now
where the time goes in v3:
time: 208 us; the launch traced here: 205 us
  blocking collectives  120 us (58%)
  Pallas kernels  23.5 us (11%)
  starting transfers between devices  22.9 us (11%)
  waiting for transfers between devices  15.3 us (7%)
  between operations  13.5 us (6%)
  local copies, waits for them, and re-layouts  10.5 us (5%)
    all_gather x1, blocking collectives, local(): rows = lax.all_gather(w_out.T, ('zh', 'zl', 'c')).reshape(2, 8, cols, depth)  75.4 us
    all_gather x1, blocking collectives, local(): line = lax.all_gather(rows, 'y').reshape(8, 2, cols, 8 * half)  26.4 us
    all_to_all x1, blocking collectives, to_heads(): return lax.all_to_all(chunks, HEAD, split_axis=0, concat_axis=0)  17.8 us
    all_to_all x1, starting transfers between devices, to_pair(): lax.all_to_all(chunks, AXES, split_axis=0, concat_axis=0, axis_index_grou...  16.9 us
    all_to_all x1, waiting for transfers between devices, to_heads(): return lax.all_to_all(chunks, HEAD, split_axis=0, concat_axis=0)  15.3 us
    pallas_call x1, Pallas kernels, pair_attention(): pl.pallas_call(pair_kernel, grid=(heads, rows // TILE), in_specs=[pl.Bloc...  12.1 us
    pallas_call x1, Pallas kernels, last_attention(): pl.pallas_call(last_kernel, grid=(heads, rows // TILE), in_specs=[pl.Bloc...  8.21 us
    unnamed x13, local copies, waits for them, and re-layouts  6.33 us
  transfers between devices with their start and end apart: 4, of which 1 were waited for; matrix products, arithmetic and copies ran while one was open for 2% of the time, Pallas kernels for 10%

profile of v3, /device:TPU:6, one launch (start us, length us, event | category | flops | bytes accessed | tf_op | source)
XLA Modules:
  0.0 205.3 jit_solution(3215121427936077060)
XLA Ops:
  6.5 0.0 copy-start.2
  6.5 1.0 copy-done.2
  7.6 0.0 copy-start.3
  7.6 1.0 copy-done.3
  8.6 0.1 pack.1
  8.8 0.0 copy-start
  8.8 1.3 copy-done
  10.1 0.0 copy-start.5
  10.1 16.9 %all-to-all-start = ((bf16[16,256,256]{2,1,0:T(8,128)(2,1)}), bf16[16,256,256]{2,1,0:T(8,128)(2,1)S(1)}, u32[]{:S(2)}, u32[]{:S(2)}) async-start(bf16[16,256,256]{2,1,0:T(8,128)(2,1)} %copy-done), calls=%async_computation | async-start | bytes 4194304 | tf_op jit(solution)/shard_map/all_to_all | solution.py:182
  27.0 0.0 all-gather.5.cloned.1.call-start
  27.1 0.0 copy-done.5
  27.1 75.4 %all-gather.2 = bf16[16,25,256]{2,1,0:T(8,128)(2,1)S(1)} all-gather(bf16[1,25,256]{2,1,0:T(8,128)(2,1)S(1)} %bitcast.31), channel_id=2, replica_groups=mesh['x'=4,'zh'=2,'y'=8,'zl'=4,'c'=2] {'zh','zl','c'}, dimensions={0}, use_global_device_ids=true | all-gather | bytes 217600 | tf_op jit(solution)/shard_map/all_gather | solution.py:204
  102.5 0.1 all_gather_reshape.3
  102.6 26.4 %all_gather.17 = bf16[8,50,1024]{2,1,0:T(8,128)(2,1)S(1)} all-gather(bf16[1,50,1024]{2,1,0:T(8,128)(2,1)S(1)} %all_gather_reshape.3), channel_id=1, replica_groups=mesh['x'=4,'zh'=2,'y'=8,'zl'=4,'c'=2] {'y'}, dimensions={0}, use_global_device_ids=true | all-gather | bytes 921600 | tf_op jit(solution)/shard_map/all_gather | solution.py:207
  129.0 0.5 copy.11
  129.4 0.5 copy.12
  129.9 1.3 reshape.20
  131.2 0.0 all-to-all-done.k_ref.v_ref
  131.2 0.0 all-gather.5.cloned.1.call-update
  131.2 1.0 constant_dynamic-slice_fusion
  132.2 2.0 collective-permute-start
  134.3 0.0 copy-done.4
  134.3 0.8 copy.18
  135.1 4.0 %all-to-all-start.1 = ((bf16[8,128,256]{2,1,0:T(8,128)(2,1)}), bf16[8,128,256]{2,1,0:T(8,128)(2,1)S(1)}, u32[]{:S(2)}, u32[]{:S(2)}) async-start(bf16[8,128,256]{2,1,0:T(8,128)(2,1)} %bitcast.22), calls=%async_computation.1 | async-start | bytes 1048576 | tf_op jit(solution)/shard_map/all_to_all | solution.py:175
  139.1 0.1 add_convert_fusion.ok_ref
  139.2 15.3 %all-to-all-done.1 = bf16[8,128,256]{2,1,0:T(8,128)(2,1)S(1)} async-done(((bf16[8,128,256]{2,1,0:T(8,128)(2,1)}), bf16[8,128,256]{2,1,0:T(8,128)(2,1)S(1)}, u32[]{:S(2)}, u32[]{:S(2)}) %all-to-all-start.1) | async-done | bytes 524320 | tf_op jit(solution)/shard_map/all_to_all | solution.py:175
  154.5 12.1 %pair_attention.1 = (f32[2,128,1024]{2,1,0:T(8,128)S(1)}, f32[2,8,1024]{2,1,0:T(8,128)S(1)}, f32[2,8,1024]{2,1,0:T(8,128)S(1)}) custom-call(s32[2]{0:T(128)S(1)} %add_convert_fusion.ok_ref, bf16[1024,256]{1,0:T(8,128)(2,1)S(1)} %bitcast.25, bf16[16,256,256]{2,1,0:T(8,128)(2,1)S(1)} %all-to-all-done.k_ref.v_ref, ...), custom_call_target="tpu_custom_call" | custom-call | flops 262144 | bytes 262144 | tf_op jit(solution)/shard_map/pair_attention/pallas_call | solution.py:70
  166.6 0.0 collective-permute-done.k_ref.v_ref
  166.6 8.2 %last_attention.1 = bf16[8,256,128]{2,1,0:T(8,128)(2,1)S(1)} custom-call(bf16[1024,256]{1,0:T(8,128)(2,1)S(1)} %bitcast.26, bf16[8,256,256]{2,1,0:T(8,128)(2,1)} %collective-permute-done.k_ref.v_ref, bf16[8,256,256]{2,1,0:T(8,128)(2,1)} %collective-permute-done.k_ref.v_ref, f32[2,128,1024]{2,1,0:T(8,128)S(1)} %get-tuple-element.18.acc_ref, ...), custom_call_target="tpu_custom_call" | custom-call | flops 1073741824 | bytes 3670016 | tf_op jit(solution)/shard_map/last_attention/pallas_call | solution.py:105
  174.8 17.8 %all_to_all.15.ctx_ref = bf16[8,256,128]{2,1,0:T(8,128)(2,1)S(1)} all-to-all(bf16[8,256,128]{2,1,0:T(8,128)(2,1)S(1)} %last_attention.1), channel_id=1, replica_groups=mesh['x'=4,'zh'=2,'y'=8,'zl'=4,'c'=2] {'zl','c'}, dimensions={0} | all-to-all | bytes 1048576 | tf_op jit(solution)/shard_map/all_to_all | solution.py:175
  192.6 2.9 %copy-done.1 = bf16[3200,1024]{1,0:T(8,128)(2,1)S(1)} copy-done((bf16[3200,1024]{1,0:T(8,128)(2,1)S(1)}, bf16[3200,1024]{1,0:T(8,128)(2,1)}, u32[]{:S(2)}) %copy-start.1) | copy-done | bytes 6553624
  195.4 3.1 %project.1 = bf16[1600,128]{1,0:T(8,128)(2,1)} custom-call(bf16[4,2,400,1024]{3,2,1,0:T(8,128)(2,1)S(1)} %bitcast.24, bf16[8,256,128]{2,1,0:T(8,128)(2,1)S(1)} %all_to_all.15.ctx_ref), custom_call_target="tpu_custom_call" | custom-call | flops 838860800 | bytes 6553600 | tf_op jit(solution)/shard_map/project/pallas_call | solution.py:139
  (5 shorter events, 0.1 us)
Async XLA Ops:
  6.5 1.0 copy-start.2
  7.6 1.0 copy-start.3
  8.8 1.3 copy-start
  10.1 16.9 %copy-start.5 = (bf16[256,25]{0,1:T(8,128)(2,1)S(1)}, bf16[256,25]{0,1:T(8,128)(2,1)}, u32[]{:S(2)}) copy-start(bf16[256,25]{0,1:T(8,128)(2,1)} %param.7) | copy-start | bytes 38404
  10.1 121.0 %all-to-all-start = ((bf16[16,256,256]{2,1,0:T(8,128)(2,1)}), bf16[16,256,256]{2,1,0:T(8,128)(2,1)S(1)}, u32[]{:S(2)}, u32[]{:S(2)}) async-start(bf16[16,256,256]{2,1,0:T(8,128)(2,1)} %copy-done), calls=%async_computation | async-start | bytes 4194304 | tf_op jit(solution)/shard_map/all_to_all | solution.py:182
  27.0 165.6 %all-gather.5.cloned.1.call-start = ((), (), s32[]{:S(2)}) async-start(), calls=%async_computation.3 | async-start | bytes 7372800 | tf_op jit(solution)/shard_map/all_gather | solution.py:211
  131.2 3.1 %copy-start.4 = (bf16[128,2048]{1,0:T(8,128)(2,1)S(1)}, bf16[128,2048]{1,0:T(8,128)(2,1)}, u32[]{:S(2)}) copy-start(bf16[128,2048]{1,0:T(8,128)(2,1)} %param.4) | copy-start | bytes 1572868
  132.2 34.3 %collective-permute-start = (bf16[8,256,256]{2,1,0:T(8,128)(2,1)}, bf16[8,256,256]{2,1,0:T(8,128)(2,1)}, u32[]{:S(2)}, u32[]{:S(2)}) collective-permute-start(bf16[8,256,256]{2,1,0:T(8,128)(2,1)} %constant_dynamic-slice_fusion), channel_id=1, source_target_pairs={{0,8},{1,9},{2,10},{3,11},{4,12},{5,13},{6,14},{7,15},{8,0},{9,1},... | collective-permute-start | bytes 3145736 | tf_op jit(solution)/shard_map/ppermute | solution.py:187
  135.1 19.3 %all-to-all-start.1 = ((bf16[8,128,256]{2,1,0:T(8,128)(2,1)}), bf16[8,128,256]{2,1,0:T(8,128)(2,1)S(1)}, u32[]{:S(2)}, u32[]{:S(2)}) async-start(bf16[8,128,256]{2,1,0:T(8,128)(2,1)} %bitcast.22), calls=%async_computation.1 | async-start | bytes 1048576 | tf_op jit(solution)/shard_map/all_to_all | solution.py:175
  192.6 2.9 %copy-start.1 = (bf16[3200,1024]{1,0:T(8,128)(2,1)S(1)}, bf16[3200,1024]{1,0:T(8,128)(2,1)}, u32[]{:S(2)}) copy-start(bf16[3200,1024]{1,0:T(8,128)(2,1)} %all-gather.5.cloned.1.call-done) | copy-start | bytes 19660804
Sparse Core Ops, SparseCore 0:
  131.3 40.8 all-gather.4

commit v4 on v2

--- a/solution.py
+++ b/solution.py
@@ -20,6 +20,7 @@
 DIMS_TN = (((0,), (0,)), ((), ()))
 VMEM = 32 * 1024 * 1024
 EXTRA = 16
+N_BLK = 64
 
 
 def own_kernel(q_ref, k_ref, v_ref, acc_ref, m_ref, l_ref):
@@ -116,24 +117,27 @@
     )(ok, q, kp, vp, kn, vn, acc, m, l)
 
 
-def project_kernel(w_ref, ctx_ref, out_ref):
+def project_kernel(mirror_ref, w_ref, ctx_ref, out_ref):
     total = None
     groups, width, tok = ctx_ref.shape
     half = width // w_ref.shape[1]
     for h in range(w_ref.shape[1]):
-        ctx = ctx_ref[:, h * half : (h + 1) * half, :].reshape(groups * half, tok)
+        ctx = jnp.concatenate(
+            [ctx_ref[g ^ mirror_ref[0], h * half : (h + 1) * half, :] for g in range(groups)], axis=0
+        )
         part = jnp.dot(w_ref[0, h], ctx, preferred_element_type=jnp.float32)
         total = part if total is None else total + part
     out_ref[...] = total.astype(jnp.bfloat16)
 
 
-def project(w, ctx):
+def project(mirror, w, ctx):
     parts, cores, rows, depth = w.shape
     tok = ctx.shape[2]
     return pl.pallas_call(
         project_kernel,
         grid=(parts,),
         in_specs=[
+            pl.BlockSpec(memory_space=pltpu.SMEM),
             pl.BlockSpec((1, cores, rows, depth), lambda i: (i, 0, 0, 0)),
             pl.BlockSpec(ctx.shape, lambda i: (0, 0, 0)),
         ],
@@ -144,52 +148,73 @@
             flops=2 * parts * rows * depth * cores * tok, bytes_accessed=2 * parts * rows * depth * cores, transcendentals=0
         ),
         name="project",
-    )(w, ctx)
-
-
-def pack_kernel(k_ref, w_ref, out_ref):
-    groups, rows, width = out_ref.shape
+    )(mirror, w, ctx)
+
+
+def columns(mirror_ref, chunk, width):
+    return pl.ds(pl.multiple_of((chunk ^ mirror_ref[0]) * width, width), width)
+
+
+def pack_kernel(mirror_ref, k_ref, w_ref, out_ref):
+    groups, _, width = out_ref.shape
     tok = k_ref.shape[0]
     half = width // 2
     cols = w_ref.shape[0]
-    low = rows - tok
     for g in range(groups):
-        out_ref[g, :tok, :] = k_ref[:, g * width : (g + 1) * width]
+        out_ref[g, :tok, :] = k_ref[:, columns(mirror_ref, g, width)]
         part = w_ref[:, (g % 2) * half : (g % 2 + 1) * half]
-        out_ref[g, tok:, :half] = part[:low]
-        out_ref[g, tok : tok + cols - low, half:] = part[low:]
-        out_ref[g, tok + cols - low :, half:] = jnp.zeros((2 * low - cols, half), out_ref.dtype)
-
-
-def pack(k, wt):
+        out_ref[g, tok:, :half] = part[:EXTRA]
+        out_ref[g, tok:, half:] = jnp.concatenate(
+            [part[EXTRA:], jnp.zeros((2 * EXTRA - cols, half), part.dtype)], axis=0
+        )
+
+
+def pack(mirror, k, wt):
     tok, width = k.shape[0], wt.shape[1]
     return pl.pallas_call(
         pack_kernel,
+        in_specs=[pl.BlockSpec(memory_space=pltpu.SMEM)] + [pl.BlockSpec(memory_space=pltpu.VMEM)] * 2,
         out_shape=jax.ShapeDtypeStruct((8, tok + EXTRA, width), k.dtype),
         compiler_params=pltpu.CompilerParams(vmem_limit_bytes=VMEM),
         name="pack",
-    )(k, wt)
+    )(mirror, k, wt)
+
+
+def split_kernel(mirror_ref, in_ref, out_ref):
+    groups, _, width = out_ref.shape
+    for g in range(groups):
+        out_ref[g] = in_ref[:, columns(mirror_ref, g, width)]
+
+
+def split_heads(mirror, value):
+    tok, width = value.shape
+    return pl.pallas_call(
+        split_kernel,
+        in_specs=[pl.BlockSpec(memory_space=pltpu.SMEM), pl.BlockSpec(memory_space=pltpu.VMEM)],
+        out_shape=jax.ShapeDtypeStruct((8, tok, width // 8), value.dtype),
+        compiler_params=pltpu.CompilerParams(vmem_limit_bytes=VMEM),
+        name="split_heads",
+    )(mirror, value)
 
 
 def unpack_kernel(in_ref, k_ref, w_ref):
-    groups, rows, width = in_ref.shape
-    tok = k_ref.shape[1]
-    low = rows - tok
+    groups, tok, width = k_ref.shape
     half = width // 2
+    cols = w_ref.shape[0]
     for g in range(groups):
         k_ref[g] = in_ref[g, :tok, :]
-        w_ref[:low, g * half : (g + 1) * half] = in_ref[g, tok:, :half]
-        w_ref[low:, g * half : (g + 1) * half] = in_ref[g, tok:, half:]
-
-
-def unpack(moved):
+        w_ref[:EXTRA, g * half : (g + 1) * half] = in_ref[g, tok:, :half]
+        w_ref[EXTRA:, g * half : (g + 1) * half] = in_ref[g, tok:, half:][: cols - EXTRA]
+
+
+def unpack(moved, cols):
     groups, rows, width = moved.shape
     tok = rows - EXTRA
     return pl.pallas_call(
         unpack_kernel,
         out_shape=[
             jax.ShapeDtypeStruct((groups, tok, width), moved.dtype),
-            jax.ShapeDtypeStruct((2 * EXTRA, groups * width // 2), moved.dtype),
+            jax.ShapeDtypeStruct((cols, groups * width // 2), moved.dtype),
         ],
         compiler_params=pltpu.CompilerParams(vmem_limit_bytes=VMEM),
         name="unpack",
@@ -200,40 +225,42 @@
     return lax.all_to_all(chunks, HEAD, split_axis=0, concat_axis=0)
 
 
-def split_heads(value):
-    tok = value.shape[0]
-    return value.reshape(tok, 8, -1).transpose(1, 0, 2)
+def to_block(value, step):
+    pairs = []
+    for b in range(N_BLK):
+        to = b + step
+        if 0 <= to < N_BLK:
+            turn = 6 if (b // 8) % 2 != (to // 8) % 2 else 0
+            pairs += [(b * 8 + i, to * 8 + (i ^ turn)) for i in range(8)]
+    return lax.ppermute(value, AXES, pairs)
 
 
 def local(queries, keys, values, w_out):
     tok = queries.shape[0]
     cols, depth = w_out.shape[1], 4 * w_out.shape[0]
-    n_blk = 64
-    up = [(i, i + 1) for i in range(n_blk - 1)]
-    down = [(i + 1, i) for i in range(n_blk - 1)]
     here = lax.axis_index(BLK)
-    ok = jnp.stack([here > 0, here < n_blk - 1]).astype(jnp.int32)
-    k, w_rows = unpack(to_heads(pack(keys, w_out.T)))
+    ok = jnp.stack([here > 0, here < N_BLK - 1]).astype(jnp.int32)
+    first = lax.axis_index("zh") == 0
+    mirror = jnp.where(first, 0, 6).astype(jnp.int32)[None]
+    k, w_rows = unpack(to_heads(pack(mirror, keys, w_out.T)), cols)
     k = k.reshape(8 * tok, -1)
 
+    kp, kn = to_block(k, 1), to_block(k, -1)
+    values, k = lax.optimization_barrier((values, k))
+    v_chunks = split_heads(mirror, values)
+    v = to_heads(v_chunks).reshape(8 * tok, -1)
     other = lax.ppermute(w_rows, "zh", [(0, 1), (1, 0)])
-    kp, kn = lax.ppermute(k, BLK, up), lax.ppermute(k, BLK, down)
-    values, k = lax.optimization_barrier((values, k))
-    v = to_heads(split_heads(values)).reshape(8 * tok, -1)
-    first = lax.axis_index("zh") == 0
     pair = jnp.stack([jnp.where(first, w_rows, other), jnp.where(first, other, w_rows)])
-    line = lax.all_gather(pair.reshape(-1, depth), "y").reshape(8, 2, -1, depth)
-    kp, kn, v, queries = lax.optimization_barrier((kp, kn, v, queries))
-
-    vp, vn = lax.ppermute(v, BLK, up), lax.ppermute(v, BLK, down)
-    q = to_heads(split_heads(queries)).reshape(8 * tok, -1)
+    line = lax.all_gather(pair, "y").transpose(1, 0, 2, 3).reshape(16 * cols, depth)
+    kp, kn, v, line, queries = lax.optimization_barrier((kp, kn, v, line, queries))
+
+    weight = lax.all_gather(line, ("x", "c")).reshape(4, 2, 16 * cols, depth)
+    vp, vn = to_block(v, 1), to_block(v, -1)
+    q = to_heads(split_heads(mirror, queries)).reshape(8 * tok, -1)
     acc, m, l = own_attention(q, k, v)
-    line, acc, vp, vn = lax.optimization_barrier((line, acc, vp, vn))
-    line = line[:, :, :cols].transpose(1, 0, 2, 3).reshape(16 * cols, depth)
-    line, acc = lax.optimization_barrier((line, acc))
-    weight = lax.all_gather(line, ("x", "c")).reshape(4, 2, 16 * cols, depth)
+    vp, vn, acc = lax.optimization_barrier((vp, vn, acc))
     ctx = near_attention(ok, q, kp, vp, kn, vn, acc, m, l, tok)
-    return project(weight, to_heads(ctx)).T
+    return project(mirror, weight, to_heads(ctx)).T
 
 
 def solution(mesh):

time: 203 us -> 186 us (0.916)
  waiting for transfers between devices: 72.1 us -> 12.6 us
  blocking collectives: 44.8 us -> 84.2 us
  starting transfers between devices: 32.1 us -> 40 us
  local copies, waits for them, and re-layouts: 13.4 us -> 9.13 us
    ppermute x4, waiting for transfers between devices: 42.8 us -> 4.22 us  [to_block(): return lax.ppermute(value, AXES, pairs)]
    all_gather x0 -> x1, blocking collectives: none -> 37.8 us  [local(): lax.all_gather(pair, 'y').transpose(1, 0, 2, 3).reshape(16 * cols, depth)]
    all_gather x1, waiting for transfers between devices: 19.6 us -> 0.01 us  [local(): weight = lax.all_gather(line, ('x', 'c')).reshape(4, 2, 16 * cols, depth)]
    ppermute x4, starting transfers between devices: 15.6 us -> 20.1 us  [to_block(): return lax.ppermute(value, AXES, pairs)]
    reshape x3 -> x1, local copies, waits for them, and re-layouts: 6.32 us -> 2.4 us  [local(): lax.all_gather(pair, 'y').transpose(1, 0, 2, 3).reshape(16 * cols, depth)]
    all_to_all x2, starting transfers between devices: 8.29 us -> 11.7 us  [to_heads(): return lax.all_to_all(chunks, HEAD, split_axis=0, concat_axis=0)]
    transpose x2 -> x0, local copies, waits for them, and re-layouts: 2.41 us -> none  [local(): line = line[:, :, :cols].transpose(1, 0, 2, 3).reshape(16 * cols, depth)]
    pallas_call x2 -> x4, Pallas kernels: 3.12 us -> 4.9 us  [the longest x1 3.07 us: project(): pl.pallas_call(project_kernel, grid=(parts,), in_specs=[pl.BlockSpec(memo...]
  transfers between devices with their start and end apart: 9 -> 8, of which waited for: 6 -> 3; matrix products, arithmetic and copies ran while one was open for 2% -> 2% of each run, Pallas kernels for 10% -> 11%
where the time goes in v4:
time: 186 us; the launch traced here: 184 us
  blocking collectives  84.2 us (45%)
  starting transfers between devices  40 us (22%)
  Pallas kernels  24.1 us (13%)
  between operations  13.5 us (7%)
  waiting for transfers between devices  12.6 us (7%)
  local copies, waits for them, and re-layouts  9.13 us (5%)
    all_to_all x2, blocking collectives, to_heads(): return lax.all_to_all(chunks, HEAD, split_axis=0, concat_axis=0)  46.4 us
    all_gather x1, blocking collectives, local(): lax.all_gather(pair, 'y').transpose(1, 0, 2, 3).reshape(16 * cols, depth)  37.8 us
    ppermute x4, starting transfers between devices, to_block(): return lax.ppermute(value, AXES, pairs)  20.1 us
    pallas_call x1, Pallas kernels, near_attention(): pl.pallas_call(near_kernel, grid=(heads, rows // TILE), in_specs=[pl.Bloc...  12 us
    all_to_all x2, starting transfers between devices, to_heads(): return lax.all_to_all(chunks, HEAD, split_axis=0, concat_axis=0)  11.7 us
    ppermute x1, starting transfers between devices, local(): other = lax.ppermute(w_rows, 'zh', [(0, 1), (1, 0)])  8.22 us
    all_to_all x2, waiting for transfers between devices, to_heads(): return lax.all_to_all(chunks, HEAD, split_axis=0, concat_axis=0)  7.74 us
    pallas_call x1, Pallas kernels, own_attention(): pl.pallas_call(own_kernel, grid=(heads, rows // TILE), in_specs=[pl.Block...  7.11 us
  transfers between devices with their start and end apart: 8, of which 3 were waited for; matrix products, arithmetic and copies ran while one was open for 2% of the time, Pallas kernels for 11%

profile of v4, /device:TPU:6, one launch (start us, length us, event | category | flops | bytes accessed | tf_op | source)
XLA Modules:
  0.0 183.7 jit_solution(5223711937162064916)
XLA Ops:
  6.5 1.0 copy-done.1
  7.6 0.7 copy-done.4
  8.3 0.1 pack.1
  8.4 24.0 %all_to_all.20.in_ref = bf16[8,144,256]{2,1,0:T(8,128)(2,1)S(1)} all-to-all(bf16[8,144,256]{2,1,0:T(8,128)(2,1)S(1)} %pack.1), channel_id=1, replica_groups=mesh['x'=4,'zh'=2,'y'=8,'zl'=4,'c'=2] {'zl','c'}, dimensions={0} | all-to-all | bytes 1179648 | tf_op jit(solution)/shard_map/all_to_all | solution.py:225
  32.4 0.0 copy-start.2
  32.4 1.0 copy-done.2
  33.4 0.9 split_heads.2
  34.3 3.5 %all-to-all-start.1 = ((bf16[8,128,256]{2,1,0:T(8,128)(2,1)}), bf16[8,128,256]{2,1,0:T(8,128)(2,1)S(1)}, u32[]{:S(2)}, u32[]{:S(2)}) async-start(bf16[8,128,256]{2,1,0:T(8,128)(2,1)} %split_heads.2), calls=%async_computation.1 | async-start | bytes 1048576 | tf_op jit(solution)/shard_map/all_to_all | solution.py:225
  37.8 0.0 all-gather.4.cloned.1.call-start
  37.9 8.2 %collective-permute-start.2 = (bf16[25,1024]{1,0:T(8,128)(2,1)S(1)}, bf16[25,1024]{1,0:T(8,128)(2,1)S(1)}, u32[]{:S(2)}, u32[]{:S(2)}) collective-permute-start(bf16[25,1024]{1,0:T(8,128)(2,1)S(1)} %get-tuple-element.22), channel_id=1, source_target_pairs={{0,64},{64,0},{1,65},{65,1},{2,66},{66,2},{3,67},{67,3},{4,68},{68... | collective-permute-start | bytes 153608 | tf_op jit(solution)/shard_map/ppermute | solution.py:252
  46.1 3.5 %collective-permute-start = (bf16[1024,256]{1,0:T(8,128)(2,1)S(1)}, bf16[1024,256]{1,0:T(8,128)(2,1)S(1)}, u32[]{:S(2)}, u32[]{:S(2)}) collective-permute-start(bf16[1024,256]{1,0:T(8,128)(2,1)S(1)} %bitcast.23), channel_id=1, source_target_pairs={{0,8},{1,9},{2,10},{3,11},{4,12},{5,13},{6,14},{7,15},{8,16},{9,17... | collective-permute-start | bytes 1572872 | tf_op jit(solution)/shard_map/ppermute | solution.py:235
  49.6 6.6 %collective-permute-start.1 = (bf16[1024,256]{1,0:T(8,128)(2,1)S(1)}, bf16[1024,256]{1,0:T(8,128)(2,1)S(1)}, u32[]{:S(2)}, u32[]{:S(2)}) collective-permute-start(bf16[1024,256]{1,0:T(8,128)(2,1)S(1)} %bitcast.24), channel_id=1, source_target_pairs={{8,0},{9,1},{10,2},{11,3},{12,4},{13,5},{14,6},{15,7},{16,8},{17,9... | collective-permute-start | bytes 1572872 | tf_op jit(solution)/shard_map/ppermute | solution.py:235
  56.2 0.6 collective-permute-done.2
  56.9 37.8 %all-gather = bf16[16,25,1024]{2,1,0:T(8,128)(2,1)S(1)} all-gather(bf16[2,25,1024]{2,1,0:T(8,128)(2,1)S(1)} %pad_maximum_fusion), channel_id=2, replica_groups=mesh['x'=4,'zh'=2,'y'=8,'zl'=4,'c'=2] {'y'}, dimensions={0}, use_global_device_ids=true | all-gather | bytes 921600 | tf_op jit(solution)/shard_map/all_gather | solution.py:254
  94.7 1.1 copy.9
  95.8 2.4 %reshape.17 = bf16[400,1024]{1,0:T(8,128)(2,1)} reshape(bf16[2,8,25,1024]{3,2,1,0:T(8,128)(2,1)} %bitcast.27) | data formatting | bytes 1638400 | tf_op jit(solution)/shard_map/reshape | solution.py:254
  98.2 0.0 collective-permute-done.kp_ref
  98.2 0.0 collective-permute-done.1.kn_ref
  98.2 0.0 all-to-all-done.1
  98.2 0.0 all-gather.4.cloned.1.call-update
  98.2 0.9 split_heads.3
  99.1 8.2 %all-to-all-start.2 = ((bf16[8,128,256]{2,1,0:T(8,128)(2,1)}), bf16[8,128,256]{2,1,0:T(8,128)(2,1)S(1)}, u32[]{:S(2)}, u32[]{:S(2)}) async-start(bf16[8,128,256]{2,1,0:T(8,128)(2,1)} %split_heads.3), calls=%async_computation.2 | async-start | bytes 1048576 | tf_op jit(solution)/shard_map/all_to_all | solution.py:225
  107.3 4.2 %collective-permute-start.3 = (bf16[1024,256]{1,0:T(8,128)(2,1)S(1)}, bf16[1024,256]{1,0:T(8,128)(2,1)S(1)}, u32[]{:S(2)}, u32[]{:S(2)}) collective-permute-start(bf16[1024,256]{1,0:T(8,128)(2,1)S(1)} %bitcast.18), channel_id=1, source_target_pairs={{0,8},{1,9},{2,10},{3,11},{4,12},{5,13},{6,14},{7,15},{8,16},{9,17... | collective-permute-start | bytes 1572872 | tf_op jit(solution)/shard_map/ppermute | solution.py:235
  111.5 5.9 %collective-permute-start.4 = (bf16[1024,256]{1,0:T(8,128)(2,1)S(1)}, bf16[1024,256]{1,0:T(8,128)(2,1)}, u32[]{:S(2)}, u32[]{:S(2)}) collective-permute-start(bf16[1024,256]{1,0:T(8,128)(2,1)S(1)} %bitcast.19), channel_id=1, source_target_pairs={{8,0},{9,1},{10,2},{11,3},{12,4},{13,5},{14,6},{15,7},{16,8},{17,9... | collective-permute-start | bytes 1572872 | tf_op jit(solution)/shard_map/ppermute | solution.py:235
  117.3 0.1 add_convert_fusion.ok_ref
  117.4 7.7 %all-to-all-done.2 = bf16[8,128,256]{2,1,0:T(8,128)(2,1)S(1)} async-done(((bf16[8,128,256]{2,1,0:T(8,128)(2,1)}), bf16[8,128,256]{2,1,0:T(8,128)(2,1)S(1)}, u32[]{:S(2)}, u32[]{:S(2)}) %all-to-all-start.2) | async-done | bytes 524320 | tf_op jit(solution)/shard_map/all_to_all | solution.py:225
  125.2 7.1 %own_attention.1 = (f32[2,128,1024]{2,1,0:T(8,128)S(1)}, f32[2,8,1024]{2,1,0:T(8,128)S(1)}, f32[2,8,1024]{2,1,0:T(8,128)S(1)}) custom-call(bf16[1024,256]{1,0:T(8,128)(2,1)S(1)} %bitcast.21, bf16[1024,256]{1,0:T(8,128)(2,1)S(1)} %bitcast.25, bf16[1024,256]{1,0:T(8,128)(2,1)S(1)} %bitcast.20), custom_call_target="tpu_custom_call" | custom-call | flops 262144 | bytes 262144 | tf_op jit(solution)/shard_map/own_attention/pallas_call | solution.py:40
  132.3 4.2 %collective-permute-done.3.vp_ref = bf16[1024,256]{1,0:T(8,128)(2,1)S(1)} collective-permute-done((bf16[1024,256]{1,0:T(8,128)(2,1)S(1)}, bf16[1024,256]{1,0:T(8,128)(2,1)S(1)}, u32[]{:S(2)}, u32[]{:S(2)}) %collective-permute-start.3) | collective-permute-done | bytes 524320 | tf_op jit(solution)/shard_map/ppermute | solution.py:235
  136.5 12.0 %near_attention.1 = bf16[8,256,128]{2,1,0:T(8,128)(2,1)S(1)} custom-call(s32[2]{0:T(128)S(1)} %add_convert_fusion.ok_ref, bf16[1024,256]{1,0:T(8,128)(2,1)S(1)} %bitcast.22, bf16[1024,256]{1,0:T(8,128)(2,1)S(1)} %collective-permute-done.kp_ref, bf16[1024,256]{1,0:T(8,128)(2,1)S(1)} %collective-permute-done.3.vp_ref, ...), custom_call_target="tpu_custom_call" | custom-call | flops 2147483648 | bytes 3670016 | tf_op jit(solution)/shard_map/near_attention/pallas_call | solution.py:96
  148.5 22.4 %all_to_all.21.ctx_ref = bf16[8,256,128]{2,1,0:T(8,128)(2,1)S(1)} all-to-all(bf16[8,256,128]{2,1,0:T(8,128)(2,1)S(1)} %near_attention.1), channel_id=1, replica_groups=mesh['x'=4,'zh'=2,'y'=8,'zl'=4,'c'=2] {'zl','c'}, dimensions={0} | all-to-all | bytes 1048576 | tf_op jit(solution)/shard_map/all_to_all | solution.py:225
  170.9 2.9 %copy-done = bf16[3200,1024]{1,0:T(8,128)(2,1)S(1)} copy-done((bf16[3200,1024]{1,0:T(8,128)(2,1)S(1)}, bf16[3200,1024]{1,0:T(8,128)(2,1)}, u32[]{:S(2)}) %copy-start) | copy-done | bytes 6553624
  173.8 3.1 %project.1 = bf16[1600,128]{1,0:T(8,128)(2,1)} custom-call(s32[1]{0:T(128)} %bitcast.mirror_ref, bf16[4,2,400,1024]{3,2,1,0:T(8,128)(2,1)S(1)} %bitcast.17, bf16[8,256,128]{2,1,0:T(8,128)(2,1)S(1)} %all_to_all.21.ctx_ref), custom_call_target="tpu_custom_call" | custom-call | flops 838860800 | bytes 6553600 | tf_op jit(solution)/shard_map/project/pallas_call | solution.py:136
  (10 shorter events, 0.1 us)
Async XLA Ops:
  6.5 1.0 copy-start.1
  7.6 0.7 copy-start.4
  8.3 89.9 %copy-start.3 = (bf16[128,2048]{1,0:T(8,128)(2,1)S(1)}, bf16[128,2048]{1,0:T(8,128)(2,1)}, u32[]{:S(2)}) copy-start(bf16[128,2048]{1,0:T(8,128)(2,1)} %in_ref.1) | copy-start | bytes 1572868
  32.4 1.0 copy-start.2
  34.3 63.9 %all-to-all-start.1 = ((bf16[8,128,256]{2,1,0:T(8,128)(2,1)}), bf16[8,128,256]{2,1,0:T(8,128)(2,1)S(1)}, u32[]{:S(2)}, u32[]{:S(2)}) async-start(bf16[8,128,256]{2,1,0:T(8,128)(2,1)} %split_heads.2), calls=%async_computation.1 | async-start | bytes 1048576 | tf_op jit(solution)/shard_map/all_to_all | solution.py:225
  37.8 133.1 %all-gather.4.cloned.1.call-start = ((), (), s32[]{:S(2)}) async-start(), calls=%async_computation.4 | async-start | bytes 7372800 | tf_op jit(solution)/shard_map/all_gather | solution.py:257
  37.9 19.0 %collective-permute-start.2 = (bf16[25,1024]{1,0:T(8,128)(2,1)S(1)}, bf16[25,1024]{1,0:T(8,128)(2,1)S(1)}, u32[]{:S(2)}, u32[]{:S(2)}) collective-permute-start(bf16[25,1024]{1,0:T(8,128)(2,1)S(1)} %get-tuple-element.22), channel_id=1, source_target_pairs={{0,64},{64,0},{1,65},{65,1},{2,66},{66,2},{3,67},{67,3},{4,68},{68... | collective-permute-start | bytes 153608 | tf_op jit(solution)/shard_map/ppermute | solution.py:252
  46.1 52.1 %collective-permute-start = (bf16[1024,256]{1,0:T(8,128)(2,1)S(1)}, bf16[1024,256]{1,0:T(8,128)(2,1)S(1)}, u32[]{:S(2)}, u32[]{:S(2)}) collective-permute-start(bf16[1024,256]{1,0:T(8,128)(2,1)S(1)} %bitcast.23), channel_id=1, source_target_pairs={{0,8},{1,9},{2,10},{3,11},{4,12},{5,13},{6,14},{7,15},{8,16},{9,17... | collective-permute-start | bytes 1572872 | tf_op jit(solution)/shard_map/ppermute | solution.py:235
  49.6 48.6 %collective-permute-start.1 = (bf16[1024,256]{1,0:T(8,128)(2,1)S(1)}, bf16[1024,256]{1,0:T(8,128)(2,1)S(1)}, u32[]{:S(2)}, u32[]{:S(2)}) collective-permute-start(bf16[1024,256]{1,0:T(8,128)(2,1)S(1)} %bitcast.24), channel_id=1, source_target_pairs={{8,0},{9,1},{10,2},{11,3},{12,4},{13,5},{14,6},{15,7},{16,8},{17,9... | collective-permute-start | bytes 1572872 | tf_op jit(solution)/shard_map/ppermute | solution.py:235
  99.1 26.1 %all-to-all-start.2 = ((bf16[8,128,256]{2,1,0:T(8,128)(2,1)}), bf16[8,128,256]{2,1,0:T(8,128)(2,1)S(1)}, u32[]{:S(2)}, u32[]{:S(2)}) async-start(bf16[8,128,256]{2,1,0:T(8,128)(2,1)} %split_heads.3), calls=%async_computation.2 | async-start | bytes 1048576 | tf_op jit(solution)/shard_map/all_to_all | solution.py:225
  107.3 29.2 %collective-permute-start.3 = (bf16[1024,256]{1,0:T(8,128)(2,1)S(1)}, bf16[1024,256]{1,0:T(8,128)(2,1)S(1)}, u32[]{:S(2)}, u32[]{:S(2)}) collective-permute-start(bf16[1024,256]{1,0:T(8,128)(2,1)S(1)} %bitcast.18), channel_id=1, source_target_pairs={{0,8},{1,9},{2,10},{3,11},{4,12},{5,13},{6,14},{7,15},{8,16},{9,17... | collective-permute-start | bytes 1572872 | tf_op jit(solution)/shard_map/ppermute | solution.py:235
  111.5 25.0 %collective-permute-start.4 = (bf16[1024,256]{1,0:T(8,128)(2,1)S(1)}, bf16[1024,256]{1,0:T(8,128)(2,1)}, u32[]{:S(2)}, u32[]{:S(2)}) collective-permute-start(bf16[1024,256]{1,0:T(8,128)(2,1)S(1)} %bitcast.19), channel_id=1, source_target_pairs={{8,0},{9,1},{10,2},{11,3},{12,4},{13,5},{14,6},{15,7},{16,8},{17,9... | collective-permute-start | bytes 1572872 | tf_op jit(solution)/shard_map/ppermute | solution.py:235
  170.9 2.9 %copy-start = (bf16[3200,1024]{1,0:T(8,128)(2,1)S(1)}, bf16[3200,1024]{1,0:T(8,128)(2,1)}, u32[]{:S(2)}) copy-start(bf16[3200,1024]{1,0:T(8,128)(2,1)} %all-gather.4.cloned.1.call-done) | copy-start | bytes 19660804
Sparse Core Ops, SparseCore 0:
  98.3 56.8 all-gather.3

commit v5 on v4

--- a/solution.py
+++ b/solution.py
@@ -19,7 +19,7 @@
 DIMS_NT = (((1,), (1,)), ((), ()))
 DIMS_TN = (((0,), (0,)), ((), ()))
 VMEM = 32 * 1024 * 1024
-EXTRA = 16
+EXTRA = 32
 N_BLK = 64
 
 
@@ -117,17 +117,21 @@
     )(ok, q, kp, vp, kn, vn, acc, m, l)
 
 
-def project_kernel(mirror_ref, w_ref, ctx_ref, out_ref):
-    total = None
-    groups, width, tok = ctx_ref.shape
-    half = width // w_ref.shape[1]
-    for h in range(w_ref.shape[1]):
-        ctx = jnp.concatenate(
-            [ctx_ref[g ^ mirror_ref[0], h * half : (h + 1) * half, :] for g in range(groups)], axis=0
-        )
-        part = jnp.dot(w_ref[0, h], ctx, preferred_element_type=jnp.float32)
-        total = part if total is None else total + part
-    out_ref[...] = total.astype(jnp.bfloat16)
+def project_kernel(mirror_ref, w_ref, ctx_ref, out_ref, total_ref):
+    h = pl.program_id(1)
+    groups, width, _ = ctx_ref.shape
+    half = width // 2
+    start = pl.multiple_of(h * half, half)
+    ctx = jnp.concatenate([ctx_ref[g ^ mirror_ref[0], pl.ds(start, half), :] for g in range(groups)], axis=0)
+    part = jnp.dot(w_ref[0, 0], ctx, preferred_element_type=jnp.float32)
+
+    @pl.when(h == 0)
+    def _():
+        total_ref[...] = part
+
+    @pl.when(h == 1)
+    def _():
+        out_ref[...] = (total_ref[...] + part).astype(jnp.bfloat16)
 
 
 def project(mirror, w, ctx):
@@ -135,15 +139,16 @@
     tok = ctx.shape[2]
     return pl.pallas_call(
         project_kernel,
-        grid=(parts,),
+        grid=(parts, cores),
         in_specs=[
             pl.BlockSpec(memory_space=pltpu.SMEM),
-            pl.BlockSpec((1, cores, rows, depth), lambda i: (i, 0, 0, 0)),
-            pl.BlockSpec(ctx.shape, lambda i: (0, 0, 0)),
-        ],
-        out_specs=pl.BlockSpec((rows, tok), lambda i: (i, 0)),
+            pl.BlockSpec((1, 1, rows, depth), lambda i, h: (i, h, 0, 0)),
+            pl.BlockSpec(ctx.shape, lambda i, h: (0, 0, 0)),
+        ],
+        out_specs=pl.BlockSpec((rows, tok), lambda i, h: (i, 0)),
         out_shape=jax.ShapeDtypeStruct((parts * rows, tok), jnp.bfloat16),
-        compiler_params=pltpu.CompilerParams(vmem_limit_bytes=VMEM),
+        scratch_shapes=[pltpu.VMEM((rows, tok), jnp.float32)],
+        compiler_params=pltpu.CompilerParams(vmem_limit_bytes=56 * 1024 * 1024),
         cost_estimate=pl.CostEstimate(
             flops=2 * parts * rows * depth * cores * tok, bytes_accessed=2 * parts * rows * depth * cores, transcendentals=0
         ),
@@ -155,29 +160,27 @@
     return pl.ds(pl.multiple_of((chunk ^ mirror_ref[0]) * width, width), width)
 
 
-def pack_kernel(mirror_ref, k_ref, w_ref, out_ref):
-    groups, _, width = out_ref.shape
-    tok = k_ref.shape[0]
+def choose_kernel(core_ref, in_ref, out_ref):
+    groups, cols, width = in_ref.shape
     half = width // 2
-    cols = w_ref.shape[0]
+    span = pl.ds(pl.multiple_of(core_ref[0] * half, half), half)
+    pad = jnp.zeros((EXTRA - cols, half), out_ref.dtype)
     for g in range(groups):
-        out_ref[g, :tok, :] = k_ref[:, columns(mirror_ref, g, width)]
-        part = w_ref[:, (g % 2) * half : (g % 2 + 1) * half]
-        out_ref[g, tok:, :half] = part[:EXTRA]
-        out_ref[g, tok:, half:] = jnp.concatenate(
-            [part[EXTRA:], jnp.zeros((2 * EXTRA - cols, half), part.dtype)], axis=0
+        z, h = g // 8, g % 8
+        out_ref[z * EXTRA : (z + 1) * EXTRA, h * half : (h + 1) * half] = jnp.concatenate(
+            [in_ref[g, :, span], pad], axis=0
         )
 
 
-def pack(mirror, k, wt):
-    tok, width = k.shape[0], wt.shape[1]
-    return pl.pallas_call(
-        pack_kernel,
-        in_specs=[pl.BlockSpec(memory_space=pltpu.SMEM)] + [pl.BlockSpec(memory_space=pltpu.VMEM)] * 2,
-        out_shape=jax.ShapeDtypeStruct((8, tok + EXTRA, width), k.dtype),
-        compiler_params=pltpu.CompilerParams(vmem_limit_bytes=VMEM),
-        name="pack",
-    )(mirror, k, wt)
+def choose(core, rows):
+    groups, _, width = rows.shape
+    return pl.pallas_call(
+        choose_kernel,
+        in_specs=[pl.BlockSpec(memory_space=pltpu.SMEM), pl.BlockSpec(memory_space=pltpu.VMEM)],
+        out_shape=jax.ShapeDtypeStruct((2 * EXTRA, groups * width // 4), rows.dtype),
+        compiler_params=pltpu.CompilerParams(vmem_limit_bytes=VMEM),
+        name="choose",
+    )(core, rows)
 
 
 def split_kernel(mirror_ref, in_ref, out_ref):
@@ -197,28 +200,20 @@
     )(mirror, value)
 
 
-def unpack_kernel(in_ref, k_ref, w_ref):
-    groups, tok, width = k_ref.shape
-    half = width // 2
-    cols = w_ref.shape[0]
-    for g in range(groups):
-        k_ref[g] = in_ref[g, :tok, :]
-        w_ref[:EXTRA, g * half : (g + 1) * half] = in_ref[g, tok:, :half]
-        w_ref[EXTRA:, g * half : (g + 1) * half] = in_ref[g, tok:, half:][: cols - EXTRA]
-
-
-def unpack(moved, cols):
-    groups, rows, width = moved.shape
-    tok = rows - EXTRA
-    return pl.pallas_call(
-        unpack_kernel,
-        out_shape=[
-            jax.ShapeDtypeStruct((groups, tok, width), moved.dtype),
-            jax.ShapeDtypeStruct((cols, groups * width // 2), moved.dtype),
-        ],
-        compiler_params=pltpu.CompilerParams(vmem_limit_bytes=VMEM),
-        name="unpack",
-    )(moved)
+def tighten_kernel(cols, in_ref, out_ref):
+    line = in_ref.shape[0]
+    pieces = [in_ref[y, z * EXTRA : z * EXTRA + cols, :].astype(jnp.float32) for z in range(2) for y in range(line)]
+    out_ref[...] = jnp.concatenate(pieces, axis=0).astype(out_ref.dtype)
+
+
+def tighten(line, cols):
+    count, _, depth = line.shape
+    return pl.pallas_call(
+        functools.partial(tighten_kernel, cols),
+        out_shape=jax.ShapeDtypeStruct((2 * count * cols, depth), line.dtype),
+        compiler_params=pltpu.CompilerParams(vmem_limit_bytes=VMEM),
+        name="tighten",
+    )(line)
 
 
 def to_heads(chunks):
@@ -242,19 +237,19 @@
     ok = jnp.stack([here > 0, here < N_BLK - 1]).astype(jnp.int32)
     first = lax.axis_index("zh") == 0
     mirror = jnp.where(first, 0, 6).astype(jnp.int32)[None]
-    k, w_rows = unpack(to_heads(pack(mirror, keys, w_out.T)), cols)
-    k = k.reshape(8 * tok, -1)
+    rows = lax.all_gather(w_out.T, ("zh", "zl", "c"))
+    rows, keys = lax.optimization_barrier((rows, keys))
+    w_rows = choose(lax.axis_index("c")[None], rows)
+    k = to_heads(split_heads(mirror, keys)).reshape(8 * tok, -1)
 
     kp, kn = to_block(k, 1), to_block(k, -1)
+    line = lax.all_gather(w_rows, "y")
     values, k = lax.optimization_barrier((values, k))
-    v_chunks = split_heads(mirror, values)
-    v = to_heads(v_chunks).reshape(8 * tok, -1)
-    other = lax.ppermute(w_rows, "zh", [(0, 1), (1, 0)])
-    pair = jnp.stack([jnp.where(first, w_rows, other), jnp.where(first, other, w_rows)])
-    line = lax.all_gather(pair, "y").transpose(1, 0, 2, 3).reshape(16 * cols, depth)
-    kp, kn, v, line, queries = lax.optimization_barrier((kp, kn, v, line, queries))
-
+    v = to_heads(split_heads(mirror, values)).reshape(8 * tok, -1)
+    kp, kn, v, queries, line = lax.optimization_barrier((kp, kn, v, queries, line))
+    line = tighten(line, cols)
     weight = lax.all_gather(line, ("x", "c")).reshape(4, 2, 16 * cols, depth)
+
     vp, vn = to_block(v, 1), to_block(v, -1)
     q = to_heads(split_heads(mirror, queries)).reshape(8 * tok, -1)
     acc, m, l = own_attention(q, k, v)

time: 186 us -> 178 us (0.957)
  blocking collectives: 84.2 us -> 43 us
  waiting for transfers between devices: 12.6 us -> 48.5 us
  Pallas kernels: 24.1 us -> 31.2 us
  local copies, waits for them, and re-layouts: 9.13 us -> 3.3 us
  starting transfers between devices: 40 us -> 36.7 us
    all_to_all x2 -> x1, blocking collectives: 46.4 us -> 18.9 us  [to_heads(): return lax.all_to_all(chunks, HEAD, split_axis=0, concat_axis=0)]
    ppermute x4, waiting for transfers between devices: 4.22 us -> 29.7 us  [to_block(): return lax.ppermute(value, AXES, pairs)]
    all_gather x1, blocking collectives: 37.8 us -> 24.1 us  [local(): rows = lax.all_gather(w_out.T, ('zh', 'zl', 'c'))]
    all_to_all x2 -> x3, waiting for transfers between devices: 7.74 us -> 18.8 us  [to_heads(): return lax.all_to_all(chunks, HEAD, split_axis=0, concat_axis=0)]
    ppermute x1 -> x0, starting transfers between devices: 8.22 us -> none  [local(): other = lax.ppermute(w_rows, 'zh', [(0, 1), (1, 0)])]
    pallas_call x3, Pallas kernels: 3.19 us -> 9.52 us  [the longest x1 7.74 us: project(): pl.pallas_call(project_kernel, grid=(parts, cores), in_specs=[pl.BlockSpe...]
    ppermute x4, starting transfers between devices: 20.1 us -> 23.4 us  [to_block(): return lax.ppermute(value, AXES, pairs)]
    reshape x1 -> x0, local copies, waits for them, and re-layouts: 2.4 us -> none  [local(): lax.all_gather(pair, 'y').transpose(1, 0, 2, 3).reshape(16 * cols, depth)]
  transfers between devices with their start and end apart: 8 -> 9, of which waited for: 3 -> 4; matrix products, arithmetic and copies ran while one was open for 2% -> 0% of each run, Pallas kernels for 11% -> 12%
where the time goes in v5:
time: 178 us; the launch traced here: 176 us
  waiting for transfers between devices  48.5 us (27%)
  blocking collectives  43 us (24%)
  starting transfers between devices  36.7 us (21%)
  Pallas kernels  31.2 us (18%)
  between operations  13.5 us (8%)
  local copies, waits for them, and re-layouts  3.3 us (2%)
    ppermute x4, waiting for transfers between devices, to_block(): return lax.ppermute(value, AXES, pairs)  29.7 us
    all_gather x1, blocking collectives, local(): rows = lax.all_gather(w_out.T, ('zh', 'zl', 'c'))  24.1 us
    ppermute x4, starting transfers between devices, to_block(): return lax.ppermute(value, AXES, pairs)  23.4 us
    all_to_all x1, blocking collectives, to_heads(): return lax.all_to_all(chunks, HEAD, split_axis=0, concat_axis=0)  18.9 us
    all_to_all x3, waiting for transfers between devices, to_heads(): return lax.all_to_all(chunks, HEAD, split_axis=0, concat_axis=0)  18.8 us
    all_to_all x3, starting transfers between devices, to_heads(): return lax.all_to_all(chunks, HEAD, split_axis=0, concat_axis=0)  13.2 us
    pallas_call x1, Pallas kernels, near_attention(): pl.pallas_call(near_kernel, grid=(heads, rows // TILE), in_specs=[pl.Bloc...  12 us
    pallas_call x1, Pallas kernels, project(): pl.pallas_call(project_kernel, grid=(parts, cores), in_specs=[pl.BlockSpe...  7.74 us
  transfers between devices with their start and end apart: 9, of which 4 were waited for; matrix products, arithmetic and copies ran while one was open for 0% of the time, Pallas kernels for 12%

profile of v5, /device:TPU:6, one launch (start us, length us, event | category | flops | bytes accessed | tf_op | source)
XLA Modules:
  0.0 176.4 jit_solution(17266769083976886636)
XLA Ops:
  6.5 24.1 %all-gather.3.in_ref = bf16[16,25,256]{2,1,0:T(8,128)(2,1)S(1)} all-gather(bf16[1,25,256]{2,1,0:T(8,128)(2,1)} %bitcast.23), channel_id=2, replica_groups=mesh['x'=4,'zh'=2,'y'=8,'zl'=4,'c'=2] {'zh','zl','c'}, dimensions={0}, use_global_device_ids=true | all-gather | bytes 217600 | tf_op jit(solution)/shard_map/all_gather | solution.py:240
  30.6 1.0 copy-done.1
  31.7 0.9 split_heads.3
  32.6 3.5 %all-to-all-start = ((bf16[8,128,256]{2,1,0:T(8,128)(2,1)}), bf16[8,128,256]{2,1,0:T(8,128)(2,1)S(1)}, u32[]{:S(2)}, u32[]{:S(2)}) async-start(bf16[8,128,256]{2,1,0:T(8,128)(2,1)} %split_heads.3), calls=%async_computation | async-start | bytes 1048576 | tf_op jit(solution)/shard_map/all_to_all | solution.py:220
  36.1 0.0 all-gather.7.cloned.1.call-start
  36.1 0.7 choose.1
  36.8 0.0 all-gather.7.cloned.1.call-update
  36.8 14.5 %all-to-all-done = bf16[8,128,256]{2,1,0:T(8,128)(2,1)S(1)} async-done(((bf16[8,128,256]{2,1,0:T(8,128)(2,1)}), bf16[8,128,256]{2,1,0:T(8,128)(2,1)S(1)}, u32[]{:S(2)}, u32[]{:S(2)}) %all-to-all-start) | async-done | bytes 524320 | tf_op jit(solution)/shard_map/all_to_all | solution.py:220
  51.3 1.0 copy-done.2
  52.4 0.9 split_heads.4
  53.3 3.5 %all-to-all-start.1 = ((bf16[8,128,256]{2,1,0:T(8,128)(2,1)}), bf16[8,128,256]{2,1,0:T(8,128)(2,1)S(1)}, u32[]{:S(2)}, u32[]{:S(2)}) async-start(bf16[8,128,256]{2,1,0:T(8,128)(2,1)} %split_heads.4), calls=%async_computation.1 | async-start | bytes 1048576 | tf_op jit(solution)/shard_map/all_to_all | solution.py:220
  56.8 0.0 all-gather.9.cloned.1.call-start
  56.8 3.5 %collective-permute-start = (bf16[1024,256]{1,0:T(8,128)(2,1)S(1)}, bf16[1024,256]{1,0:T(8,128)(2,1)S(1)}, u32[]{:S(2)}, u32[]{:S(2)}) collective-permute-start(bf16[1024,256]{1,0:T(8,128)(2,1)S(1)} %bitcast.13), channel_id=1, source_target_pairs={{0,8},{1,9},{2,10},{3,11},{4,12},{5,13},{6,14},{7,15},{8,16},{9,17... | collective-permute-start | bytes 1572872 | tf_op jit(solution)/shard_map/ppermute | solution.py:230
  60.3 6.6 %collective-permute-start.1 = (bf16[1024,256]{1,0:T(8,128)(2,1)S(1)}, bf16[1024,256]{1,0:T(8,128)(2,1)S(1)}, u32[]{:S(2)}, u32[]{:S(2)}) collective-permute-start(bf16[1024,256]{1,0:T(8,128)(2,1)S(1)} %bitcast.14), channel_id=1, source_target_pairs={{8,0},{9,1},{10,2},{11,3},{12,4},{13,5},{14,6},{15,7},{16,8},{17,9... | collective-permute-start | bytes 1572872 | tf_op jit(solution)/shard_map/ppermute | solution.py:230
  66.9 20.4 %collective-permute-done.kp_ref = bf16[1024,256]{1,0:T(8,128)(2,1)S(1)} collective-permute-done((bf16[1024,256]{1,0:T(8,128)(2,1)S(1)}, bf16[1024,256]{1,0:T(8,128)(2,1)S(1)}, u32[]{:S(2)}, u32[]{:S(2)}) %collective-permute-start) | collective-permute-done | bytes 524320 | tf_op jit(solution)/shard_map/ppermute | solution.py:230
  87.3 0.0 collective-permute-done.1.kn_ref
  87.3 0.0 all-to-all-done.1
  87.3 0.0 all-gather.7.cloned.1.call-done
  87.3 1.2 copy-done
  88.6 1.1 tighten.1
  89.6 0.0 all-gather.9.cloned.1.call-update
  89.7 0.9 split_heads.5
  90.5 6.2 %all-to-all-start.2 = ((bf16[8,128,256]{2,1,0:T(8,128)(2,1)}), bf16[8,128,256]{2,1,0:T(8,128)(2,1)S(1)}, u32[]{:S(2)}, u32[]{:S(2)}) async-start(bf16[8,128,256]{2,1,0:T(8,128)(2,1)} %split_heads.5), calls=%async_computation.2 | async-start | bytes 1048576 | tf_op jit(solution)/shard_map/all_to_all | solution.py:220
  96.8 1.9 %collective-permute-start.2 = (bf16[1024,256]{1,0:T(8,128)(2,1)S(1)}, bf16[1024,256]{1,0:T(8,128)(2,1)S(1)}, u32[]{:S(2)}, u32[]{:S(2)}) collective-permute-start(bf16[1024,256]{1,0:T(8,128)(2,1)S(1)} %bitcast.16), channel_id=1, source_target_pairs={{0,8},{1,9},{2,10},{3,11},{4,12},{5,13},{6,14},{7,15},{8,16},{9,17... | collective-permute-start | bytes 1572872 | tf_op jit(solution)/shard_map/ppermute | solution.py:230
  98.7 11.5 %collective-permute-start.3 = (bf16[1024,256]{1,0:T(8,128)(2,1)S(1)}, bf16[1024,256]{1,0:T(8,128)(2,1)}, u32[]{:S(2)}, u32[]{:S(2)}) collective-permute-start(bf16[1024,256]{1,0:T(8,128)(2,1)S(1)} %bitcast.17), channel_id=1, source_target_pairs={{8,0},{9,1},{10,2},{11,3},{12,4},{13,5},{14,6},{15,7},{16,8},{17,9... | collective-permute-start | bytes 1572872 | tf_op jit(solution)/shard_map/ppermute | solution.py:230
  110.2 0.1 add_convert_fusion.ok_ref
  110.3 4.2 %all-to-all-done.2 = bf16[8,128,256]{2,1,0:T(8,128)(2,1)S(1)} async-done(((bf16[8,128,256]{2,1,0:T(8,128)(2,1)}), bf16[8,128,256]{2,1,0:T(8,128)(2,1)S(1)}, u32[]{:S(2)}, u32[]{:S(2)}) %all-to-all-start.2) | async-done | bytes 524320 | tf_op jit(solution)/shard_map/all_to_all | solution.py:220
  114.5 7.1 %own_attention.1 = (f32[2,128,1024]{2,1,0:T(8,128)S(1)}, f32[2,8,1024]{2,1,0:T(8,128)S(1)}, f32[2,8,1024]{2,1,0:T(8,128)S(1)}) custom-call(bf16[1024,256]{1,0:T(8,128)(2,1)S(1)} %bitcast.19, bf16[1024,256]{1,0:T(8,128)(2,1)S(1)} %bitcast.15, bf16[1024,256]{1,0:T(8,128)(2,1)S(1)} %bitcast.18), custom_call_target="tpu_custom_call" | custom-call | flops 262144 | bytes 262144 | tf_op jit(solution)/shard_map/own_attention/pallas_call | solution.py:40
  121.6 9.3 %collective-permute-done.2.vp_ref = bf16[1024,256]{1,0:T(8,128)(2,1)S(1)} collective-permute-done((bf16[1024,256]{1,0:T(8,128)(2,1)S(1)}, bf16[1024,256]{1,0:T(8,128)(2,1)S(1)}, u32[]{:S(2)}, u32[]{:S(2)}) %collective-permute-start.2) | collective-permute-done | bytes 524320 | tf_op jit(solution)/shard_map/ppermute | solution.py:230
  130.9 12.0 %near_attention.1 = bf16[8,256,128]{2,1,0:T(8,128)(2,1)S(1)} custom-call(s32[2]{0:T(128)S(1)} %add_convert_fusion.ok_ref, bf16[1024,256]{1,0:T(8,128)(2,1)S(1)} %bitcast.20, bf16[1024,256]{1,0:T(8,128)(2,1)S(1)} %collective-permute-done.kp_ref, bf16[1024,256]{1,0:T(8,128)(2,1)S(1)} %collective-permute-done.2.vp_ref, ...), custom_call_target="tpu_custom_call" | custom-call | flops 2147483648 | bytes 3670016 | tf_op jit(solution)/shard_map/near_attention/pallas_call | solution.py:96
  142.9 18.9 %all_to_all.20.ctx_ref = bf16[8,256,128]{2,1,0:T(8,128)(2,1)} all-to-all(bf16[8,256,128]{2,1,0:T(8,128)(2,1)S(1)} %near_attention.1), channel_id=1, replica_groups=mesh['x'=4,'zh'=2,'y'=8,'zl'=4,'c'=2] {'zl','c'}, dimensions={0} | all-to-all | bytes 1048576 | tf_op jit(solution)/shard_map/all_to_all | solution.py:220
  161.8 7.7 %project.1 = bf16[1600,128]{1,0:T(8,128)(2,1)} custom-call(s32[1]{0:T(128)} %bitcast.mirror_ref, bf16[4,2,400,1024]{3,2,1,0:T(8,128)(2,1)} %bitcast.22, bf16[8,256,128]{2,1,0:T(8,128)(2,1)} %all_to_all.20.ctx_ref), custom_call_target="tpu_custom_call" | custom-call | flops 838860800 | bytes 6553600 | tf_op jit(solution)/shard_map/project/pallas_call | solution.py:140
  (7 shorter events, 0.0 us)
Async XLA Ops:
  30.6 1.0 copy-start.1
  31.7 58.0 %copy-start.3 = (bf16[128,2048]{1,0:T(8,128)(2,1)S(1)}, bf16[128,2048]{1,0:T(8,128)(2,1)}, u32[]{:S(2)}) copy-start(bf16[128,2048]{1,0:T(8,128)(2,1)} %in_ref.2) | copy-start | bytes 1572868
  32.6 18.8 %all-to-all-start = ((bf16[8,128,256]{2,1,0:T(8,128)(2,1)}), bf16[8,128,256]{2,1,0:T(8,128)(2,1)S(1)}, u32[]{:S(2)}, u32[]{:S(2)}) async-start(bf16[8,128,256]{2,1,0:T(8,128)(2,1)} %split_heads.3), calls=%async_computation | async-start | bytes 1048576 | tf_op jit(solution)/shard_map/all_to_all | solution.py:220
  36.1 51.3 %all-gather.7.cloned.1.call-start = ((), (), s32[]{:S(2)}) async-start(), calls=%async_computation.4 | async-start | bytes 1179648 | tf_op jit(solution)/shard_map/all_gather | solution.py:246
  51.3 1.0 copy-start.2
  53.3 34.0 %all-to-all-start.1 = ((bf16[8,128,256]{2,1,0:T(8,128)(2,1)}), bf16[8,128,256]{2,1,0:T(8,128)(2,1)S(1)}, u32[]{:S(2)}, u32[]{:S(2)}) async-start(bf16[8,128,256]{2,1,0:T(8,128)(2,1)} %split_heads.4), calls=%async_computation.1 | async-start | bytes 1048576 | tf_op jit(solution)/shard_map/all_to_all | solution.py:220
  56.8 105.0 %all-gather.9.cloned.1.call-start = ((), (), s32[]{:S(2)}) async-start(), calls=%async_computation.5 | async-start | bytes 7372800 | tf_op jit(solution)/shard_map/all_gather | solution.py:251
  56.8 30.5 %collective-permute-start = (bf16[1024,256]{1,0:T(8,128)(2,1)S(1)}, bf16[1024,256]{1,0:T(8,128)(2,1)S(1)}, u32[]{:S(2)}, u32[]{:S(2)}) collective-permute-start(bf16[1024,256]{1,0:T(8,128)(2,1)S(1)} %bitcast.13), channel_id=1, source_target_pairs={{0,8},{1,9},{2,10},{3,11},{4,12},{5,13},{6,14},{7,15},{8,16},{9,17... | collective-permute-start | bytes 1572872 | tf_op jit(solution)/shard_map/ppermute | solution.py:230
  60.3 27.0 %collective-permute-start.1 = (bf16[1024,256]{1,0:T(8,128)(2,1)S(1)}, bf16[1024,256]{1,0:T(8,128)(2,1)S(1)}, u32[]{:S(2)}, u32[]{:S(2)}) collective-permute-start(bf16[1024,256]{1,0:T(8,128)(2,1)S(1)} %bitcast.14), channel_id=1, source_target_pairs={{8,0},{9,1},{10,2},{11,3},{12,4},{13,5},{14,6},{15,7},{16,8},{17,9... | collective-permute-start | bytes 1572872 | tf_op jit(solution)/shard_map/ppermute | solution.py:230
  87.3 1.2 copy-start
  90.5 23.9 %all-to-all-start.2 = ((bf16[8,128,256]{2,1,0:T(8,128)(2,1)}), bf16[8,128,256]{2,1,0:T(8,128)(2,1)S(1)}, u32[]{:S(2)}, u32[]{:S(2)}) async-start(bf16[8,128,256]{2,1,0:T(8,128)(2,1)} %split_heads.5), calls=%async_computation.2 | async-start | bytes 1048576 | tf_op jit(solution)/shard_map/all_to_all | solution.py:220
  96.8 34.1 %collective-permute-start.2 = (bf16[1024,256]{1,0:T(8,128)(2,1)S(1)}, bf16[1024,256]{1,0:T(8,128)(2,1)S(1)}, u32[]{:S(2)}, u32[]{:S(2)}) collective-permute-start(bf16[1024,256]{1,0:T(8,128)(2,1)S(1)} %bitcast.16), channel_id=1, source_target_pairs={{0,8},{1,9},{2,10},{3,11},{4,12},{5,13},{6,14},{7,15},{8,16},{9,17... | collective-permute-start | bytes 1572872 | tf_op jit(solution)/shard_map/ppermute | solution.py:230
  98.7 32.2 %collective-permute-start.3 = (bf16[1024,256]{1,0:T(8,128)(2,1)S(1)}, bf16[1024,256]{1,0:T(8,128)(2,1)}, u32[]{:S(2)}, u32[]{:S(2)}) collective-permute-start(bf16[1024,256]{1,0:T(8,128)(2,1)S(1)} %bitcast.17), channel_id=1, source_target_pairs={{8,0},{9,1},{10,2},{11,3},{12,4},{13,5},{14,6},{15,7},{16,8},{17,9... | collective-permute-start | bytes 1572872 | tf_op jit(solution)/shard_map/ppermute | solution.py:230
Sparse Core Ops, SparseCore 0:
  39.0 42.2 all-gather.6
  89.8 58.9 all-gather.8

commit v6 on v4

v6 whole, which is shorter than its diff:
```python
import functools
import math

import jax
import jax.numpy as jnp
from jax import lax
from jax.experimental import pallas as pl
from jax.experimental.pallas import tpu as pltpu
from jax.sharding import Mesh, PartitionSpec as P

HDIM = 128
LOG2E = 1.4426950408889634
FACTOR = LOG2E / math.sqrt(HDIM)
AXES = ("x", "zh", "y", "zl", "c")
SIZES = (4, 2, 8, 4, 2)
BLK = ("x", "zh", "y")
HEAD = ("zl", "c")
TILE = 1024
MIX_TILE = 1024
CHUNK = 256
PROJECT_STEP = 2
PROJECT_VMEM = 56 * 1024 * 1024
DIMS_NT = (((1,), (1,)), ((), ()))
DIMS_TN = (((0,), (0,)), ((), ()))
VMEM = 40 * 1024 * 1024
EXTRA = 32
N_BLK = 64


def score_kernel(ok_ref, q_ref, k_ref, v_ref, kp_ref, kn_ref, acc_ref, total_ref, pp_ref, pn_ref):
    far = jnp.float32(1e30)
    q = q_ref[...]
    blocks = ((k_ref, None), (kp_ref, ok_ref[0] > 0), (kn_ref, ok_ref[1] > 0))
    scores, m = [], None
    for block, (keys, ok) in enumerate(blocks):
        largest = None
        for start in range(0, keys.shape[0], CHUNK):
            s = lax.dot_general(keys[start : start + CHUNK], q, DIMS_NT, preferred_element_type=jnp.float32)
            scores.append((block, start, s))
            top = jnp.max(s, axis=0, keepdims=True)
            largest = top if largest is None else jnp.maximum(largest, top)
        largest = largest * FACTOR
        if ok is not None:
            largest = jnp.where(ok, largest, -far)
        m = largest if m is None else jnp.maximum(m, largest)
    shifts = [m if ok is None else jnp.where(ok, m, far) for _, ok in blocks]
    total, acc = jnp.zeros_like(m), None
    for block, start, s in scores:
        raised = jnp.exp2(s * FACTOR - shifts[block])
        total += jnp.sum(raised, axis=0, keepdims=True)
        probs = raised.astype(jnp.bfloat16)
        rows = slice(start, start + CHUNK)
        if block == 0:
            part = lax.dot_general(v_ref[rows], probs, DIMS_TN, preferred_element_type=jnp.float32)
            acc = part if acc is None else acc + part
        else:
            (pp_ref if block == 1 else pn_ref)[0, rows] = probs
    acc_ref[0] = acc
    total_ref[0] = jnp.broadcast_to(total, total_ref.shape[1:])


def score(ok, q, k, v, kp, kn):
    rows, width = q.shape
    heads = width // HDIM
    tile = min(TILE, rows)
    side = pl.BlockSpec((rows, HDIM), lambda h, i: (0, h))
    probs = pl.BlockSpec((1, rows, tile), lambda h, i: (h, 0, i))
    return pl.pallas_call(
        score_kernel,
        grid=(heads, rows // tile),
        in_specs=[
            pl.BlockSpec(memory_space=pltpu.SMEM),
            pl.BlockSpec((tile, HDIM), lambda h, i: (i, h)),
            side,
            side,
            side,
            side,
        ],
        out_specs=[
            pl.BlockSpec((1, HDIM, tile), lambda h, i: (h, 0, i)),
            pl.BlockSpec((1, 8, tile), lambda h, i: (h, 0, i)),
            probs,
            probs,
        ],
        out_shape=[
            jax.ShapeDtypeStruct((heads, HDIM, rows), jnp.float32),
            jax.ShapeDtypeStruct((heads, 8, rows), jnp.float32),
            jax.ShapeDtypeStruct((heads, rows, rows), jnp.bfloat16),
            jax.ShapeDtypeStruct((heads, rows, rows), jnp.bfloat16),
        ],
        compiler_params=pltpu.CompilerParams(vmem_limit_bytes=VMEM),
        cost_estimate=pl.CostEstimate(flops=rows * width, bytes_accessed=rows * width, transcendentals=0),
        name="score",
    )(ok, q, k, v, kp, kn)


def mix_kernel(pp_ref, pn_ref, vp_ref, vn_ref, acc_ref, total_ref, out_ref):
    tok = out_ref.shape[2]
    acc = acc_ref[0]
    for probs, values in ((pp_ref, vp_ref), (pn_ref, vn_ref)):
        acc += lax.dot_general(values[...], probs[0], DIMS_TN, preferred_element_type=jnp.float32)
    result = (acc / total_ref[0][:1]).astype(jnp.bfloat16)
    for part in range(out_ref.shape[0]):
        out_ref[part] = result[:, part * tok : (part + 1) * tok]


def mix(pp, pn, vp, vn, acc, total, tok):
    rows, width = vp.shape
    heads = width // HDIM
    tile = min(MIX_TILE, rows)
    side = pl.BlockSpec((rows, HDIM), lambda h, i: (0, h))
    probs = pl.BlockSpec((1, rows, tile), lambda h, i: (h, 0, i))
    return pl.pallas_call(
        mix_kernel,
        grid=(heads, rows // tile),
        in_specs=[
            probs,
            probs,
            side,
            side,
            pl.BlockSpec((1, HDIM, tile), lambda h, i: (h, 0, i)),
            pl.BlockSpec((1, 8, tile), lambda h, i: (h, 0, i)),
        ],
        out_specs=pl.BlockSpec((tile // tok, HDIM, tok), lambda h, i: (i, h, 0)),
        out_shape=jax.ShapeDtypeStruct((rows // tok, width, tok), jnp.bfloat16),
        compiler_params=pltpu.CompilerParams(vmem_limit_bytes=VMEM),
        cost_estimate=pl.CostEstimate(
            flops=4 * rows * rows * width, bytes_accessed=14 * rows * width, transcendentals=0
        ),
        name="mix",
    )(pp, pn, vp, vn, acc, total)


def project_kernel(mirror_ref, w_ref, ctx_ref, out_ref):
    groups, width, _ = ctx_ref.shape
    half = width // 2
    rows = w_ref.shape[2]
    ctx = []
    for h in range(2):
        pieces = [ctx_ref[g ^ mirror_ref[0], h * half : (h + 1) * half, :] for g in range(groups)]
        ctx.append(jnp.concatenate(pieces, axis=0))
    for part in range(w_ref.shape[0]):
        total = jnp.dot(w_ref[part, 0], ctx[0], preferred_element_type=jnp.float32)
        total += jnp.dot(w_ref[part, 1], ctx[1], preferred_element_type=jnp.float32)
        out_ref[part * rows : (part + 1) * rows] = total.astype(jnp.bfloat16)


def project(mirror, w, ctx):
    parts, halves, rows, depth = w.shape
    tok = ctx.shape[2]
    step = PROJECT_STEP
    return pl.pallas_call(
        project_kernel,
        grid=(parts // step,),
        in_specs=[
            pl.BlockSpec(memory_space=pltpu.SMEM),
            pl.BlockSpec((step, halves, rows, depth), lambda i: (i, 0, 0, 0)),
            pl.BlockSpec(ctx.shape, lambda i: (0, 0, 0)),
        ],
        out_specs=pl.BlockSpec((step * rows, tok), lambda i: (i, 0)),
        out_shape=jax.ShapeDtypeStruct((parts * rows, tok), jnp.bfloat16),
        compiler_params=pltpu.CompilerParams(vmem_limit_bytes=PROJECT_VMEM),
        cost_estimate=pl.CostEstimate(
            flops=2 * parts * rows * depth * halves * tok, bytes_accessed=2 * parts * rows * depth * halves, transcendentals=0
        ),
        name="project",
    )(mirror, w, ctx)


def columns(mirror_ref, chunk, width):
    return pl.ds(pl.multiple_of((chunk ^ mirror_ref[0]) * width, width), width)


def pack_kernel(mirror_ref, k_ref, own_ref, other_ref, out_ref):
    groups, _, width = out_ref.shape
    tok = k_ref.shape[0]
    half = width // 2
    cols = own_ref.shape[0]
    first = mirror_ref[0] == 0
    pad = jnp.zeros((EXTRA - cols, width), out_ref.dtype)
    own, other = own_ref[...].astype(jnp.float32), other_ref[...].astype(jnp.float32)
    low = jnp.where(first, own, other).astype(out_ref.dtype)
    high = jnp.where(first, other, own).astype(out_ref.dtype)
    below = []
    for c in range(2):
        span = slice(c * half, (c + 1) * half)
        below.append(jnp.concatenate([jnp.concatenate([low[:, span], high[:, span]], axis=1), pad], axis=0))
    for g in range(groups):
        out_ref[g, :tok, :] = k_ref[:, columns(mirror_ref, g, width)]
        out_ref[g, tok:, :] = below[g % 2]


def pack(mirror, k, own, other):
    tok, width = k.shape[0], own.shape[1]
    return pl.pallas_call(
        pack_kernel,
        in_specs=[pl.BlockSpec(memory_space=pltpu.SMEM)] + [pl.BlockSpec(memory_space=pltpu.VMEM)] * 3,
        out_shape=jax.ShapeDtypeStruct((8, tok + EXTRA, width), k.dtype),
        compiler_params=pltpu.CompilerParams(vmem_limit_bytes=VMEM),
        name="pack",
    )(mirror, k, own, other)


def split_kernel(mirror_ref, in_ref, out_ref):
    groups, _, width = out_ref.shape
    for g in range(groups):
        out_ref[g] = in_ref[:, columns(mirror_ref, g, width)]


def split_heads(mirror, value):
    tok, width = value.shape
    return pl.pallas_call(
        split_kernel,
        in_specs=[pl.BlockSpec(memory_space=pltpu.SMEM), pl.BlockSpec(memory_space=pltpu.VMEM)],
        out_shape=jax.ShapeDtypeStruct((8, tok, width // 8), value.dtype),
        compiler_params=pltpu.CompilerParams(vmem_limit_bytes=VMEM),
        name="split_heads",
    )(mirror, value)


def unpack_kernel(in_ref, k_ref, w_ref):
    groups, tok, width = k_ref.shape
    half = width // 2
    for g in range(groups):
        k_ref[g] = in_ref[g, :tok, :]
        for z in range(2):
            w_ref[z * EXTRA : (z + 1) * EXTRA, g * half : (g + 1) * half] = in_ref[
                g, tok:, z * half : (z + 1) * half
            ]


def unpack(moved):
    groups, rows, width = moved.shape
    tok = rows - EXTRA
    return pl.pallas_call(
        unpack_kernel,
        out_shape=[
            jax.ShapeDtypeStruct((groups, tok, width), moved.dtype),
            jax.ShapeDtypeStruct((2 * EXTRA, groups * width // 2), moved.dtype),
        ],
        compiler_params=pltpu.CompilerParams(vmem_limit_bytes=VMEM),
        name="unpack",
    )(moved)


def tighten_kernel(cols, in_ref, out_ref):
    line = in_ref.shape[0]
    pieces = [in_ref[y, z * EXTRA : z * EXTRA + cols, :].astype(jnp.float32) for z in range(2) for y in range(line)]
    out_ref[...] = jnp.concatenate(pieces, axis=0).astype(out_ref.dtype)


def tighten(line, cols):
    count, _, depth = line.shape
    return pl.pallas_call(
        functools.partial(tighten_kernel, cols),
        out_shape=jax.ShapeDtypeStruct((2 * count * cols, depth), line.dtype),
        compiler_params=pltpu.CompilerParams(vmem_limit_bytes=VMEM),
        name="tighten",
    )(line)


def to_heads(chunks):
    return lax.all_to_all(chunks, HEAD, split_axis=0, concat_axis=0)


def to_block(value, step):
    pairs = []
    for b in range(N_BLK):
        to = b + step
        if 0 <= to < N_BLK:
            turn = 6 if (b // 8) % 2 != (to // 8) % 2 else 0
            pairs += [(b * 8 + i, to * 8 + (i ^ turn)) for i in range(8)]
    return lax.ppermute(value, AXES, pairs)


def local(queries, keys, values, w_out):
    tok = queries.shape[0]
    cols, depth = w_out.shape[1], 4 * w_out.shape[0]
    here = lax.axis_index(BLK)
    ok = jnp.stack([here > 0, here < N_BLK - 1]).astype(jnp.int32)
    first = lax.axis_index("zh") == 0
    mirror = jnp.where(first, 0, 6).astype(jnp.int32)[None]
    own_w = w_out.T
    other_w = lax.ppermute(own_w, "zh", [(0, 1), (1, 0)])
    k, w_rows = unpack(to_heads(pack(mirror, keys, own_w, other_w)))
    k = k.reshape(8 * tok, -1)

    kp, kn = to_block(k, 1), to_block(k, -1)
    line = lax.all_gather(w_rows, "y")
    values, k = lax.optimization_barrier((values, k))
    v = to_heads(split_heads(mirror, values)).reshape(8 * tok, -1)
    kp, kn, v, queries, line = lax.optimization_barrier((kp, kn, v, queries, line))
    line = tighten(line, cols)
    weight = lax.all_gather(line, ("x", "c")).reshape(4, 2, 16 * cols, depth)

    vp, vn = to_block(v, 1), to_block(v, -1)
    q = to_heads(split_heads(mirror, queries)).reshape(8 * tok, -1)
    acc, total, pp, pn = score(ok, q, k, v, kp, kn)
    vp, vn, acc = lax.optimization_barrier((vp, vn, acc))
    ctx = mix(pp, pn, vp, vn, acc, total, tok)
    return project(mirror, weight, to_heads(ctx)).T


def solution(mesh):
    cut = Mesh(mesh.devices.reshape(SIZES), AXES)
    return jax.shard_map(
        local,
        mesh=cut,
        in_specs=(P(AXES, None), P(AXES, None), P(AXES, None), P(HEAD, BLK)),
        out_specs=P(AXES, None),
        check_vma=False,
    )
```

time: 186 us -> 166 us (0.89)
  the two profiles are of different devices: /device:TPU:6 before, /device:TPU:56 now
where the time goes in v6:
time: 166 us
  waiting for transfers between devices  44.7 us (27%)
  blocking collectives  42.9 us (26%)
  starting transfers between devices  38.5 us (23%)
  Pallas kernels  22 us (13%)
  between operations  13.5 us (8%)
  local copies, waits for them, and re-layouts  4.02 us (2%)
    all_to_all x2, blocking collectives, to_heads(): return lax.all_to_all(chunks, HEAD, split_axis=0, concat_axis=0)  42.9 us
    ppermute x4, waiting for transfers between devices, to_block(): return lax.ppermute(value, AXES, pairs)  35.3 us
    ppermute x4, starting transfers between devices, to_block(): return lax.ppermute(value, AXES, pairs)  19.2 us
    pallas_call x1, Pallas kernels, score(): pl.pallas_call(score_kernel, grid=(heads, rows // tile), in_specs=[pl.Blo...  11.1 us
    ppermute x1, starting transfers between devices, local(): other_w = lax.ppermute(own_w, 'zh', [(0, 1), (1, 0)])  10.9 us
    all_to_all x2, starting transfers between devices, to_heads(): return lax.all_to_all(chunks, HEAD, split_axis=0, concat_axis=0)  8.36 us
    all_to_all x2, waiting for transfers between devices, to_heads(): return lax.all_to_all(chunks, HEAD, split_axis=0, concat_axis=0)  5.49 us
    pallas_call x1, Pallas kernels, project(): pl.pallas_call(project_kernel, grid=(parts // step,), in_specs=[pl.BlockS...  4.78 us
  transfers between devices with their start and end apart: 9, of which 7 were waited for; matrix products, arithmetic and copies ran while one was open for 0% of the time, Pallas kernels for 9%

profile of v6, /device:TPU:56, one launch (start us, length us, event | category | flops | bytes accessed | tf_op | source)
XLA Modules:
  0.0 165.7 jit_solution(148690394720861256)
XLA Ops:
  6.5 10.9 %collective-permute-start = (bf16[25,256]{1,0:T(8,128)(2,1)}, bf16[25,256]{1,0:T(8,128)(2,1)S(1)}, u32[]{:S(2)}, u32[]{:S(2)}) collective-permute-start(bf16[25,256]{1,0:T(8,128)(2,1)} %bitcast.18), channel_id=1, source_target_pairs={{0,64},{64,0},{1,65},{65,1},{2,66},{66,2},{3,67},{67,3},{4,68},{68... | collective-permute-start | bytes 38408 | tf_op jit(solution)/shard_map/ppermute | solution.py:284
  17.5 1.9 %collective-permute-done.other_ref = bf16[25,256]{1,0:T(8,128)(2,1)S(1)} collective-permute-done((bf16[25,256]{1,0:T(8,128)(2,1)}, bf16[25,256]{1,0:T(8,128)(2,1)S(1)}, u32[]{:S(2)}, u32[]{:S(2)}) %collective-permute-start) | collective-permute-done | bytes 12832 | tf_op jit(solution)/shard_map/ppermute | solution.py:284
  19.4 1.0 copy-done.1
  20.4 0.7 copy-done.4
  21.1 0.1 pack.1
  21.2 22.7 %all_to_all.20.in_ref = bf16[8,160,256]{2,1,0:T(8,128)(2,1)S(1)} all-to-all(bf16[8,160,256]{2,1,0:T(8,128)(2,1)S(1)} %pack.1), channel_id=1, replica_groups=mesh['x'=4,'zh'=2,'y'=8,'zl'=4,'c'=2] {'zl','c'}, dimensions={0} | all-to-all | bytes 1310720 | tf_op jit(solution)/shard_map/all_to_all | solution.py:263
  43.9 0.7 unpack.1
  44.6 0.0 all-gather.5.cloned.1.call-update
  44.6 1.0 copy-done.2
  45.7 0.9 split_heads.2
  46.5 3.5 %all-to-all-start.1 = ((bf16[8,128,256]{2,1,0:T(8,128)(2,1)}), bf16[8,128,256]{2,1,0:T(8,128)(2,1)S(1)}, u32[]{:S(2)}, u32[]{:S(2)}) async-start(bf16[8,128,256]{2,1,0:T(8,128)(2,1)} %split_heads.2), calls=%async_computation.1 | async-start | bytes 1048576 | tf_op jit(solution)/shard_map/all_to_all | solution.py:263
  50.0 0.0 all-gather.7.cloned.1.call-start
  50.1 7.5 %collective-permute-start.1 = (bf16[1024,256]{1,0:T(8,128)(2,1)S(1)}, bf16[1024,256]{1,0:T(8,128)(2,1)S(1)}, u32[]{:S(2)}, u32[]{:S(2)}) collective-permute-start(bf16[1024,256]{1,0:T(8,128)(2,1)S(1)} %bitcast.15), channel_id=1, source_target_pairs={{0,8},{1,9},{2,10},{3,11},{4,12},{5,13},{6,14},{7,15},{8,16},{9,17... | collective-permute-start | bytes 1572872 | tf_op jit(solution)/shard_map/ppermute | solution.py:273
  57.5 1.9 %collective-permute-start.2 = (bf16[1024,256]{1,0:T(8,128)(2,1)S(1)}, bf16[1024,256]{1,0:T(8,128)(2,1)S(1)}, u32[]{:S(2)}, u32[]{:S(2)}) collective-permute-start(bf16[1024,256]{1,0:T(8,128)(2,1)S(1)} %bitcast.16), channel_id=1, source_target_pairs={{8,0},{9,1},{10,2},{11,3},{12,4},{13,5},{14,6},{15,7},{16,8},{17,9... | collective-permute-start | bytes 1572872 | tf_op jit(solution)/shard_map/ppermute | solution.py:273
  59.5 17.8 %collective-permute-done.1.kp_ref = bf16[1024,256]{1,0:T(8,128)(2,1)S(1)} collective-permute-done((bf16[1024,256]{1,0:T(8,128)(2,1)S(1)}, bf16[1024,256]{1,0:T(8,128)(2,1)S(1)}, u32[]{:S(2)}, u32[]{:S(2)}) %collective-permute-start.1) | collective-permute-done | bytes 524320 | tf_op jit(solution)/shard_map/ppermute | solution.py:273
  77.2 8.1 %collective-permute-done.2.kn_ref = bf16[1024,256]{1,0:T(8,128)(2,1)S(1)} collective-permute-done((bf16[1024,256]{1,0:T(8,128)(2,1)S(1)}, bf16[1024,256]{1,0:T(8,128)(2,1)S(1)}, u32[]{:S(2)}, u32[]{:S(2)}) %collective-permute-start.2) | collective-permute-done | bytes 524320 | tf_op jit(solution)/shard_map/ppermute | solution.py:273
  85.3 1.9 %all-gather.5.cloned.1.call-done = bf16[512,1024]{1,0:T(8,128)(2,1)} async-done(((bf16[64,1024]{1,0:T(8,128)(2,1)}), bf16[512,1024]{1,0:T(8,128)(2,1)}) %all-gather.5.cloned.1.call-update) | async-done | bytes 1048592 | tf_op jit(solution)/shard_map/all_gather | solution.py:289
  87.3 1.2 copy-done
  88.5 1.1 tighten.1
  89.6 0.0 all-gather.7.cloned.1.call-update
  89.6 0.9 split_heads.3
  90.5 4.9 %all-to-all-start.2 = ((bf16[8,128,256]{2,1,0:T(8,128)(2,1)}), bf16[8,128,256]{2,1,0:T(8,128)(2,1)S(1)}, u32[]{:S(2)}, u32[]{:S(2)}) async-start(bf16[8,128,256]{2,1,0:T(8,128)(2,1)} %split_heads.3), calls=%async_computation.2 | async-start | bytes 1048576 | tf_op jit(solution)/shard_map/all_to_all | solution.py:263
  95.3 7.8 %collective-permute-start.3 = (bf16[1024,256]{1,0:T(8,128)(2,1)S(1)}, bf16[1024,256]{1,0:T(8,128)(2,1)S(1)}, u32[]{:S(2)}, u32[]{:S(2)}) collective-permute-start(bf16[1024,256]{1,0:T(8,128)(2,1)S(1)} %bitcast.10), channel_id=1, source_target_pairs={{0,8},{1,9},{2,10},{3,11},{4,12},{5,13},{6,14},{7,15},{8,16},{9,17... | collective-permute-start | bytes 1572872 | tf_op jit(solution)/shard_map/ppermute | solution.py:273
  103.2 1.9 %collective-permute-start.4 = (bf16[1024,256]{1,0:T(8,128)(2,1)S(1)}, bf16[1024,256]{1,0:T(8,128)(2,1)}, u32[]{:S(2)}, u32[]{:S(2)}) collective-permute-start(bf16[1024,256]{1,0:T(8,128)(2,1)S(1)} %bitcast.11), channel_id=1, source_target_pairs={{8,0},{9,1},{10,2},{11,3},{12,4},{13,5},{14,6},{15,7},{16,8},{17,9... | collective-permute-start | bytes 1572872 | tf_op jit(solution)/shard_map/ppermute | solution.py:273
  105.1 0.1 add_convert_fusion.ok_ref
  105.2 5.5 %all-to-all-done.2 = bf16[8,128,256]{2,1,0:T(8,128)(2,1)S(1)} async-done(((bf16[8,128,256]{2,1,0:T(8,128)(2,1)}), bf16[8,128,256]{2,1,0:T(8,128)(2,1)S(1)}, u32[]{:S(2)}, u32[]{:S(2)}) %all-to-all-start.2) | async-done | bytes 524320 | tf_op jit(solution)/shard_map/all_to_all | solution.py:263
  110.7 11.1 %score.1 = (f32[2,128,1024]{2,1,0:T(8,128)S(1)}, f32[2,8,1024]{2,1,0:T(8,128)S(1)}, bf16[2,1024,1024]{2,1,0:T(8,128)(2,1)S(1)}, bf16[2,1024,1024]{2,1,0:T(8,128)(2,1)S(1)}) custom-call(s32[2]{0:T(128)S(1)} %add_convert_fusion.ok_ref, bf16[1024,256]{1,0:T(8,128)(2,1)S(1)} %bitcast.13, bf16[1024,256]{1,0:T(8,128)(2,1)S(1)} %bitcast.17, ...), custom_call_target="tpu_custom_call" | custom-call | flops 262144 | bytes 262144 | tf_op jit(solution)/shard_map/score/pallas_call | solution.py:68
  121.8 0.5 collective-permute-done.3.vp_ref
  122.3 8.9 %collective-permute-done.4.vn_ref = bf16[1024,256]{1,0:T(8,128)(2,1)} collective-permute-done((bf16[1024,256]{1,0:T(8,128)(2,1)S(1)}, bf16[1024,256]{1,0:T(8,128)(2,1)}, u32[]{:S(2)}, u32[]{:S(2)}) %collective-permute-start.4) | collective-permute-done | bytes 524320 | tf_op jit(solution)/shard_map/ppermute | solution.py:273
  131.2 2.6 %mix.1 = bf16[8,256,128]{2,1,0:T(8,128)(2,1)S(1)} custom-call(bf16[2,1024,1024]{2,1,0:T(8,128)(2,1)S(1)} %get-tuple-element.30.pp_ref, bf16[2,1024,1024]{2,1,0:T(8,128)(2,1)S(1)} %get-tuple-element.31.pn_ref, bf16[1024,256]{1,0:T(8,128)(2,1)S(1)} %collective-permute-done.3.vp_ref, bf16[1024,256]{1,0:T(8,128)(2,1)} %collective-permute-done.4.vn_ref, ...), custom_call_target="tpu_custom_call" | custom-call | flops 1073741824 | bytes 3670016 | tf_op jit(solution)/shard_map/mix/pallas_call | solution.py:113
  133.8 20.2 %all_to_all.21.ctx_ref = bf16[8,256,128]{2,1,0:T(8,128)(2,1)} all-to-all(bf16[8,256,128]{2,1,0:T(8,128)(2,1)S(1)} %mix.1), channel_id=1, replica_groups=mesh['x'=4,'zh'=2,'y'=8,'zl'=4,'c'=2] {'zl','c'}, dimensions={0} | all-to-all | bytes 1048576 | tf_op jit(solution)/shard_map/all_to_all | solution.py:263
  154.0 4.8 %project.1 = bf16[1600,128]{1,0:T(8,128)(2,1)} custom-call(s32[1]{0:T(128)} %bitcast.mirror_ref, bf16[4,2,400,1024]{3,2,1,0:T(8,128)(2,1)} %bitcast.20, bf16[8,256,128]{2,1,0:T(8,128)(2,1)} %all_to_all.21.ctx_ref), custom_call_target="tpu_custom_call" | custom-call | flops 838860800 | bytes 6553600 | tf_op jit(solution)/shard_map/project/pallas_call | solution.py:152
  (9 shorter events, 0.0 us)
Async XLA Ops:
  6.5 80.7 %all-gather.5.cloned.1.call-start = ((), (), s32[]{:S(2)}) async-start(), calls=%async_computation.4 | async-start | bytes 1179648 | tf_op jit(solution)/shard_map/all_gather | solution.py:289
  6.5 12.8 %collective-permute-start = (bf16[25,256]{1,0:T(8,128)(2,1)}, bf16[25,256]{1,0:T(8,128)(2,1)S(1)}, u32[]{:S(2)}, u32[]{:S(2)}) collective-permute-start(bf16[25,256]{1,0:T(8,128)(2,1)} %bitcast.18), channel_id=1, source_target_pairs={{0,64},{64,0},{1,65},{65,1},{2,66},{66,2},{3,67},{67,3},{4,68},{68... | collective-permute-start | bytes 38408 | tf_op jit(solution)/shard_map/ppermute | solution.py:284
  19.4 1.0 copy-start.1
  20.4 0.7 copy-start.4
  21.1 68.5 %copy-start.3 = (bf16[128,2048]{1,0:T(8,128)(2,1)S(1)}, bf16[128,2048]{1,0:T(8,128)(2,1)}, u32[]{:S(2)}) copy-start(bf16[128,2048]{1,0:T(8,128)(2,1)} %in_ref.1) | copy-start | bytes 1572868
  44.6 1.0 copy-start.2
  46.5 38.8 %all-to-all-start.1 = ((bf16[8,128,256]{2,1,0:T(8,128)(2,1)}), bf16[8,128,256]{2,1,0:T(8,128)(2,1)S(1)}, u32[]{:S(2)}, u32[]{:S(2)}) async-start(bf16[8,128,256]{2,1,0:T(8,128)(2,1)} %split_heads.2), calls=%async_computation.1 | async-start | bytes 1048576 | tf_op jit(solution)/shard_map/all_to_all | solution.py:263
  50.0 104.0 %all-gather.7.cloned.1.call-start = ((), (), s32[]{:S(2)}) async-start(), calls=%async_computation.5 | async-start | bytes 7372800 | tf_op jit(solution)/shard_map/all_gather | solution.py:294
  50.1 27.2 %collective-permute-start.1 = (bf16[1024,256]{1,0:T(8,128)(2,1)S(1)}, bf16[1024,256]{1,0:T(8,128)(2,1)S(1)}, u32[]{:S(2)}, u32[]{:S(2)}) collective-permute-start(bf16[1024,256]{1,0:T(8,128)(2,1)S(1)} %bitcast.15), channel_id=1, source_target_pairs={{0,8},{1,9},{2,10},{3,11},{4,12},{5,13},{6,14},{7,15},{8,16},{9,17... | collective-permute-start | bytes 1572872 | tf_op jit(solution)/shard_map/ppermute | solution.py:273
  57.5 27.8 %collective-permute-start.2 = (bf16[1024,256]{1,0:T(8,128)(2,1)S(1)}, bf16[1024,256]{1,0:T(8,128)(2,1)S(1)}, u32[]{:S(2)}, u32[]{:S(2)}) collective-permute-start(bf16[1024,256]{1,0:T(8,128)(2,1)S(1)} %bitcast.16), channel_id=1, source_target_pairs={{8,0},{9,1},{10,2},{11,3},{12,4},{13,5},{14,6},{15,7},{16,8},{17,9... | collective-permute-start | bytes 1572872 | tf_op jit(solution)/shard_map/ppermute | solution.py:273
  87.3 1.2 copy-start
  90.5 20.2 %all-to-all-start.2 = ((bf16[8,128,256]{2,1,0:T(8,128)(2,1)}), bf16[8,128,256]{2,1,0:T(8,128)(2,1)S(1)}, u32[]{:S(2)}, u32[]{:S(2)}) async-start(bf16[8,128,256]{2,1,0:T(8,128)(2,1)} %split_heads.3), calls=%async_computation.2 | async-start | bytes 1048576 | tf_op jit(solution)/shard_map/all_to_all | solution.py:263
  95.3 27.0 %collective-permute-start.3 = (bf16[1024,256]{1,0:T(8,128)(2,1)S(1)}, bf16[1024,256]{1,0:T(8,128)(2,1)S(1)}, u32[]{:S(2)}, u32[]{:S(2)}) collective-permute-start(bf16[1024,256]{1,0:T(8,128)(2,1)S(1)} %bitcast.10), channel_id=1, source_target_pairs={{0,8},{1,9},{2,10},{3,11},{4,12},{5,13},{6,14},{7,15},{8,16},{9,17... | collective-permute-start | bytes 1572872 | tf_op jit(solution)/shard_map/ppermute | solution.py:273
  103.2 28.0 %collective-permute-start.4 = (bf16[1024,256]{1,0:T(8,128)(2,1)S(1)}, bf16[1024,256]{1,0:T(8,128)(2,1)}, u32[]{:S(2)}, u32[]{:S(2)}) collective-permute-start(bf16[1024,256]{1,0:T(8,128)(2,1)S(1)} %bitcast.11), channel_id=1, source_target_pairs={{8,0},{9,1},{10,2},{11,3},{12,4},{13,5},{14,6},{15,7},{16,8},{17,9... | collective-permute-start | bytes 1572872 | tf_op jit(solution)/shard_map/ppermute | solution.py:273
Sparse Core Ops, SparseCore 0:
  44.7 42.4 all-gather.4
  89.7 47.1 all-gather.6

commit v7 on v6

--- a/solution.py
+++ b/solution.py
@@ -18,12 +18,12 @@
 TILE = 1024
 MIX_TILE = 1024
 CHUNK = 256
-PROJECT_STEP = 2
+PROJECT_STEP = 4
 PROJECT_VMEM = 56 * 1024 * 1024
 DIMS_NT = (((1,), (1,)), ((), ()))
 DIMS_TN = (((0,), (0,)), ((), ()))
 VMEM = 40 * 1024 * 1024
-EXTRA = 32
+EXTRA = 16
 N_BLK = 64
 
 
@@ -131,37 +131,47 @@
     )(pp, pn, vp, vn, acc, total)
 
 
-def project_kernel(mirror_ref, w_ref, ctx_ref, out_ref):
+def project_kernel(cols, mirror_ref, w_ref, ctx_ref, out_ref, total_ref):
+    step = pl.program_id(0)
     groups, width, _ = ctx_ref.shape
     half = width // 2
-    rows = w_ref.shape[2]
+    lines, _, rows, _ = w_ref.shape
     ctx = []
     for h in range(2):
         pieces = [ctx_ref[g ^ mirror_ref[0], h * half : (h + 1) * half, :] for g in range(groups)]
         ctx.append(jnp.concatenate(pieces, axis=0))
-    for part in range(w_ref.shape[0]):
+    for part in range(lines):
         total = jnp.dot(w_ref[part, 0], ctx[0], preferred_element_type=jnp.float32)
         total += jnp.dot(w_ref[part, 1], ctx[1], preferred_element_type=jnp.float32)
-        out_ref[part * rows : (part + 1) * rows] = total.astype(jnp.bfloat16)
-
-
-def project(mirror, w, ctx):
-    parts, halves, rows, depth = w.shape
+        total_ref[step * lines + part] = total
+
+    @pl.when(step == pl.num_programs(0) - 1)
+    def _():
+        pieces = []
+        for outer in range(rows // cols):
+            for y in range(total_ref.shape[0]):
+                pieces.append(total_ref[y, outer * cols : (outer + 1) * cols, :])
+        out_ref[...] = jnp.concatenate(pieces, axis=0).astype(jnp.bfloat16)
+
+
+def project(mirror, w, ctx, cols):
+    count, halves, rows, depth = w.shape
     tok = ctx.shape[2]
     step = PROJECT_STEP
     return pl.pallas_call(
-        project_kernel,
-        grid=(parts // step,),
+        functools.partial(project_kernel, cols),
+        grid=(count // step,),
         in_specs=[
             pl.BlockSpec(memory_space=pltpu.SMEM),
             pl.BlockSpec((step, halves, rows, depth), lambda i: (i, 0, 0, 0)),
             pl.BlockSpec(ctx.shape, lambda i: (0, 0, 0)),
         ],
-        out_specs=pl.BlockSpec((step * rows, tok), lambda i: (i, 0)),
-        out_shape=jax.ShapeDtypeStruct((parts * rows, tok), jnp.bfloat16),
+        out_specs=pl.BlockSpec((count * rows, tok), lambda i: (0, 0)),
+        out_shape=jax.ShapeDtypeStruct((count * rows, tok), jnp.bfloat16),
+        scratch_shapes=[pltpu.VMEM((count, rows, tok), jnp.float32)],
         compiler_params=pltpu.CompilerParams(vmem_limit_bytes=PROJECT_VMEM),
         cost_estimate=pl.CostEstimate(
-            flops=2 * parts * rows * depth * halves * tok, bytes_accessed=2 * parts * rows * depth * halves, transcendentals=0
+            flops=2 * count * rows * depth * halves * tok, bytes_accessed=2 * count * rows * depth * halves, transcendentals=0
         ),
         name="project",
     )(mirror, w, ctx)
@@ -171,34 +181,29 @@
     return pl.ds(pl.multiple_of((chunk ^ mirror_ref[0]) * width, width), width)
 
 
-def pack_kernel(mirror_ref, k_ref, own_ref, other_ref, out_ref):
+def pack_kernel(mirror_ref, k_ref, w_ref, out_ref):
     groups, _, width = out_ref.shape
     tok = k_ref.shape[0]
     half = width // 2
-    cols = own_ref.shape[0]
-    first = mirror_ref[0] == 0
-    pad = jnp.zeros((EXTRA - cols, width), out_ref.dtype)
-    own, other = own_ref[...].astype(jnp.float32), other_ref[...].astype(jnp.float32)
-    low = jnp.where(first, own, other).astype(out_ref.dtype)
-    high = jnp.where(first, other, own).astype(out_ref.dtype)
-    below = []
-    for c in range(2):
-        span = slice(c * half, (c + 1) * half)
-        below.append(jnp.concatenate([jnp.concatenate([low[:, span], high[:, span]], axis=1), pad], axis=0))
+    cols = w_ref.shape[0]
     for g in range(groups):
         out_ref[g, :tok, :] = k_ref[:, columns(mirror_ref, g, width)]
-        out_ref[g, tok:, :] = below[g % 2]
-
-
-def pack(mirror, k, own, other):
-    tok, width = k.shape[0], own.shape[1]
+        part = w_ref[:, (g % 2) * half : (g % 2 + 1) * half]
+        out_ref[g, tok:, :half] = part[:EXTRA]
+        out_ref[g, tok:, half:] = jnp.concatenate(
+            [part[EXTRA:], jnp.zeros((2 * EXTRA - cols, half), part.dtype)], axis=0
+        )
+
+
+def pack(mirror, k, wt):
+    tok, width = k.shape[0], wt.shape[1]
     return pl.pallas_call(
         pack_kernel,
-        in_specs=[pl.BlockSpec(memory_space=pltpu.SMEM)] + [pl.BlockSpec(memory_space=pltpu.VMEM)] * 3,
+        in_specs=[pl.BlockSpec(memory_space=pltpu.SMEM)] + [pl.BlockSpec(memory_space=pltpu.VMEM)] * 2,
         out_shape=jax.ShapeDtypeStruct((8, tok + EXTRA, width), k.dtype),
         compiler_params=pltpu.CompilerParams(vmem_limit_bytes=VMEM),
         name="pack",
-    )(mirror, k, own, other)
+    )(mirror, k, wt)
 
 
 def split_kernel(mirror_ref, in_ref, out_ref):
@@ -223,10 +228,8 @@
     half = width // 2
     for g in range(groups):
         k_ref[g] = in_ref[g, :tok, :]
-        for z in range(2):
-            w_ref[z * EXTRA : (z + 1) * EXTRA, g * half : (g + 1) * half] = in_ref[
-                g, tok:, z * half : (z + 1) * half
-            ]
+        w_ref[:EXTRA, g * half : (g + 1) * half] = in_ref[g, tok:, :half]
+        w_ref[EXTRA:, g * half : (g + 1) * half] = in_ref[g, tok:, half:]
 
 
 def unpack(moved):
@@ -244,8 +247,11 @@
 
 
 def tighten_kernel(cols, in_ref, out_ref):
-    line = in_ref.shape[0]
-    pieces = [in_ref[y, z * EXTRA : z * EXTRA + cols, :].astype(jnp.float32) for z in range(2) for y in range(line)]
+    rows = 2 * EXTRA
+    pieces = []
+    for x in range(in_ref.shape[0]):
+        for z in range(2):
+            pieces.append(in_ref[x, z * rows : z * rows + cols, :].astype(jnp.float32))
     out_ref[...] = jnp.concatenate(pieces, axis=0).astype(out_ref.dtype)
 
 
@@ -280,25 +286,24 @@
     ok = jnp.stack([here > 0, here < N_BLK - 1]).astype(jnp.int32)
     first = lax.axis_index("zh") == 0
     mirror = jnp.where(first, 0, 6).astype(jnp.int32)[None]
-    own_w = w_out.T
-    other_w = lax.ppermute(own_w, "zh", [(0, 1), (1, 0)])
-    k, w_rows = unpack(to_heads(pack(mirror, keys, own_w, other_w)))
+    k, w_rows = unpack(to_heads(pack(mirror, keys, w_out.T)))
     k = k.reshape(8 * tok, -1)
 
     kp, kn = to_block(k, 1), to_block(k, -1)
-    line = lax.all_gather(w_rows, "y")
     values, k = lax.optimization_barrier((values, k))
     v = to_heads(split_heads(mirror, values)).reshape(8 * tok, -1)
-    kp, kn, v, queries, line = lax.optimization_barrier((kp, kn, v, queries, line))
-    line = tighten(line, cols)
-    weight = lax.all_gather(line, ("x", "c")).reshape(4, 2, 16 * cols, depth)
-
+    other = lax.ppermute(w_rows, "zh", [(0, 1), (1, 0)])
+    pair = jnp.concatenate([jnp.where(first, w_rows, other), jnp.where(first, other, w_rows)])
+    line = tighten(lax.all_gather(pair, "x"), cols)
+    kp, kn, v, line, queries = lax.optimization_barrier((kp, kn, v, line, queries))
+
+    weight = lax.all_gather(line, ("y", "c")).reshape(8, 2, 8 * cols, depth)
     vp, vn = to_block(v, 1), to_block(v, -1)
     q = to_heads(split_heads(mirror, queries)).reshape(8 * tok, -1)
     acc, total, pp, pn = score(ok, q, k, v, kp, kn)
     vp, vn, acc = lax.optimization_barrier((vp, vn, acc))
     ctx = mix(pp, pn, vp, vn, acc, total, tok)
-    return project(mirror, weight, to_heads(ctx)).T
+    return project(mirror, weight, to_heads(ctx), cols).T
 
 
 def solution(mesh):

time: 166 us -> 155 us (0.934)
  the two profiles are of different devices: /device:TPU:56 before, /device:TPU:6 now
where the time goes in v7:
time: 155 us; the launch traced here: 152 us
  blocking collectives  58.4 us (38%)
  starting transfers between devices  40.8 us (26%)
  Pallas kernels  21.4 us (14%)
  waiting for transfers between devices  14.8 us (10%)
  between operations  13.5 us (9%)
  local copies, waits for them, and re-layouts  2.8 us (2%)
    all_to_all x2, blocking collectives, to_heads(): return lax.all_to_all(chunks, HEAD, split_axis=0, concat_axis=0)  44.1 us
    ppermute x4, starting transfers between devices, to_block(): return lax.ppermute(value, AXES, pairs)  21.8 us
    all_gather x1, blocking collectives, local(): line = tighten(lax.all_gather(pair, 'x'), cols)  14.2 us
    pallas_call x1, Pallas kernels, score(): pl.pallas_call(score_kernel, grid=(heads, rows // tile), in_specs=[pl.Blo...  11.1 us
    all_to_all x2, starting transfers between devices, to_heads(): return lax.all_to_all(chunks, HEAD, split_axis=0, concat_axis=0)  10.8 us
    ppermute x1, starting transfers between devices, local(): other = lax.ppermute(w_rows, 'zh', [(0, 1), (1, 0)])  8.22 us
    ppermute x4, waiting for transfers between devices, to_block(): return lax.ppermute(value, AXES, pairs)  8.1 us
    all_to_all x2, waiting for transfers between devices, to_heads(): return lax.all_to_all(chunks, HEAD, split_axis=0, concat_axis=0)  6.02 us
  transfers between devices with their start and end apart: 8, of which 5 were waited for; matrix products, arithmetic and copies ran while one was open for 0% of the time, Pallas kernels for 10%

profile of v7, /device:TPU:6, one launch (start us, length us, event | category | flops | bytes accessed | tf_op | source)
XLA Modules:
  0.0 151.8 jit_solution(2427457684332323329)
XLA Ops:
  6.5 1.0 copy-done
  7.6 0.7 copy-done.3
  8.3 0.1 pack.1
  8.4 24.0 %all_to_all.20.in_ref = bf16[8,144,256]{2,1,0:T(8,128)(2,1)S(1)} all-to-all(bf16[8,144,256]{2,1,0:T(8,128)(2,1)S(1)} %pack.1), channel_id=1, replica_groups=mesh['x'=4,'zh'=2,'y'=8,'zl'=4,'c'=2] {'zl','c'}, dimensions={0} | all-to-all | bytes 1179648 | tf_op jit(solution)/shard_map/all_to_all | solution.py:269
  32.4 0.0 copy-start.1
  32.4 1.0 copy-done.1
  33.4 0.9 split_heads.2
  34.3 3.5 %all-to-all-start.1 = ((bf16[8,128,256]{2,1,0:T(8,128)(2,1)}), bf16[8,128,256]{2,1,0:T(8,128)(2,1)S(1)}, u32[]{:S(2)}, u32[]{:S(2)}) async-start(bf16[8,128,256]{2,1,0:T(8,128)(2,1)} %split_heads.2), calls=%async_computation.1 | async-start | bytes 1048576 | tf_op jit(solution)/shard_map/all_to_all | solution.py:269
  37.8 0.0 all-gather.4.cloned.1.call-start
  37.8 8.2 %collective-permute-start.2 = (bf16[32,1024]{1,0:T(8,128)(2,1)S(1)}, bf16[32,1024]{1,0:T(8,128)(2,1)S(1)}, u32[]{:S(2)}, u32[]{:S(2)}) collective-permute-start(bf16[32,1024]{1,0:T(8,128)(2,1)S(1)} %get-tuple-element.23), channel_id=1, source_target_pairs={{0,64},{64,0},{1,65},{65,1},{2,66},{66,2},{3,67},{67,3},{4,68},{68... | collective-permute-start | bytes 196616 | tf_op jit(solution)/shard_map/ppermute | solution.py:295
  46.1 3.5 %collective-permute-start = (bf16[1024,256]{1,0:T(8,128)(2,1)S(1)}, bf16[1024,256]{1,0:T(8,128)(2,1)S(1)}, u32[]{:S(2)}, u32[]{:S(2)}) collective-permute-start(bf16[1024,256]{1,0:T(8,128)(2,1)S(1)} %bitcast.15), channel_id=1, source_target_pairs={{0,8},{1,9},{2,10},{3,11},{4,12},{5,13},{6,14},{7,15},{8,16},{9,17... | collective-permute-start | bytes 1572872 | tf_op jit(solution)/shard_map/ppermute | solution.py:279
  49.6 6.6 %collective-permute-start.1 = (bf16[1024,256]{1,0:T(8,128)(2,1)S(1)}, bf16[1024,256]{1,0:T(8,128)(2,1)S(1)}, u32[]{:S(2)}, u32[]{:S(2)}) collective-permute-start(bf16[1024,256]{1,0:T(8,128)(2,1)S(1)} %bitcast.16), channel_id=1, source_target_pairs={{8,0},{9,1},{10,2},{11,3},{12,4},{13,5},{14,6},{15,7},{16,8},{17,9... | collective-permute-start | bytes 1572872 | tf_op jit(solution)/shard_map/ppermute | solution.py:279
  56.2 0.6 collective-permute-done.2
  56.8 14.2 %all-gather = bf16[256,1024]{1,0:T(8,128)(2,1)S(1)} all-gather(bf16[64,1024]{1,0:T(8,128)(2,1)S(1)} %pad_maximum_fusion), channel_id=2, replica_groups=mesh['x'=4,'zh'=2,'y'=8,'zl'=4,'c'=2] {'x'}, dimensions={0}, use_global_device_ids=true | all-gather | bytes 655360 | tf_op jit(solution)/shard_map/all_gather | solution.py:297
  71.0 0.9 tighten.1
  71.9 4.3 %collective-permute-done.kp_ref = bf16[1024,256]{1,0:T(8,128)(2,1)S(1)} collective-permute-done((bf16[1024,256]{1,0:T(8,128)(2,1)S(1)}, bf16[1024,256]{1,0:T(8,128)(2,1)S(1)}, u32[]{:S(2)}, u32[]{:S(2)}) %collective-permute-start) | collective-permute-done | bytes 524320 | tf_op jit(solution)/shard_map/ppermute | solution.py:279
  76.2 0.0 collective-permute-done.1.kn_ref
  76.2 0.0 all-to-all-done.1
  76.2 0.0 all-gather.4.cloned.1.call-update
  76.2 0.0 copy-done.2
  76.3 0.9 split_heads.3
  77.1 7.3 %all-to-all-start.2 = ((bf16[8,128,256]{2,1,0:T(8,128)(2,1)}), bf16[8,128,256]{2,1,0:T(8,128)(2,1)S(1)}, u32[]{:S(2)}, u32[]{:S(2)}) async-start(bf16[8,128,256]{2,1,0:T(8,128)(2,1)} %split_heads.3), calls=%async_computation.2 | async-start | bytes 1048576 | tf_op jit(solution)/shard_map/all_to_all | solution.py:269
  84.4 1.9 %collective-permute-start.3 = (bf16[1024,256]{1,0:T(8,128)(2,1)S(1)}, bf16[1024,256]{1,0:T(8,128)(2,1)S(1)}, u32[]{:S(2)}, u32[]{:S(2)}) collective-permute-start(bf16[1024,256]{1,0:T(8,128)(2,1)S(1)} %bitcast.11), channel_id=1, source_target_pairs={{0,8},{1,9},{2,10},{3,11},{4,12},{5,13},{6,14},{7,15},{8,16},{9,17... | collective-permute-start | bytes 1572872 | tf_op jit(solution)/shard_map/ppermute | solution.py:279
  86.3 9.8 %collective-permute-start.4 = (bf16[1024,256]{1,0:T(8,128)(2,1)S(1)}, bf16[1024,256]{1,0:T(8,128)(2,1)}, u32[]{:S(2)}, u32[]{:S(2)}) collective-permute-start(bf16[1024,256]{1,0:T(8,128)(2,1)S(1)} %bitcast.12), channel_id=1, source_target_pairs={{8,0},{9,1},{10,2},{11,3},{12,4},{13,5},{14,6},{15,7},{16,8},{17,9... | collective-permute-start | bytes 1572872 | tf_op jit(solution)/shard_map/ppermute | solution.py:279
  96.2 0.1 add_convert_fusion.ok_ref
  96.3 6.0 %all-to-all-done.2 = bf16[8,128,256]{2,1,0:T(8,128)(2,1)S(1)} async-done(((bf16[8,128,256]{2,1,0:T(8,128)(2,1)}), bf16[8,128,256]{2,1,0:T(8,128)(2,1)S(1)}, u32[]{:S(2)}, u32[]{:S(2)}) %all-to-all-start.2) | async-done | bytes 524320 | tf_op jit(solution)/shard_map/all_to_all | solution.py:269
  102.3 11.1 %score.1 = (f32[2,128,1024]{2,1,0:T(8,128)S(1)}, f32[2,8,1024]{2,1,0:T(8,128)S(1)}, bf16[2,1024,1024]{2,1,0:T(8,128)(2,1)S(1)}, bf16[2,1024,1024]{2,1,0:T(8,128)(2,1)S(1)}) custom-call(s32[2]{0:T(128)S(1)} %add_convert_fusion.ok_ref, bf16[1024,256]{1,0:T(8,128)(2,1)S(1)} %bitcast.14, bf16[1024,256]{1,0:T(8,128)(2,1)S(1)} %bitcast.17, ...), custom_call_target="tpu_custom_call" | custom-call | flops 262144 | bytes 262144 | tf_op jit(solution)/shard_map/score/pallas_call | solution.py:68
  113.4 3.7 %collective-permute-done.3.vp_ref = bf16[1024,256]{1,0:T(8,128)(2,1)S(1)} collective-permute-done((bf16[1024,256]{1,0:T(8,128)(2,1)S(1)}, bf16[1024,256]{1,0:T(8,128)(2,1)S(1)}, u32[]{:S(2)}, u32[]{:S(2)}) %collective-permute-start.3) | collective-permute-done | bytes 524320 | tf_op jit(solution)/shard_map/ppermute | solution.py:279
  117.0 0.1 collective-permute-done.4.vn_ref
  117.2 2.6 %mix.1 = bf16[8,256,128]{2,1,0:T(8,128)(2,1)S(1)} custom-call(bf16[2,1024,1024]{2,1,0:T(8,128)(2,1)S(1)} %get-tuple-element.30.pp_ref, bf16[2,1024,1024]{2,1,0:T(8,128)(2,1)S(1)} %get-tuple-element.31.pn_ref, bf16[1024,256]{1,0:T(8,128)(2,1)S(1)} %collective-permute-done.3.vp_ref, bf16[1024,256]{1,0:T(8,128)(2,1)} %collective-permute-done.4.vn_ref, ...), custom_call_target="tpu_custom_call" | custom-call | flops 1073741824 | bytes 3670016 | tf_op jit(solution)/shard_map/mix/pallas_call | solution.py:113
  119.8 20.2 %all_to_all.21.ctx_ref = bf16[8,256,128]{2,1,0:T(8,128)(2,1)} all-to-all(bf16[8,256,128]{2,1,0:T(8,128)(2,1)S(1)} %mix.1), channel_id=1, replica_groups=mesh['x'=4,'zh'=2,'y'=8,'zl'=4,'c'=2] {'zl','c'}, dimensions={0} | all-to-all | bytes 1048576 | tf_op jit(solution)/shard_map/all_to_all | solution.py:269
  140.0 5.0 %project.1 = bf16[1600,128]{1,0:T(8,128)(2,1)} custom-call(s32[1]{0:T(128)} %bitcast.mirror_ref, bf16[8,2,200,1024]{3,2,1,0:T(8,128)(2,1)} %bitcast.19, bf16[8,256,128]{2,1,0:T(8,128)(2,1)} %all_to_all.21.ctx_ref), custom_call_target="tpu_custom_call" | custom-call | flops 838860800 | bytes 6553600 | tf_op jit(solution)/shard_map/project/pallas_call | solution.py:161
  (7 shorter events, 0.1 us)
Async XLA Ops:
  6.5 1.0 copy-start
  7.6 0.7 copy-start.3
  8.3 68.0 %copy-start.2 = (bf16[128,2048]{1,0:T(8,128)(2,1)S(1)}, bf16[128,2048]{1,0:T(8,128)(2,1)}, u32[]{:S(2)}) copy-start(bf16[128,2048]{1,0:T(8,128)(2,1)} %in_ref.1) | copy-start | bytes 1572868
  32.4 1.0 copy-start.1
  34.3 41.9 %all-to-all-start.1 = ((bf16[8,128,256]{2,1,0:T(8,128)(2,1)}), bf16[8,128,256]{2,1,0:T(8,128)(2,1)S(1)}, u32[]{:S(2)}, u32[]{:S(2)}) async-start(bf16[8,128,256]{2,1,0:T(8,128)(2,1)} %split_heads.2), calls=%async_computation.1 | async-start | bytes 1048576 | tf_op jit(solution)/shard_map/all_to_all | solution.py:269
  37.8 102.2 %all-gather.4.cloned.1.call-start = ((), (), s32[]{:S(2)}) async-start(), calls=%async_computation.4 | async-start | bytes 6963200 | tf_op jit(solution)/shard_map/all_gather | solution.py:300
  37.8 19.0 %collective-permute-start.2 = (bf16[32,1024]{1,0:T(8,128)(2,1)S(1)}, bf16[32,1024]{1,0:T(8,128)(2,1)S(1)}, u32[]{:S(2)}, u32[]{:S(2)}) collective-permute-start(bf16[32,1024]{1,0:T(8,128)(2,1)S(1)} %get-tuple-element.23), channel_id=1, source_target_pairs={{0,64},{64,0},{1,65},{65,1},{2,66},{66,2},{3,67},{67,3},{4,68},{68... | collective-permute-start | bytes 196616 | tf_op jit(solution)/shard_map/ppermute | solution.py:295
  46.1 30.1 %collective-permute-start = (bf16[1024,256]{1,0:T(8,128)(2,1)S(1)}, bf16[1024,256]{1,0:T(8,128)(2,1)S(1)}, u32[]{:S(2)}, u32[]{:S(2)}) collective-permute-start(bf16[1024,256]{1,0:T(8,128)(2,1)S(1)} %bitcast.15), channel_id=1, source_target_pairs={{0,8},{1,9},{2,10},{3,11},{4,12},{5,13},{6,14},{7,15},{8,16},{9,17... | collective-permute-start | bytes 1572872 | tf_op jit(solution)/shard_map/ppermute | solution.py:279
  49.6 26.7 %collective-permute-start.1 = (bf16[1024,256]{1,0:T(8,128)(2,1)S(1)}, bf16[1024,256]{1,0:T(8,128)(2,1)S(1)}, u32[]{:S(2)}, u32[]{:S(2)}) collective-permute-start(bf16[1024,256]{1,0:T(8,128)(2,1)S(1)} %bitcast.16), channel_id=1, source_target_pairs={{8,0},{9,1},{10,2},{11,3},{12,4},{13,5},{14,6},{15,7},{16,8},{17,9... | collective-permute-start | bytes 1572872 | tf_op jit(solution)/shard_map/ppermute | solution.py:279
  77.1 25.2 %all-to-all-start.2 = ((bf16[8,128,256]{2,1,0:T(8,128)(2,1)}), bf16[8,128,256]{2,1,0:T(8,128)(2,1)S(1)}, u32[]{:S(2)}, u32[]{:S(2)}) async-start(bf16[8,128,256]{2,1,0:T(8,128)(2,1)} %split_heads.3), calls=%async_computation.2 | async-start | bytes 1048576 | tf_op jit(solution)/shard_map/all_to_all | solution.py:269
  84.4 32.6 %collective-permute-start.3 = (bf16[1024,256]{1,0:T(8,128)(2,1)S(1)}, bf16[1024,256]{1,0:T(8,128)(2,1)S(1)}, u32[]{:S(2)}, u32[]{:S(2)}) collective-permute-start(bf16[1024,256]{1,0:T(8,128)(2,1)S(1)} %bitcast.11), channel_id=1, source_target_pairs={{0,8},{1,9},{2,10},{3,11},{4,12},{5,13},{6,14},{7,15},{8,16},{9,17... | collective-permute-start | bytes 1572872 | tf_op jit(solution)/shard_map/ppermute | solution.py:279
  86.3 30.8 %collective-permute-start.4 = (bf16[1024,256]{1,0:T(8,128)(2,1)S(1)}, bf16[1024,256]{1,0:T(8,128)(2,1)}, u32[]{:S(2)}, u32[]{:S(2)}) collective-permute-start(bf16[1024,256]{1,0:T(8,128)(2,1)S(1)} %bitcast.12), channel_id=1, source_target_pairs={{8,0},{9,1},{10,2},{11,3},{12,4},{13,5},{14,6},{15,7},{16,8},{17,9... | collective-permute-start | bytes 1572872 | tf_op jit(solution)/shard_map/ppermute | solution.py:279
Sparse Core Ops, SparseCore 0:
  76.4 60.2 all-gather.3

commit v8 on v7

--- a/solution.py
+++ b/solution.py
@@ -29,7 +29,9 @@
 
 def score_kernel(ok_ref, q_ref, k_ref, v_ref, kp_ref, kn_ref, acc_ref, total_ref, pp_ref, pn_ref):
     far = jnp.float32(1e30)
-    q = q_ref[...]
+    chunks, tok, _ = q_ref.shape
+    q = q_ref[...].reshape(chunks * tok, HDIM)
+    own = v_ref[...].reshape(chunks * tok, HDIM)
     blocks = ((k_ref, None), (kp_ref, ok_ref[0] > 0), (kn_ref, ok_ref[1] > 0))
     scores, m = [], None
     for block, (keys, ok) in enumerate(blocks):
@@ -51,7 +53,7 @@
         probs = raised.astype(jnp.bfloat16)
         rows = slice(start, start + CHUNK)
         if block == 0:
-            part = lax.dot_general(v_ref[rows], probs, DIMS_TN, preferred_element_type=jnp.float32)
+            part = lax.dot_general(own[rows], probs, DIMS_TN, preferred_element_type=jnp.float32)
             acc = part if acc is None else acc + part
         else:
             (pp_ref if block == 1 else pn_ref)[0, rows] = probs
@@ -59,26 +61,26 @@
     total_ref[0] = jnp.broadcast_to(total, total_ref.shape[1:])
 
 
-def score(ok, q, k, v, kp, kn):
-    rows, width = q.shape
+def score(ok, vq, k, kp, kn):
+    rows, width = k.shape
     heads = width // HDIM
-    tile = min(TILE, rows)
-    side = pl.BlockSpec((rows, HDIM), lambda h, i: (0, h))
-    probs = pl.BlockSpec((1, rows, tile), lambda h, i: (h, 0, i))
+    joint = (vq.shape[0], vq.shape[1] // 2, HDIM)
+    side = pl.BlockSpec((rows, HDIM), lambda h: (0, h))
+    probs = pl.BlockSpec((1, rows, rows), lambda h: (h, 0, 0))
     return pl.pallas_call(
         score_kernel,
-        grid=(heads, rows // tile),
+        grid=(heads,),
         in_specs=[
             pl.BlockSpec(memory_space=pltpu.SMEM),
-            pl.BlockSpec((tile, HDIM), lambda h, i: (i, h)),
-            side,
-            side,
+            pl.BlockSpec(joint, lambda h: (0, 1, h)),
+            side,
+            pl.BlockSpec(joint, lambda h: (0, 0, h)),
             side,
             side,
         ],
         out_specs=[
-            pl.BlockSpec((1, HDIM, tile), lambda h, i: (h, 0, i)),
-            pl.BlockSpec((1, 8, tile), lambda h, i: (h, 0, i)),
+            pl.BlockSpec((1, HDIM, rows), lambda h: (h, 0, 0)),
+            pl.BlockSpec((1, 8, rows), lambda h: (h, 0, 0)),
             probs,
             probs,
         ],
@@ -91,7 +93,7 @@
         compiler_params=pltpu.CompilerParams(vmem_limit_bytes=VMEM),
         cost_estimate=pl.CostEstimate(flops=rows * width, bytes_accessed=rows * width, transcendentals=0),
         name="score",
-    )(ok, q, k, v, kp, kn)
+    )(ok, vq, k, vq, kp, kn)
 
 
 def mix_kernel(pp_ref, pn_ref, vp_ref, vn_ref, acc_ref, total_ref, out_ref):
@@ -206,21 +208,23 @@
     )(mirror, k, wt)
 
 
-def split_kernel(mirror_ref, in_ref, out_ref):
-    groups, _, width = out_ref.shape
+def join_kernel(mirror_ref, v_ref, q_ref, out_ref):
+    groups, rows, width = out_ref.shape
+    tok = rows // 2
     for g in range(groups):
-        out_ref[g] = in_ref[:, columns(mirror_ref, g, width)]
-
-
-def split_heads(mirror, value):
-    tok, width = value.shape
-    return pl.pallas_call(
-        split_kernel,
-        in_specs=[pl.BlockSpec(memory_space=pltpu.SMEM), pl.BlockSpec(memory_space=pltpu.VMEM)],
-        out_shape=jax.ShapeDtypeStruct((8, tok, width // 8), value.dtype),
-        compiler_params=pltpu.CompilerParams(vmem_limit_bytes=VMEM),
-        name="split_heads",
-    )(mirror, value)
+        out_ref[g, :tok, :] = v_ref[:, columns(mirror_ref, g, width)]
+        out_ref[g, tok:, :] = q_ref[:, columns(mirror_ref, g, width)]
+
+
+def join_heads(mirror, v, q):
+    tok, width = v.shape
+    return pl.pallas_call(
+        join_kernel,
+        in_specs=[pl.BlockSpec(memory_space=pltpu.SMEM)] + [pl.BlockSpec(memory_space=pltpu.VMEM)] * 2,
+        out_shape=jax.ShapeDtypeStruct((8, 2 * tok, width // 8), v.dtype),
+        compiler_params=pltpu.CompilerParams(vmem_limit_bytes=VMEM),
+        name="join_heads",
+    )(mirror, v, q)
 
 
 def unpack_kernel(in_ref, k_ref, w_ref):
@@ -291,16 +295,16 @@
 
     kp, kn = to_block(k, 1), to_block(k, -1)
     values, k = lax.optimization_barrier((values, k))
-    v = to_heads(split_heads(mirror, values)).reshape(8 * tok, -1)
+    vq = to_heads(join_heads(mirror, values, queries))
     other = lax.ppermute(w_rows, "zh", [(0, 1), (1, 0)])
     pair = jnp.concatenate([jnp.where(first, w_rows, other), jnp.where(first, other, w_rows)])
     line = tighten(lax.all_gather(pair, "x"), cols)
-    kp, kn, v, line, queries = lax.optimization_barrier((kp, kn, v, line, queries))
-
+    kp, kn, vq, line = lax.optimization_barrier((kp, kn, vq, line))
+
+    v = vq[:, :tok].reshape(8 * tok, -1)
+    vp, vn = to_block(v, 1), to_block(v, -1)
     weight = lax.all_gather(line, ("y", "c")).reshape(8, 2, 8 * cols, depth)
-    vp, vn = to_block(v, 1), to_block(v, -1)
-    q = to_heads(split_heads(mirror, queries)).reshape(8 * tok, -1)
-    acc, total, pp, pn = score(ok, q, k, v, kp, kn)
+    acc, total, pp, pn = score(ok, vq, k, kp, kn)
     vp, vn, acc = lax.optimization_barrier((vp, vn, acc))
     ctx = mix(pp, pn, vp, vn, acc, total, tok)
     return project(mirror, weight, to_heads(ctx), cols).T

time: 155 us -> 165 us (1.065)
  the two profiles are of different devices: /device:TPU:6 before, /device:TPU:56 now
where the time goes in v8:
time: 165 us; the launch traced here: 164 us
  blocking collectives  78.1 us (47%)
  starting transfers between devices  24.7 us (15%)
  waiting for transfers between devices  22.6 us (14%)
  Pallas kernels  20.7 us (13%)
  between operations  13.5 us (8%)
  local copies, waits for them, and re-layouts  4.69 us (3%)
    all_to_all x2, blocking collectives, to_heads(): return lax.all_to_all(chunks, HEAD, split_axis=0, concat_axis=0)  64.3 us
    ppermute x1, waiting for transfers between devices, local(): other = lax.ppermute(w_rows, 'zh', [(0, 1), (1, 0)])  20.2 us
    all_gather x1, blocking collectives, local(): line = tighten(lax.all_gather(pair, 'x'), cols)  13.8 us
    ppermute x4, starting transfers between devices, to_block(): return lax.ppermute(value, AXES, pairs)  12.9 us
    pallas_call x1, Pallas kernels, score(): pl.pallas_call(score_kernel, grid=(heads,), in_specs=[pl.BlockSpec(memory...  11.1 us
    ppermute x1, starting transfers between devices, local(): other = lax.ppermute(w_rows, 'zh', [(0, 1), (1, 0)])  8.22 us
    pallas_call x1, Pallas kernels, project(): pl.pallas_call(functools.partial(project_kernel, cols), grid=(count // st...  4.96 us
    unnamed x8, local copies, waits for them, and re-layouts  3.84 us
  transfers between devices with their start and end apart: 7, of which 2 were waited for; matrix products, arithmetic and copies ran while one was open for 1% of the time, Pallas kernels for 9%

profile of v8, /device:TPU:56, one launch (start us, length us, event | category | flops | bytes accessed | tf_op | source)
XLA Modules:
  0.0 164.3 jit_solution(5845919279479274174)
XLA Ops:
  6.5 0.0 copy-start.2
  6.5 1.0 copy-done.2
  7.6 0.0 copy-start.3
  7.6 0.7 copy-done.3
  8.3 0.1 pack.1
  8.4 23.8 %all_to_all.15.in_ref = bf16[8,144,256]{2,1,0:T(8,128)(2,1)S(1)} all-to-all(bf16[8,144,256]{2,1,0:T(8,128)(2,1)S(1)} %pack.1), channel_id=1, replica_groups=mesh['x'=4,'zh'=2,'y'=8,'zl'=4,'c'=2] {'zl','c'}, dimensions={0} | all-to-all | bytes 1179648 | tf_op jit(solution)/shard_map/all_to_all | solution.py:273
  32.2 0.0 copy-start
  32.3 1.0 copy-done
  33.3 1.0 copy-done.1
  34.3 1.1 join_heads.1
  35.4 3.6 %all-to-all-start.1 = ((bf16[8,256,256]{2,1,0:T(8,128)(2,1)}), bf16[8,256,256]{2,1,0:T(8,128)(2,1)S(1)}, u32[]{:S(2)}, u32[]{:S(2)}) async-start(bf16[8,256,256]{2,1,0:T(8,128)(2,1)} %join_heads.1), calls=%async_computation.1 | async-start | bytes 2097152 | tf_op jit(solution)/shard_map/all_to_all | solution.py:273
  39.0 0.0 all-gather.4.cloned.1.call-start
  39.1 8.2 %collective-permute-start.2 = (bf16[32,1024]{1,0:T(8,128)(2,1)S(1)}, bf16[32,1024]{1,0:T(8,128)(2,1)S(1)}, u32[]{:S(2)}, u32[]{:S(2)}) collective-permute-start(bf16[32,1024]{1,0:T(8,128)(2,1)S(1)} %get-tuple-element.22), channel_id=1, source_target_pairs={{0,64},{64,0},{1,65},{65,1},{2,66},{66,2},{3,67},{67,3},{4,68},{68... | collective-permute-start | bytes 196616 | tf_op jit(solution)/shard_map/ppermute | solution.py:299
  47.3 1.9 %collective-permute-start = (bf16[1024,256]{1,0:T(8,128)(2,1)S(1)}, bf16[1024,256]{1,0:T(8,128)(2,1)S(1)}, u32[]{:S(2)}, u32[]{:S(2)}) collective-permute-start(bf16[1024,256]{1,0:T(8,128)(2,1)S(1)} %bitcast.10), channel_id=1, source_target_pairs={{0,8},{1,9},{2,10},{3,11},{4,12},{5,13},{6,14},{7,15},{8,16},{9,17... | collective-permute-start | bytes 1572872 | tf_op jit(solution)/shard_map/ppermute | solution.py:283
  49.2 3.9 %collective-permute-start.1 = (bf16[1024,256]{1,0:T(8,128)(2,1)S(1)}, bf16[1024,256]{1,0:T(8,128)(2,1)S(1)}, u32[]{:S(2)}, u32[]{:S(2)}) collective-permute-start(bf16[1024,256]{1,0:T(8,128)(2,1)S(1)} %bitcast.11), channel_id=1, source_target_pairs={{8,0},{9,1},{10,2},{11,3},{12,4},{13,5},{14,6},{15,7},{16,8},{17,9... | collective-permute-start | bytes 1572872 | tf_op jit(solution)/shard_map/ppermute | solution.py:283
  53.1 20.2 %collective-permute-done.2 = bf16[32,1024]{1,0:T(8,128)(2,1)S(1)} collective-permute-done((bf16[32,1024]{1,0:T(8,128)(2,1)S(1)}, bf16[32,1024]{1,0:T(8,128)(2,1)S(1)}, u32[]{:S(2)}, u32[]{:S(2)}) %collective-permute-start.2) | collective-permute-done | bytes 65568 | tf_op jit(solution)/shard_map/ppermute | solution.py:299
  73.3 13.8 %all-gather = bf16[256,1024]{1,0:T(8,128)(2,1)S(1)} all-gather(bf16[64,1024]{1,0:T(8,128)(2,1)S(1)} %pad_maximum_fusion), channel_id=2, replica_groups=mesh['x'=4,'zh'=2,'y'=8,'zl'=4,'c'=2] {'x'}, dimensions={0}, use_global_device_ids=true | all-gather | bytes 655360 | tf_op jit(solution)/shard_map/all_gather | solution.py:301
  87.1 0.9 tighten.1
  88.0 0.0 collective-permute-done.kp_ref
  88.0 0.0 collective-permute-done.1.kn_ref
  88.0 0.0 all-to-all-done.1.q_ref.v_ref
  88.0 0.0 all-gather.4.cloned.1.call-update
  88.0 0.9 slice.3
  88.8 5.1 %collective-permute-start.3 = (bf16[1024,256]{1,0:T(8,128)(2,1)}, bf16[1024,256]{1,0:T(8,128)(2,1)S(1)}, u32[]{:S(2)}, u32[]{:S(2)}) collective-permute-start(bf16[1024,256]{1,0:T(8,128)(2,1)} %bitcast.7), channel_id=1, source_target_pairs={{0,8},{1,9},{2,10},{3,11},{4,12},{5,13},{6,14},{7,15},{8,16},{9,17... | collective-permute-start | bytes 1572872 | tf_op jit(solution)/shard_map/ppermute | solution.py:283
  94.0 1.9 %collective-permute-start.4 = (bf16[1024,256]{1,0:T(8,128)(2,1)}, bf16[1024,256]{1,0:T(8,128)(2,1)}, u32[]{:S(2)}, u32[]{:S(2)}) collective-permute-start(bf16[1024,256]{1,0:T(8,128)(2,1)} %bitcast.7), channel_id=1, source_target_pairs={{8,0},{9,1},{10,2},{11,3},{12,4},{13,5},{14,6},{15,7},{16,8},{17,9... | collective-permute-start | bytes 1572872 | tf_op jit(solution)/shard_map/ppermute | solution.py:283
  95.9 0.1 add_convert_fusion.ok_ref
  96.0 11.1 %score.1 = (f32[2,128,1024]{2,1,0:T(8,128)S(1)}, f32[2,8,1024]{2,1,0:T(8,128)S(1)}, bf16[2,1024,1024]{2,1,0:T(8,128)(2,1)S(1)}, bf16[2,1024,1024]{2,1,0:T(8,128)(2,1)S(1)}) custom-call(s32[2]{0:T(128)S(1)} %add_convert_fusion.ok_ref, bf16[8,256,256]{2,1,0:T(8,128)(2,1)S(1)} %all-to-all-done.1.q_ref.v_ref, bf16[1024,256]{1,0:T(8,128)(2,1)S(1)} %bitcast.12, ...), custom_call_target="tpu_custom_call" | custom-call | flops 262144 | bytes 262144 | tf_op jit(solution)/shard_map/score/pallas_call | solution.py:70
  107.1 0.0 collective-permute-done.3.vp_ref
  107.1 2.4 %collective-permute-done.4.vn_ref = bf16[1024,256]{1,0:T(8,128)(2,1)} collective-permute-done((bf16[1024,256]{1,0:T(8,128)(2,1)}, bf16[1024,256]{1,0:T(8,128)(2,1)}, u32[]{:S(2)}, u32[]{:S(2)}) %collective-permute-start.4) | collective-permute-done | bytes 524320 | tf_op jit(solution)/shard_map/ppermute | solution.py:283
  109.5 2.6 %mix.1 = bf16[8,256,128]{2,1,0:T(8,128)(2,1)S(1)} custom-call(bf16[2,1024,1024]{2,1,0:T(8,128)(2,1)S(1)} %get-tuple-element.28.pp_ref, bf16[2,1024,1024]{2,1,0:T(8,128)(2,1)S(1)} %get-tuple-element.29.pn_ref, bf16[1024,256]{1,0:T(8,128)(2,1)S(1)} %collective-permute-done.3.vp_ref, bf16[1024,256]{1,0:T(8,128)(2,1)} %collective-permute-done.4.vn_ref, ...), custom_call_target="tpu_custom_call" | custom-call | flops 1073741824 | bytes 3670016 | tf_op jit(solution)/shard_map/mix/pallas_call | solution.py:115
  112.1 40.5 %all_to_all.16.ctx_ref = bf16[8,256,128]{2,1,0:T(8,128)(2,1)} all-to-all(bf16[8,256,128]{2,1,0:T(8,128)(2,1)S(1)} %mix.1), channel_id=1, replica_groups=mesh['x'=4,'zh'=2,'y'=8,'zl'=4,'c'=2] {'zl','c'}, dimensions={0} | all-to-all | bytes 1048576 | tf_op jit(solution)/shard_map/all_to_all | solution.py:273
  152.5 5.0 %project.1 = bf16[1600,128]{1,0:T(8,128)(2,1)} custom-call(s32[1]{0:T(128)} %bitcast.mirror_ref, bf16[8,2,200,1024]{3,2,1,0:T(8,128)(2,1)} %bitcast.14, bf16[8,256,128]{2,1,0:T(8,128)(2,1)} %all_to_all.16.ctx_ref), custom_call_target="tpu_custom_call" | custom-call | flops 838860800 | bytes 6553600 | tf_op jit(solution)/shard_map/project/pallas_call | solution.py:163
  (5 shorter events, 0.1 us)
Async XLA Ops:
  6.5 1.0 copy-start.2
  7.6 0.7 copy-start.3
  32.2 1.0 copy-start
  33.3 1.0 copy-start.1
  35.4 52.5 %all-to-all-start.1 = ((bf16[8,256,256]{2,1,0:T(8,128)(2,1)}), bf16[8,256,256]{2,1,0:T(8,128)(2,1)S(1)}, u32[]{:S(2)}, u32[]{:S(2)}) async-start(bf16[8,256,256]{2,1,0:T(8,128)(2,1)} %join_heads.1), calls=%async_computation.1 | async-start | bytes 2097152 | tf_op jit(solution)/shard_map/all_to_all | solution.py:273
  39.0 113.5 %all-gather.4.cloned.1.call-start = ((), (), s32[]{:S(2)}) async-start(), calls=%async_computation.3 | async-start | bytes 6963200 | tf_op jit(solution)/shard_map/all_gather | solution.py:306
  39.1 34.2 %collective-permute-start.2 = (bf16[32,1024]{1,0:T(8,128)(2,1)S(1)}, bf16[32,1024]{1,0:T(8,128)(2,1)S(1)}, u32[]{:S(2)}, u32[]{:S(2)}) collective-permute-start(bf16[32,1024]{1,0:T(8,128)(2,1)S(1)} %get-tuple-element.22), channel_id=1, source_target_pairs={{0,64},{64,0},{1,65},{65,1},{2,66},{66,2},{3,67},{67,3},{4,68},{68... | collective-permute-start | bytes 196616 | tf_op jit(solution)/shard_map/ppermute | solution.py:299
  47.3 40.7 %collective-permute-start = (bf16[1024,256]{1,0:T(8,128)(2,1)S(1)}, bf16[1024,256]{1,0:T(8,128)(2,1)S(1)}, u32[]{:S(2)}, u32[]{:S(2)}) collective-permute-start(bf16[1024,256]{1,0:T(8,128)(2,1)S(1)} %bitcast.10), channel_id=1, source_target_pairs={{0,8},{1,9},{2,10},{3,11},{4,12},{5,13},{6,14},{7,15},{8,16},{9,17... | collective-permute-start | bytes 1572872 | tf_op jit(solution)/shard_map/ppermute | solution.py:283
  49.2 38.7 %collective-permute-start.1 = (bf16[1024,256]{1,0:T(8,128)(2,1)S(1)}, bf16[1024,256]{1,0:T(8,128)(2,1)S(1)}, u32[]{:S(2)}, u32[]{:S(2)}) collective-permute-start(bf16[1024,256]{1,0:T(8,128)(2,1)S(1)} %bitcast.11), channel_id=1, source_target_pairs={{8,0},{9,1},{10,2},{11,3},{12,4},{13,5},{14,6},{15,7},{16,8},{17,9... | collective-permute-start | bytes 1572872 | tf_op jit(solution)/shard_map/ppermute | solution.py:283
  88.8 18.2 %collective-permute-start.3 = (bf16[1024,256]{1,0:T(8,128)(2,1)}, bf16[1024,256]{1,0:T(8,128)(2,1)S(1)}, u32[]{:S(2)}, u32[]{:S(2)}) collective-permute-start(bf16[1024,256]{1,0:T(8,128)(2,1)} %bitcast.7), channel_id=1, source_target_pairs={{0,8},{1,9},{2,10},{3,11},{4,12},{5,13},{6,14},{7,15},{8,16},{9,17... | collective-permute-start | bytes 1572872 | tf_op jit(solution)/shard_map/ppermute | solution.py:283
  94.0 15.5 %collective-permute-start.4 = (bf16[1024,256]{1,0:T(8,128)(2,1)}, bf16[1024,256]{1,0:T(8,128)(2,1)}, u32[]{:S(2)}, u32[]{:S(2)}) collective-permute-start(bf16[1024,256]{1,0:T(8,128)(2,1)} %bitcast.7), channel_id=1, source_target_pairs={{8,0},{9,1},{10,2},{11,3},{12,4},{13,5},{14,6},{15,7},{16,8},{17,9... | collective-permute-start | bytes 1572872 | tf_op jit(solution)/shard_map/ppermute | solution.py:283
Sparse Core Ops, SparseCore 0:
  88.1 53.1 all-gather.3

commit v9 on v8

--- a/solution.py
+++ b/solution.py
@@ -294,9 +294,9 @@
     k = k.reshape(8 * tok, -1)
 
     kp, kn = to_block(k, 1), to_block(k, -1)
-    values, k = lax.optimization_barrier((values, k))
+    other = lax.ppermute(w_rows, "zh", [(0, 1), (1, 0)])
+    values, other = lax.optimization_barrier((values, other))
     vq = to_heads(join_heads(mirror, values, queries))
-    other = lax.ppermute(w_rows, "zh", [(0, 1), (1, 0)])
     pair = jnp.concatenate([jnp.where(first, w_rows, other), jnp.where(first, other, w_rows)])
     line = tighten(lax.all_gather(pair, "x"), cols)
     kp, kn, vq, line = lax.optimization_barrier((kp, kn, vq, line))

time: 165 us -> 154 us (0.933)
  the two profiles are of different devices: /device:TPU:56 before, /device:TPU:6 now
where the time goes in v9:
time: 154 us; the launch traced here: 153 us
  blocking collectives  60.7 us (39%)
  starting transfers between devices  35.9 us (23%)
  Pallas kernels  20.7 us (13%)
  waiting for transfers between devices  17.6 us (11%)
  between operations  13.5 us (9%)
  local copies, waits for them, and re-layouts  4.7 us (3%)
    all_to_all x2, blocking collectives, to_heads(): return lax.all_to_all(chunks, HEAD, split_axis=0, concat_axis=0)  46.8 us
    ppermute x4, starting transfers between devices, to_block(): return lax.ppermute(value, AXES, pairs)  24.1 us
    ppermute x4, waiting for transfers between devices, to_block(): return lax.ppermute(value, AXES, pairs)  15.3 us
    all_gather x1, blocking collectives, local(): line = tighten(lax.all_gather(pair, 'x'), cols)  13.9 us
    pallas_call x1, Pallas kernels, score(): pl.pallas_call(score_kernel, grid=(heads,), in_specs=[pl.BlockSpec(memory...  11.1 us
    ppermute x1, starting transfers between devices, local(): other = lax.ppermute(w_rows, 'zh', [(0, 1), (1, 0)])  8.22 us
    pallas_call x1, Pallas kernels, project(): pl.pallas_call(functools.partial(project_kernel, cols), grid=(count // st...  4.96 us
    unnamed x8, local copies, waits for them, and re-layouts  3.84 us
  transfers between devices with their start and end apart: 7, of which 4 were waited for; matrix products, arithmetic and copies ran while one was open for 1% of the time, Pallas kernels for 9%

profile of v9, /device:TPU:6, one launch (start us, length us, event | category | flops | bytes accessed | tf_op | source)
XLA Modules:
  0.0 153.2 jit_solution(15701825482059111871)
XLA Ops:
  6.5 0.0 copy-start.2
  6.5 1.0 copy-done.2
  7.6 0.0 copy-start.3
  7.6 0.7 copy-done.3
  8.3 0.1 pack.1
  8.4 23.8 %all_to_all.15.in_ref = bf16[8,144,256]{2,1,0:T(8,128)(2,1)S(1)} all-to-all(bf16[8,144,256]{2,1,0:T(8,128)(2,1)S(1)} %pack.1), channel_id=1, replica_groups=mesh['x'=4,'zh'=2,'y'=8,'zl'=4,'c'=2] {'zl','c'}, dimensions={0} | all-to-all | bytes 1179648 | tf_op jit(solution)/shard_map/all_to_all | solution.py:273
  32.2 8.2 %collective-permute-start.2 = (bf16[32,1024]{1,0:T(8,128)(2,1)S(1)}, bf16[32,1024]{1,0:T(8,128)(2,1)S(1)}, u32[]{:S(2)}, u32[]{:S(2)}) collective-permute-start(bf16[32,1024]{1,0:T(8,128)(2,1)S(1)} %get-tuple-element.21), channel_id=1, source_target_pairs={{0,64},{64,0},{1,65},{65,1},{2,66},{66,2},{3,67},{67,3},{4,68},{68... | collective-permute-start | bytes 196616 | tf_op jit(solution)/shard_map/ppermute | solution.py:297
  40.5 2.2 %collective-permute-done.2 = bf16[32,1024]{1,0:T(8,128)(2,1)S(1)} collective-permute-done((bf16[32,1024]{1,0:T(8,128)(2,1)S(1)}, bf16[32,1024]{1,0:T(8,128)(2,1)S(1)}, u32[]{:S(2)}, u32[]{:S(2)}) %collective-permute-start.2) | collective-permute-done | bytes 65568 | tf_op jit(solution)/shard_map/ppermute | solution.py:297
  42.7 0.0 copy-start
  42.7 1.0 copy-done
  43.7 1.0 copy-done.1
  44.8 1.1 join_heads.1
  45.9 3.6 %all-to-all-start.1 = ((bf16[8,256,256]{2,1,0:T(8,128)(2,1)}), bf16[8,256,256]{2,1,0:T(8,128)(2,1)S(1)}, u32[]{:S(2)}, u32[]{:S(2)}) async-start(bf16[8,256,256]{2,1,0:T(8,128)(2,1)} %join_heads.1), calls=%async_computation.1 | async-start | bytes 2097152 | tf_op jit(solution)/shard_map/all_to_all | solution.py:273
  49.5 0.0 all-gather.4.cloned.1.call-start
  49.5 3.5 %collective-permute-start = (bf16[1024,256]{1,0:T(8,128)(2,1)S(1)}, bf16[1024,256]{1,0:T(8,128)(2,1)S(1)}, u32[]{:S(2)}, u32[]{:S(2)}) collective-permute-start(bf16[1024,256]{1,0:T(8,128)(2,1)S(1)} %bitcast.10), channel_id=1, source_target_pairs={{0,8},{1,9},{2,10},{3,11},{4,12},{5,13},{6,14},{7,15},{8,16},{9,17... | collective-permute-start | bytes 1572872 | tf_op jit(solution)/shard_map/ppermute | solution.py:283
  53.0 9.9 %collective-permute-start.1 = (bf16[1024,256]{1,0:T(8,128)(2,1)S(1)}, bf16[1024,256]{1,0:T(8,128)(2,1)S(1)}, u32[]{:S(2)}, u32[]{:S(2)}) collective-permute-start(bf16[1024,256]{1,0:T(8,128)(2,1)S(1)} %bitcast.11), channel_id=1, source_target_pairs={{8,0},{9,1},{10,2},{11,3},{12,4},{13,5},{14,6},{15,7},{16,8},{17,9... | collective-permute-start | bytes 1572872 | tf_op jit(solution)/shard_map/ppermute | solution.py:283
  62.9 13.9 %all-gather = bf16[256,1024]{1,0:T(8,128)(2,1)S(1)} all-gather(bf16[64,1024]{1,0:T(8,128)(2,1)S(1)} %pad_maximum_fusion), channel_id=2, replica_groups=mesh['x'=4,'zh'=2,'y'=8,'zl'=4,'c'=2] {'x'}, dimensions={0}, use_global_device_ids=true | all-gather | bytes 655360 | tf_op jit(solution)/shard_map/all_gather | solution.py:301
  76.8 0.9 tighten.1
  77.7 6.0 %collective-permute-done.kp_ref = bf16[1024,256]{1,0:T(8,128)(2,1)S(1)} collective-permute-done((bf16[1024,256]{1,0:T(8,128)(2,1)S(1)}, bf16[1024,256]{1,0:T(8,128)(2,1)S(1)}, u32[]{:S(2)}, u32[]{:S(2)}) %collective-permute-start) | collective-permute-done | bytes 524320 | tf_op jit(solution)/shard_map/ppermute | solution.py:283
  83.7 0.0 collective-permute-done.1.kn_ref
  83.7 0.0 all-to-all-done.1.q_ref.v_ref
  83.7 0.0 all-gather.4.cloned.1.call-update
  83.7 0.9 slice.3
  84.6 1.9 %collective-permute-start.3 = (bf16[1024,256]{1,0:T(8,128)(2,1)}, bf16[1024,256]{1,0:T(8,128)(2,1)S(1)}, u32[]{:S(2)}, u32[]{:S(2)}) collective-permute-start(bf16[1024,256]{1,0:T(8,128)(2,1)} %bitcast.7), channel_id=1, source_target_pairs={{0,8},{1,9},{2,10},{3,11},{4,12},{5,13},{6,14},{7,15},{8,16},{9,17... | collective-permute-start | bytes 1572872 | tf_op jit(solution)/shard_map/ppermute | solution.py:283
  86.5 8.8 %collective-permute-start.4 = (bf16[1024,256]{1,0:T(8,128)(2,1)}, bf16[1024,256]{1,0:T(8,128)(2,1)}, u32[]{:S(2)}, u32[]{:S(2)}) collective-permute-start(bf16[1024,256]{1,0:T(8,128)(2,1)} %bitcast.7), channel_id=1, source_target_pairs={{8,0},{9,1},{10,2},{11,3},{12,4},{13,5},{14,6},{15,7},{16,8},{17,9... | collective-permute-start | bytes 1572872 | tf_op jit(solution)/shard_map/ppermute | solution.py:283
  95.4 0.1 add_convert_fusion.ok_ref
  95.5 11.1 %score.1 = (f32[2,128,1024]{2,1,0:T(8,128)S(1)}, f32[2,8,1024]{2,1,0:T(8,128)S(1)}, bf16[2,1024,1024]{2,1,0:T(8,128)(2,1)S(1)}, bf16[2,1024,1024]{2,1,0:T(8,128)(2,1)S(1)}) custom-call(s32[2]{0:T(128)S(1)} %add_convert_fusion.ok_ref, bf16[8,256,256]{2,1,0:T(8,128)(2,1)S(1)} %all-to-all-done.1.q_ref.v_ref, bf16[1024,256]{1,0:T(8,128)(2,1)S(1)} %bitcast.12, ...), custom_call_target="tpu_custom_call" | custom-call | flops 262144 | bytes 262144 | tf_op jit(solution)/shard_map/score/pallas_call | solution.py:70
  106.5 6.5 %collective-permute-done.3.vp_ref = bf16[1024,256]{1,0:T(8,128)(2,1)S(1)} collective-permute-done((bf16[1024,256]{1,0:T(8,128)(2,1)}, bf16[1024,256]{1,0:T(8,128)(2,1)S(1)}, u32[]{:S(2)}, u32[]{:S(2)}) %collective-permute-start.3) | collective-permute-done | bytes 524320 | tf_op jit(solution)/shard_map/ppermute | solution.py:283
  113.0 2.8 %collective-permute-done.4.vn_ref = bf16[1024,256]{1,0:T(8,128)(2,1)} collective-permute-done((bf16[1024,256]{1,0:T(8,128)(2,1)}, bf16[1024,256]{1,0:T(8,128)(2,1)}, u32[]{:S(2)}, u32[]{:S(2)}) %collective-permute-start.4) | collective-permute-done | bytes 524320 | tf_op jit(solution)/shard_map/ppermute | solution.py:283
  115.9 2.6 %mix.1 = bf16[8,256,128]{2,1,0:T(8,128)(2,1)S(1)} custom-call(bf16[2,1024,1024]{2,1,0:T(8,128)(2,1)S(1)} %get-tuple-element.28.pp_ref, bf16[2,1024,1024]{2,1,0:T(8,128)(2,1)S(1)} %get-tuple-element.29.pn_ref, bf16[1024,256]{1,0:T(8,128)(2,1)S(1)} %collective-permute-done.3.vp_ref, bf16[1024,256]{1,0:T(8,128)(2,1)} %collective-permute-done.4.vn_ref, ...), custom_call_target="tpu_custom_call" | custom-call | flops 1073741824 | bytes 3670016 | tf_op jit(solution)/shard_map/mix/pallas_call | solution.py:115
  118.5 23.0 %all_to_all.16.ctx_ref = bf16[8,256,128]{2,1,0:T(8,128)(2,1)} all-to-all(bf16[8,256,128]{2,1,0:T(8,128)(2,1)S(1)} %mix.1), channel_id=1, replica_groups=mesh['x'=4,'zh'=2,'y'=8,'zl'=4,'c'=2] {'zl','c'}, dimensions={0} | all-to-all | bytes 1048576 | tf_op jit(solution)/shard_map/all_to_all | solution.py:273
  141.4 5.0 %project.1 = bf16[1600,128]{1,0:T(8,128)(2,1)} custom-call(s32[1]{0:T(128)} %bitcast.mirror_ref, bf16[8,2,200,1024]{3,2,1,0:T(8,128)(2,1)} %bitcast.14, bf16[8,256,128]{2,1,0:T(8,128)(2,1)} %all_to_all.16.ctx_ref), custom_call_target="tpu_custom_call" | custom-call | flops 838860800 | bytes 6553600 | tf_op jit(solution)/shard_map/project/pallas_call | solution.py:163
  (5 shorter events, 0.1 us)
Async XLA Ops:
  6.5 1.0 copy-start.2
  7.6 0.7 copy-start.3
  32.2 10.5 %collective-permute-start.2 = (bf16[32,1024]{1,0:T(8,128)(2,1)S(1)}, bf16[32,1024]{1,0:T(8,128)(2,1)S(1)}, u32[]{:S(2)}, u32[]{:S(2)}) collective-permute-start(bf16[32,1024]{1,0:T(8,128)(2,1)S(1)} %get-tuple-element.21), channel_id=1, source_target_pairs={{0,64},{64,0},{1,65},{65,1},{2,66},{66,2},{3,67},{67,3},{4,68},{68... | collective-permute-start | bytes 196616 | tf_op jit(solution)/shard_map/ppermute | solution.py:297
  42.7 1.0 copy-start
  43.7 1.0 copy-start.1
  45.9 37.8 %all-to-all-start.1 = ((bf16[8,256,256]{2,1,0:T(8,128)(2,1)}), bf16[8,256,256]{2,1,0:T(8,128)(2,1)S(1)}, u32[]{:S(2)}, u32[]{:S(2)}) async-start(bf16[8,256,256]{2,1,0:T(8,128)(2,1)} %join_heads.1), calls=%async_computation.1 | async-start | bytes 2097152 | tf_op jit(solution)/shard_map/all_to_all | solution.py:273
  49.5 92.0 %all-gather.4.cloned.1.call-start = ((), (), s32[]{:S(2)}) async-start(), calls=%async_computation.3 | async-start | bytes 6963200 | tf_op jit(solution)/shard_map/all_gather | solution.py:306
  49.5 34.2 %collective-permute-start = (bf16[1024,256]{1,0:T(8,128)(2,1)S(1)}, bf16[1024,256]{1,0:T(8,128)(2,1)S(1)}, u32[]{:S(2)}, u32[]{:S(2)}) collective-permute-start(bf16[1024,256]{1,0:T(8,128)(2,1)S(1)} %bitcast.10), channel_id=1, source_target_pairs={{0,8},{1,9},{2,10},{3,11},{4,12},{5,13},{6,14},{7,15},{8,16},{9,17... | collective-permute-start | bytes 1572872 | tf_op jit(solution)/shard_map/ppermute | solution.py:283
  53.0 30.7 %collective-permute-start.1 = (bf16[1024,256]{1,0:T(8,128)(2,1)S(1)}, bf16[1024,256]{1,0:T(8,128)(2,1)S(1)}, u32[]{:S(2)}, u32[]{:S(2)}) collective-permute-start(bf16[1024,256]{1,0:T(8,128)(2,1)S(1)} %bitcast.11), channel_id=1, source_target_pairs={{8,0},{9,1},{10,2},{11,3},{12,4},{13,5},{14,6},{15,7},{16,8},{17,9... | collective-permute-start | bytes 1572872 | tf_op jit(solution)/shard_map/ppermute | solution.py:283
  84.6 28.4 %collective-permute-start.3 = (bf16[1024,256]{1,0:T(8,128)(2,1)}, bf16[1024,256]{1,0:T(8,128)(2,1)S(1)}, u32[]{:S(2)}, u32[]{:S(2)}) collective-permute-start(bf16[1024,256]{1,0:T(8,128)(2,1)} %bitcast.7), channel_id=1, source_target_pairs={{0,8},{1,9},{2,10},{3,11},{4,12},{5,13},{6,14},{7,15},{8,16},{9,17... | collective-permute-start | bytes 1572872 | tf_op jit(solution)/shard_map/ppermute | solution.py:283
  86.5 29.3 %collective-permute-start.4 = (bf16[1024,256]{1,0:T(8,128)(2,1)}, bf16[1024,256]{1,0:T(8,128)(2,1)}, u32[]{:S(2)}, u32[]{:S(2)}) collective-permute-start(bf16[1024,256]{1,0:T(8,128)(2,1)} %bitcast.7), channel_id=1, source_target_pairs={{8,0},{9,1},{10,2},{11,3},{12,4},{13,5},{14,6},{15,7},{16,8},{17,9... | collective-permute-start | bytes 1572872 | tf_op jit(solution)/shard_map/ppermute | solution.py:283
Sparse Core Ops, SparseCore 0:
  83.9 54.2 all-gather.3

commit v10 on v8

--- a/solution.py
+++ b/solution.py
@@ -19,6 +19,7 @@
 MIX_TILE = 1024
 CHUNK = 256
 PROJECT_STEP = 4
+HINT = 28_750_000_000
 PROJECT_VMEM = 56 * 1024 * 1024
 DIMS_NT = (((1,), (1,)), ((), ()))
 DIMS_TN = (((0,), (0,)), ((), ()))
@@ -273,6 +274,22 @@
     return lax.all_to_all(chunks, HEAD, split_axis=0, concat_axis=0)
 
 
+def behind_kernel(ok_ref, kp_ref, kn_ref, out_ref):
+    for side in range(2):
+        out_ref[side] = ok_ref[side]
+
+
+def behind(ok, kp, kn):
+    return pl.pallas_call(
+        behind_kernel,
+        in_specs=[pl.BlockSpec(memory_space=pltpu.SMEM)] + [pl.BlockSpec(memory_space=pl.ANY)] * 2,
+        out_specs=pl.BlockSpec(memory_space=pltpu.SMEM),
+        out_shape=jax.ShapeDtypeStruct(ok.shape, ok.dtype),
+        cost_estimate=pl.CostEstimate(flops=HINT, bytes_accessed=0, transcendentals=0),
+        name="behind",
+    )(ok, kp, kn)
+
+
 def to_block(value, step):
     pairs = []
     for b in range(N_BLK):
@@ -299,7 +316,8 @@
     other = lax.ppermute(w_rows, "zh", [(0, 1), (1, 0)])
     pair = jnp.concatenate([jnp.where(first, w_rows, other), jnp.where(first, other, w_rows)])
     line = tighten(lax.all_gather(pair, "x"), cols)
-    kp, kn, vq, line = lax.optimization_barrier((kp, kn, vq, line))
+    ok = behind(ok, kp, kn)
+    ok, vq, line = lax.optimization_barrier((ok, vq, line))
 
     v = vq[:, :tok].reshape(8 * tok, -1)
     vp, vn = to_block(v, 1), to_block(v, -1)

time: 165 us -> 152 us (0.921)
  the two profiles are of different devices: /device:TPU:56 before, /device:TPU:6 now
where the time goes in v10:
time: 152 us; the launch traced here: 151 us
  starting transfers between devices  39.2 us (26%)
  waiting for transfers between devices  34.7 us (23%)
  blocking collectives  32.3 us (21%)
  Pallas kernels  21.9 us (14%)
  between operations  13.5 us (9%)
  local copies, waits for them, and re-layouts  8.2 us (5%)
    all_to_all x2, waiting for transfers between devices, to_heads(): return lax.all_to_all(chunks, HEAD, split_axis=0, concat_axis=0)  25.7 us
    ppermute x4, starting transfers between devices, to_block(): return lax.ppermute(value, AXES, pairs)  20.1 us
    all_to_all x1, blocking collectives, to_heads(): return lax.all_to_all(chunks, HEAD, split_axis=0, concat_axis=0)  18.4 us
    all_gather x1, blocking collectives, local(): line = tighten(lax.all_gather(pair, 'x'), cols)  13.9 us
    pallas_call x1, Pallas kernels, score(): pl.pallas_call(score_kernel, grid=(heads,), in_specs=[pl.BlockSpec(memory...  11.1 us
    all_to_all x2, starting transfers between devices, to_heads(): return lax.all_to_all(chunks, HEAD, split_axis=0, concat_axis=0)  10.8 us
    ppermute x4, waiting for transfers between devices, to_block(): return lax.ppermute(value, AXES, pairs)  9.01 us
    ppermute x1, starting transfers between devices, local(): other = lax.ppermute(w_rows, 'zh', [(0, 1), (1, 0)])  8.22 us
  transfers between devices with their start and end apart: 8, of which 4 were waited for; matrix products, arithmetic and copies ran while one was open for 0% of the time, Pallas kernels for 11%

profile of v10, /device:TPU:6, one launch (start us, length us, event | category | flops | bytes accessed | tf_op | source)
XLA Modules:
  0.0 150.5 jit_solution(2163467424212573289)
XLA Ops:
  6.5 1.0 copy-done.2
  7.6 0.7 copy-done.7
  8.3 0.9 pack.1
  9.2 7.3 %all-to-all-start = ((bf16[8,144,256]{2,1,0:T(8,128)(2,1)}), bf16[8,144,256]{2,1,0:T(8,128)(2,1)S(1)}, u32[]{:S(2)}, u32[]{:S(2)}) async-start(bf16[8,144,256]{2,1,0:T(8,128)(2,1)} %pack.1), calls=%async_computation | async-start | bytes 1179648 | tf_op jit(solution)/shard_map/all_to_all | solution.py:274
  16.5 16.8 %all-to-all-done.in_ref = bf16[8,144,256]{2,1,0:T(8,128)(2,1)S(1)} async-done(((bf16[8,144,256]{2,1,0:T(8,128)(2,1)}), bf16[8,144,256]{2,1,0:T(8,128)(2,1)S(1)}, u32[]{:S(2)}, u32[]{:S(2)}) %all-to-all-start) | async-done | bytes 589856 | tf_op jit(solution)/shard_map/all_to_all | solution.py:274
  33.3 8.2 %collective-permute-start.2 = (bf16[32,1024]{1,0:T(8,128)(2,1)S(1)}, bf16[32,1024]{1,0:T(8,128)(2,1)S(1)}, u32[]{:S(2)}, u32[]{:S(2)}) collective-permute-start(bf16[32,1024]{1,0:T(8,128)(2,1)S(1)} %get-tuple-element.21), channel_id=1, source_target_pairs={{0,64},{64,0},{1,65},{65,1},{2,66},{66,2},{3,67},{67,3},{4,68},{68... | collective-permute-start | bytes 196616 | tf_op jit(solution)/shard_map/ppermute | solution.py:316
  41.5 0.6 add_convert_fusion.ok_ref
  42.1 3.5 %collective-permute-start = (bf16[1024,256]{1,0:T(8,128)(2,1)S(1)}, bf16[1024,256]{1,0:T(8,128)(2,1)S(1)}, u32[]{:S(2)}, u32[]{:S(2)}) collective-permute-start(bf16[1024,256]{1,0:T(8,128)(2,1)S(1)} %bitcast.10), channel_id=1, source_target_pairs={{0,8},{1,9},{2,10},{3,11},{4,12},{5,13},{6,14},{7,15},{8,16},{9,17... | collective-permute-start | bytes 1572872 | tf_op jit(solution)/shard_map/ppermute | solution.py:300
  45.6 6.6 %collective-permute-start.1 = (bf16[1024,256]{1,0:T(8,128)(2,1)S(1)}, bf16[1024,256]{1,0:T(8,128)(2,1)S(1)}, u32[]{:S(2)}, u32[]{:S(2)}) collective-permute-start(bf16[1024,256]{1,0:T(8,128)(2,1)S(1)} %bitcast.11), channel_id=1, source_target_pairs={{8,0},{9,1},{10,2},{11,3},{12,4},{13,5},{14,6},{15,7},{16,8},{17,9... | collective-permute-start | bytes 1572872 | tf_op jit(solution)/shard_map/ppermute | solution.py:300
  52.2 1.0 copy-done
  53.2 1.0 copy-done.1
  54.3 1.1 join_heads.1
  55.4 3.6 %all-to-all-start.1 = ((bf16[8,256,256]{2,1,0:T(8,128)(2,1)}), bf16[8,256,256]{2,1,0:T(8,128)(2,1)S(1)}, u32[]{:S(2)}, u32[]{:S(2)}) async-start(bf16[8,256,256]{2,1,0:T(8,128)(2,1)} %join_heads.1), calls=%async_computation.1 | async-start | bytes 2097152 | tf_op jit(solution)/shard_map/all_to_all | solution.py:274
  59.0 0.0 all-gather.4.cloned.1.call-start
  59.1 13.9 %all-gather = bf16[256,1024]{1,0:T(8,128)(2,1)S(1)} all-gather(bf16[64,1024]{1,0:T(8,128)(2,1)S(1)} %pad_maximum_fusion), channel_id=2, replica_groups=mesh['x'=4,'zh'=2,'y'=8,'zl'=4,'c'=2] {'x'}, dimensions={0}, use_global_device_ids=true | all-gather | bytes 655360 | tf_op jit(solution)/shard_map/all_gather | solution.py:318
  72.9 0.9 tighten.1
  73.8 0.8 copy-done.3
  74.6 0.8 copy-done.5
  75.4 1.2 behind.1.ok_ref
  76.6 8.9 %all-to-all-done.1.q_ref.v_ref = bf16[8,256,256]{2,1,0:T(8,128)(2,1)S(1)} async-done(((bf16[8,256,256]{2,1,0:T(8,128)(2,1)}), bf16[8,256,256]{2,1,0:T(8,128)(2,1)S(1)}, u32[]{:S(2)}, u32[]{:S(2)}) %all-to-all-start.1) | async-done | bytes 1048608 | tf_op jit(solution)/shard_map/all_to_all | solution.py:274
  85.5 0.0 all-gather.4.cloned.1.call-update
  85.5 1.9 %collective-permute-start.3 = (bf16[1024,256]{1,0:T(8,128)(2,1)S(1)}, bf16[1024,256]{1,0:T(8,128)(2,1)S(1)}, u32[]{:S(2)}, u32[]{:S(2)}) collective-permute-start(bf16[1024,256]{1,0:T(8,128)(2,1)S(1)} %bitcast.15), channel_id=1, source_target_pairs={{0,8},{1,9},{2,10},{3,11},{4,12},{5,13},{6,14},{7,15},{8,16},{9,17... | collective-permute-start | bytes 1572872 | tf_op jit(solution)/shard_map/ppermute | solution.py:300
  87.5 8.1 %collective-permute-start.4 = (bf16[1024,256]{1,0:T(8,128)(2,1)S(1)}, bf16[1024,256]{1,0:T(8,128)(2,1)S(1)}, u32[]{:S(2)}, u32[]{:S(2)}) collective-permute-start(bf16[1024,256]{1,0:T(8,128)(2,1)S(1)} %bitcast.16), channel_id=1, source_target_pairs={{8,0},{9,1},{10,2},{11,3},{12,4},{13,5},{14,6},{15,7},{16,8},{17,9... | collective-permute-start | bytes 1572872 | tf_op jit(solution)/shard_map/ppermute | solution.py:300
  95.6 1.0 copy-done.4
  96.7 1.0 copy-done.6
  97.7 0.7 copy-done.8
  98.4 11.1 %score.1 = (f32[2,128,1024]{2,1,0:T(8,128)S(1)}, f32[2,8,1024]{2,1,0:T(8,128)S(1)}, bf16[2,1024,1024]{2,1,0:T(8,128)(2,1)S(1)}, bf16[2,1024,1024]{2,1,0:T(8,128)(2,1)S(1)}) custom-call(s32[2]{0:T(128)S(1)} %copy-done.8, bf16[8,256,256]{2,1,0:T(8,128)(2,1)S(1)} %all-to-all-done.1.q_ref.v_ref, bf16[1024,256]{1,0:T(8,128)(2,1)S(1)} %bitcast.12, ...), custom_call_target="tpu_custom_call" | custom-call | flops 262144 | bytes 262144 | tf_op jit(solution)/shard_map/score/pallas_call | solution.py:71
  109.5 6.9 %collective-permute-done.3.vp_ref = bf16[1024,256]{1,0:T(8,128)(2,1)S(1)} collective-permute-done((bf16[1024,256]{1,0:T(8,128)(2,1)S(1)}, bf16[1024,256]{1,0:T(8,128)(2,1)S(1)}, u32[]{:S(2)}, u32[]{:S(2)}) %collective-permute-start.3) | collective-permute-done | bytes 524320 | tf_op jit(solution)/shard_map/ppermute | solution.py:300
  116.4 2.1 %collective-permute-done.4.vn_ref = bf16[1024,256]{1,0:T(8,128)(2,1)S(1)} collective-permute-done((bf16[1024,256]{1,0:T(8,128)(2,1)S(1)}, bf16[1024,256]{1,0:T(8,128)(2,1)S(1)}, u32[]{:S(2)}, u32[]{:S(2)}) %collective-permute-start.4) | collective-permute-done | bytes 524320 | tf_op jit(solution)/shard_map/ppermute | solution.py:300
  118.5 1.8 %mix.1 = bf16[8,256,128]{2,1,0:T(8,128)(2,1)S(1)} custom-call(bf16[2,1024,1024]{2,1,0:T(8,128)(2,1)S(1)} %get-tuple-element.26.pp_ref, bf16[2,1024,1024]{2,1,0:T(8,128)(2,1)S(1)} %get-tuple-element.27.pn_ref, bf16[1024,256]{1,0:T(8,128)(2,1)S(1)} %collective-permute-done.3.vp_ref, bf16[1024,256]{1,0:T(8,128)(2,1)S(1)} %collective-permute-done.4.vn_ref, ...), custom_call_target="tpu_custom_call" | custom-call | flops 1073741824 | bytes 3670016 | tf_op jit(solution)/shard_map/mix/pallas_call | solution.py:116
  120.3 18.4 %all_to_all.15.ctx_ref = bf16[8,256,128]{2,1,0:T(8,128)(2,1)} all-to-all(bf16[8,256,128]{2,1,0:T(8,128)(2,1)S(1)} %mix.1), channel_id=1, replica_groups=mesh['x'=4,'zh'=2,'y'=8,'zl'=4,'c'=2] {'zl','c'}, dimensions={0} | all-to-all | bytes 1048576 | tf_op jit(solution)/shard_map/all_to_all | solution.py:274
  138.7 5.0 %project.1 = bf16[1600,128]{1,0:T(8,128)(2,1)} custom-call(s32[1]{0:T(128)} %bitcast.mirror_ref, bf16[8,2,200,1024]{3,2,1,0:T(8,128)(2,1)} %bitcast.14, bf16[8,256,128]{2,1,0:T(8,128)(2,1)} %all_to_all.15.ctx_ref), custom_call_target="tpu_custom_call" | custom-call | flops 838860800 | bytes 6553600 | tf_op jit(solution)/shard_map/project/pallas_call | solution.py:164
  (17 shorter events, 0.1 us)
Async XLA Ops:
  6.5 1.0 copy-start.2
  7.6 0.7 copy-start.7
  9.2 24.0 %all-to-all-start = ((bf16[8,144,256]{2,1,0:T(8,128)(2,1)}), bf16[8,144,256]{2,1,0:T(8,128)(2,1)S(1)}, u32[]{:S(2)}, u32[]{:S(2)}) async-start(bf16[8,144,256]{2,1,0:T(8,128)(2,1)} %pack.1), calls=%async_computation | async-start | bytes 1179648 | tf_op jit(solution)/shard_map/all_to_all | solution.py:274
  33.3 25.7 %collective-permute-start.2 = (bf16[32,1024]{1,0:T(8,128)(2,1)S(1)}, bf16[32,1024]{1,0:T(8,128)(2,1)S(1)}, u32[]{:S(2)}, u32[]{:S(2)}) collective-permute-start(bf16[32,1024]{1,0:T(8,128)(2,1)S(1)} %get-tuple-element.21), channel_id=1, source_target_pairs={{0,64},{64,0},{1,65},{65,1},{2,66},{66,2},{3,67},{67,3},{4,68},{68... | collective-permute-start | bytes 196616 | tf_op jit(solution)/shard_map/ppermute | solution.py:316
  42.1 31.7 %collective-permute-start = (bf16[1024,256]{1,0:T(8,128)(2,1)S(1)}, bf16[1024,256]{1,0:T(8,128)(2,1)S(1)}, u32[]{:S(2)}, u32[]{:S(2)}) collective-permute-start(bf16[1024,256]{1,0:T(8,128)(2,1)S(1)} %bitcast.10), channel_id=1, source_target_pairs={{0,8},{1,9},{2,10},{3,11},{4,12},{5,13},{6,14},{7,15},{8,16},{9,17... | collective-permute-start | bytes 1572872 | tf_op jit(solution)/shard_map/ppermute | solution.py:300
  45.6 28.2 %collective-permute-start.1 = (bf16[1024,256]{1,0:T(8,128)(2,1)S(1)}, bf16[1024,256]{1,0:T(8,128)(2,1)S(1)}, u32[]{:S(2)}, u32[]{:S(2)}) collective-permute-start(bf16[1024,256]{1,0:T(8,128)(2,1)S(1)} %bitcast.11), channel_id=1, source_target_pairs={{8,0},{9,1},{10,2},{11,3},{12,4},{13,5},{14,6},{15,7},{16,8},{17,9... | collective-permute-start | bytes 1572872 | tf_op jit(solution)/shard_map/ppermute | solution.py:300
  52.2 1.0 copy-start
  53.2 1.0 copy-start.1
  55.4 30.1 %all-to-all-start.1 = ((bf16[8,256,256]{2,1,0:T(8,128)(2,1)}), bf16[8,256,256]{2,1,0:T(8,128)(2,1)S(1)}, u32[]{:S(2)}, u32[]{:S(2)}) async-start(bf16[8,256,256]{2,1,0:T(8,128)(2,1)} %join_heads.1), calls=%async_computation.1 | async-start | bytes 2097152 | tf_op jit(solution)/shard_map/all_to_all | solution.py:274
  59.0 79.8 %all-gather.4.cloned.1.call-start = ((), (), s32[]{:S(2)}) async-start(), calls=%async_computation.3 | async-start | bytes 6963200 | tf_op jit(solution)/shard_map/all_gather | solution.py:324
  73.8 0.8 copy-start.3
  74.6 0.8 copy-start.5
  85.5 30.8 %collective-permute-start.3 = (bf16[1024,256]{1,0:T(8,128)(2,1)S(1)}, bf16[1024,256]{1,0:T(8,128)(2,1)S(1)}, u32[]{:S(2)}, u32[]{:S(2)}) collective-permute-start(bf16[1024,256]{1,0:T(8,128)(2,1)S(1)} %bitcast.15), channel_id=1, source_target_pairs={{0,8},{1,9},{2,10},{3,11},{4,12},{5,13},{6,14},{7,15},{8,16},{9,17... | collective-permute-start | bytes 1572872 | tf_op jit(solution)/shard_map/ppermute | solution.py:300
  87.5 31.0 %collective-permute-start.4 = (bf16[1024,256]{1,0:T(8,128)(2,1)S(1)}, bf16[1024,256]{1,0:T(8,128)(2,1)S(1)}, u32[]{:S(2)}, u32[]{:S(2)}) collective-permute-start(bf16[1024,256]{1,0:T(8,128)(2,1)S(1)} %bitcast.16), channel_id=1, source_target_pairs={{8,0},{9,1},{10,2},{11,3},{12,4},{13,5},{14,6},{15,7},{16,8},{17,9... | collective-permute-start | bytes 1572872 | tf_op jit(solution)/shard_map/ppermute | solution.py:300
  95.6 1.0 copy-start.4
  96.7 1.0 copy-start.6
  97.7 0.7 copy-start.8
Sparse Core Ops, SparseCore 0:
  85.6 52.9 all-gather.3

commit v11 on v10

--- a/solution.py
+++ b/solution.py
@@ -20,6 +20,7 @@
 CHUNK = 256
 PROJECT_STEP = 4
 HINT = 28_750_000_000
+HINT_LAST = 9_200_000_000
 PROJECT_VMEM = 56 * 1024 * 1024
 DIMS_NT = (((1,), (1,)), ((), ()))
 DIMS_TN = (((0,), (0,)), ((), ()))
@@ -97,7 +98,7 @@
     )(ok, vq, k, vq, kp, kn)
 
 
-def mix_kernel(pp_ref, pn_ref, vp_ref, vn_ref, acc_ref, total_ref, out_ref):
+def mix_kernel(ok_ref, pp_ref, pn_ref, vp_ref, vn_ref, acc_ref, total_ref, out_ref):
     tok = out_ref.shape[2]
     acc = acc_ref[0]
     for probs, values in ((pp_ref, vp_ref), (pn_ref, vn_ref)):
@@ -107,46 +108,50 @@
         out_ref[part] = result[:, part * tok : (part + 1) * tok]
 
 
-def mix(pp, pn, vp, vn, acc, total, tok):
-    rows, width = vp.shape
-    heads = width // HDIM
-    tile = min(MIX_TILE, rows)
-    side = pl.BlockSpec((rows, HDIM), lambda h, i: (0, h))
-    probs = pl.BlockSpec((1, rows, tile), lambda h, i: (h, 0, i))
+def mix(head, ok, pp, pn, vp, vn, acc, total, tok):
+    rows = vp.shape[0]
+    side = pl.BlockSpec((rows, HDIM), lambda i: (0, 0))
+    probs = pl.BlockSpec((1, rows, rows), lambda i: (head, 0, 0))
     return pl.pallas_call(
         mix_kernel,
-        grid=(heads, rows // tile),
+        grid=(1,),
         in_specs=[
+            pl.BlockSpec(memory_space=pltpu.SMEM),
             probs,
             probs,
             side,
             side,
-            pl.BlockSpec((1, HDIM, tile), lambda h, i: (h, 0, i)),
-            pl.BlockSpec((1, 8, tile), lambda h, i: (h, 0, i)),
-        ],
-        out_specs=pl.BlockSpec((tile // tok, HDIM, tok), lambda h, i: (i, h, 0)),
-        out_shape=jax.ShapeDtypeStruct((rows // tok, width, tok), jnp.bfloat16),
+            pl.BlockSpec((1, HDIM, rows), lambda i: (head, 0, 0)),
+            pl.BlockSpec((1, 8, rows), lambda i: (head, 0, 0)),
+        ],
+        out_specs=pl.BlockSpec((rows // tok, HDIM, tok), lambda i: (0, 0, 0)),
+        out_shape=jax.ShapeDtypeStruct((rows // tok, HDIM, tok), jnp.bfloat16),
         compiler_params=pltpu.CompilerParams(vmem_limit_bytes=VMEM),
         cost_estimate=pl.CostEstimate(
-            flops=4 * rows * rows * width, bytes_accessed=14 * rows * width, transcendentals=0
+            flops=4 * rows * rows * HDIM, bytes_accessed=14 * rows * HDIM, transcendentals=0
         ),
         name="mix",
-    )(pp, pn, vp, vn, acc, total)
-
-
-def project_kernel(cols, mirror_ref, w_ref, ctx_ref, out_ref, total_ref):
+    )(ok, pp, pn, vp, vn, acc, total)
+
+
+def gathered(mirror_ref, ctx_ref):
+    return jnp.concatenate([ctx_ref[g ^ mirror_ref[0]] for g in range(ctx_ref.shape[0])], axis=0)
+
+
+def project_first_kernel(mirror_ref, w_ref, ctx_ref, total_ref):
+    ctx = gathered(mirror_ref, ctx_ref)
+    for part in range(w_ref.shape[0]):
+        total_ref[part] = jnp.dot(w_ref[part, 0], ctx, preferred_element_type=jnp.float32)
+
+
+def project_last_kernel(cols, mirror_ref, w_ref, ctx_ref, first_ref, out_ref, total_ref):
     step = pl.program_id(0)
-    groups, width, _ = ctx_ref.shape
-    half = width // 2
+    ctx = gathered(mirror_ref, ctx_ref)
     lines, _, rows, _ = w_ref.shape
-    ctx = []
-    for h in range(2):
-        pieces = [ctx_ref[g ^ mirror_ref[0], h * half : (h + 1) * half, :] for g in range(groups)]
-        ctx.append(jnp.concatenate(pieces, axis=0))
     for part in range(lines):
-        total = jnp.dot(w_ref[part, 0], ctx[0], preferred_element_type=jnp.float32)
-        total += jnp.dot(w_ref[part, 1], ctx[1], preferred_element_type=jnp.float32)
-        total_ref[step * lines + part] = total
+        total_ref[step * lines + part] = first_ref[part] + jnp.dot(
+            w_ref[part, 0], ctx, preferred_element_type=jnp.float32
+        )
 
     @pl.when(step == pl.num_programs(0) - 1)
     def _():
@@ -157,27 +162,41 @@
         out_ref[...] = jnp.concatenate(pieces, axis=0).astype(jnp.bfloat16)
 
 
-def project(mirror, w, ctx, cols):
-    count, halves, rows, depth = w.shape
+def project(head, mirror, w, ctx, cols, first=None):
+    count, _, rows, depth = w.shape
     tok = ctx.shape[2]
     step = PROJECT_STEP
-    return pl.pallas_call(
-        functools.partial(project_kernel, cols),
+    totals = pl.BlockSpec((step, rows, tok), lambda i: (i, 0, 0))
+    in_specs = [
+        pl.BlockSpec(memory_space=pltpu.SMEM),
+        pl.BlockSpec((step, 1, rows, depth), lambda i: (i, head, 0, 0)),
+        pl.BlockSpec(ctx.shape, lambda i: (0, 0, 0)),
+    ]
+    options = dict(
         grid=(count // step,),
-        in_specs=[
-            pl.BlockSpec(memory_space=pltpu.SMEM),
-            pl.BlockSpec((step, halves, rows, depth), lambda i: (i, 0, 0, 0)),
-            pl.BlockSpec(ctx.shape, lambda i: (0, 0, 0)),
-        ],
+        compiler_params=pltpu.CompilerParams(vmem_limit_bytes=PROJECT_VMEM),
+        cost_estimate=pl.CostEstimate(
+            flops=2 * count * rows * depth * tok, bytes_accessed=2 * count * rows * depth, transcendentals=0
+        ),
+    )
+    if first is None:
+        return pl.pallas_call(
+            project_first_kernel,
+            in_specs=in_specs,
+            out_specs=totals,
+            out_shape=jax.ShapeDtypeStruct((count, rows, tok), jnp.float32),
+            name="project_first",
+            **options,
+        )(mirror, w, ctx)
+    return pl.pallas_call(
+        functools.partial(project_last_kernel, cols),
+        in_specs=in_specs + [totals],
         out_specs=pl.BlockSpec((count * rows, tok), lambda i: (0, 0)),
         out_shape=jax.ShapeDtypeStruct((count * rows, tok), jnp.bfloat16),
         scratch_shapes=[pltpu.VMEM((count, rows, tok), jnp.float32)],
-        compiler_params=pltpu.CompilerParams(vmem_limit_bytes=PROJECT_VMEM),
-        cost_estimate=pl.CostEstimate(
-            flops=2 * count * rows * depth * halves * tok, bytes_accessed=2 * count * rows * depth * halves, transcendentals=0
-        ),
-        name="project",
-    )(mirror, w, ctx)
+        name="project_last",
+        **options,
+    )(mirror, w, ctx, first)
 
 
 def columns(mirror_ref, chunk, width):
@@ -279,13 +298,13 @@
         out_ref[side] = ok_ref[side]
 
 
-def behind(ok, kp, kn):
+def behind(ok, kp, kn, hint):
     return pl.pallas_call(
         behind_kernel,
         in_specs=[pl.BlockSpec(memory_space=pltpu.SMEM)] + [pl.BlockSpec(memory_space=pl.ANY)] * 2,
         out_specs=pl.BlockSpec(memory_space=pltpu.SMEM),
         out_shape=jax.ShapeDtypeStruct(ok.shape, ok.dtype),
-        cost_estimate=pl.CostEstimate(flops=HINT, bytes_accessed=0, transcendentals=0),
+        cost_estimate=pl.CostEstimate(flops=hint, bytes_accessed=0, transcendentals=0),
         name="behind",
     )(ok, kp, kn)
 
@@ -316,16 +335,21 @@
     other = lax.ppermute(w_rows, "zh", [(0, 1), (1, 0)])
     pair = jnp.concatenate([jnp.where(first, w_rows, other), jnp.where(first, other, w_rows)])
     line = tighten(lax.all_gather(pair, "x"), cols)
-    ok = behind(ok, kp, kn)
+    ok = behind(ok, kp, kn, HINT)
     ok, vq, line = lax.optimization_barrier((ok, vq, line))
 
-    v = vq[:, :tok].reshape(8 * tok, -1)
-    vp, vn = to_block(v, 1), to_block(v, -1)
+    v = [vq[:, :tok, h * HDIM : (h + 1) * HDIM].reshape(8 * tok, HDIM) for h in range(2)]
+    vp0, vn0 = to_block(v[0], 1), to_block(v[0], -1)
+    vp1, vn1 = to_block(v[1], 1), to_block(v[1], -1)
     weight = lax.all_gather(line, ("y", "c")).reshape(8, 2, 8 * cols, depth)
     acc, total, pp, pn = score(ok, vq, k, kp, kn)
-    vp, vn, acc = lax.optimization_barrier((vp, vn, acc))
-    ctx = mix(pp, pn, vp, vn, acc, total, tok)
-    return project(mirror, weight, to_heads(ctx), cols).T
+    vp0, vn0, acc = lax.optimization_barrier((vp0, vn0, acc))
+    ctx0 = mix(0, ok, pp, pn, vp0, vn0, acc, total, tok)
+    ctx0 = to_heads(ctx0)
+    ok = behind(ok, vp1, vn1, HINT_LAST)
+    ctx1 = to_heads(mix(1, ok, pp, pn, vp1, vn1, acc, total, tok))
+    totals = project(0, mirror, weight, ctx0, cols)
+    return project(1, mirror, weight, ctx1, cols, totals).T
 
 
 def solution(mesh):

time: 152 us -> 170 us (1.12)
  starting transfers between devices: 39.2 us -> 58.9 us
  blocking collectives: 32.3 us -> 13.9 us
  local copies, waits for them, and re-layouts: 8.2 us -> 21.4 us
  Pallas kernels: 21.9 us -> 27.4 us
  waiting for transfers between devices: 34.7 us -> 32 us
    all_to_all x1 -> x0, blocking collectives: 18.4 us -> none  [to_heads(): return lax.all_to_all(chunks, HEAD, split_axis=0, concat_axis=0)]
    unnamed x18 -> x40, local copies, waits for them, and re-layouts: 8.16 us -> 21.3 us
    ppermute x4 -> x6, starting transfers between devices: 20.1 us -> 30.2 us  [to_block(): return lax.ppermute(value, AXES, pairs)]
    all_to_all x2 -> x4, starting transfers between devices: 10.8 us -> 20.4 us  [to_heads(): return lax.all_to_all(chunks, HEAD, split_axis=0, concat_axis=0)]
    ppermute x4 -> x6, waiting for transfers between devices: 9.01 us -> 0.02 us  [to_block(): return lax.ppermute(value, AXES, pairs)]
    all_to_all x2 -> x4, waiting for transfers between devices: 25.7 us -> 31.9 us  [to_heads(): return lax.all_to_all(chunks, HEAD, split_axis=0, concat_axis=0)]
    pallas_call x2 -> x4, Pallas kernels: 6.75 us -> 11.1 us  [the longest x2 4.01 us: mix(): pl.pallas_call(mix_kernel, grid=(1,), in_specs=[pl.BlockSpec(memory_space...]
  transfers between devices with their start and end apart: 8 -> 12, of which waited for: 4 -> 3; matrix products, arithmetic and copies ran while one was open for 0% -> 0% of each run, Pallas kernels for 11% -> 14%
where the time goes in v11:
time: 170 us; the launch traced here: 168 us
  starting transfers between devices  58.9 us (35%)
  waiting for transfers between devices  32 us (19%)
  Pallas kernels  27.4 us (16%)
  local copies, waits for them, and re-layouts  21.4 us (13%)
  blocking collectives  13.9 us (8%)
  between operations  13.6 us (8%)
    all_to_all x4, waiting for transfers between devices, to_heads(): return lax.all_to_all(chunks, HEAD, split_axis=0, concat_axis=0)  31.9 us
    ppermute x6, starting transfers between devices, to_block(): return lax.ppermute(value, AXES, pairs)  30.2 us
    unnamed x40, local copies, waits for them, and re-layouts  21.3 us
    all_to_all x4, starting transfers between devices, to_heads(): return lax.all_to_all(chunks, HEAD, split_axis=0, concat_axis=0)  20.4 us
    all_gather x1, blocking collectives, local(): line = tighten(lax.all_gather(pair, 'x'), cols)  13.9 us
    pallas_call x1, Pallas kernels, score(): pl.pallas_call(score_kernel, grid=(heads,), in_specs=[pl.BlockSpec(memory...  11.1 us
    ppermute x1, starting transfers between devices, local(): other = lax.ppermute(w_rows, 'zh', [(0, 1), (1, 0)])  8.22 us
    pallas_call x2, Pallas kernels, mix(): pl.pallas_call(mix_kernel, grid=(1,), in_specs=[pl.BlockSpec(memory_space...  4.01 us
  transfers between devices with their start and end apart: 12, of which 3 were waited for; matrix products, arithmetic and copies ran while one was open for 0% of the time, Pallas kernels for 14%

profile of v11, /device:TPU:6, one launch (start us, length us, event | category | flops | bytes accessed | tf_op | source)
XLA Modules:
  0.0 167.9 jit_solution(7827660907925854396)
XLA Ops:
  6.5 1.0 copy-done.6
  9.2 7.3 %all-to-all-start = ((bf16[8,144,256]{2,1,0:T(8,128)(2,1)}), bf16[8,144,256]{2,1,0:T(8,128)(2,1)S(1)}, u32[]{:S(2)}, u32[]{:S(2)}) async-start(bf16[8,144,256]{2,1,0:T(8,128)(2,1)} %pack.1), calls=%async_computation | async-start | bytes 1179648 | tf_op jit(solution)/shard_map/all_to_all | solution.py:293
  16.4 16.8 %all-to-all-done.in_ref = bf16[8,144,256]{2,1,0:T(8,128)(2,1)S(1)} async-done(((bf16[8,144,256]{2,1,0:T(8,128)(2,1)}), bf16[8,144,256]{2,1,0:T(8,128)(2,1)S(1)}, u32[]{:S(2)}, u32[]{:S(2)}) %all-to-all-start) | async-done | bytes 589856 | tf_op jit(solution)/shard_map/all_to_all | solution.py:293
  33.3 8.2 %collective-permute-start.2 = (bf16[32,1024]{1,0:T(8,128)(2,1)S(1)}, bf16[32,1024]{1,0:T(8,128)(2,1)S(1)}, u32[]{:S(2)}, u32[]{:S(2)}) collective-permute-start(bf16[32,1024]{1,0:T(8,128)(2,1)S(1)} %get-tuple-element.21), channel_id=1, source_target_pairs={{0,64},{64,0},{1,65},{65,1},{2,66},{66,2},{3,67},{67,3},{4,68},{68... | collective-permute-start | bytes 196616 | tf_op jit(solution)/shard_map/ppermute | solution.py:335
  42.1 3.5 %collective-permute-start = (bf16[1024,256]{1,0:T(8,128)(2,1)S(1)}, bf16[1024,256]{1,0:T(8,128)(2,1)S(1)}, u32[]{:S(2)}, u32[]{:S(2)}) collective-permute-start(bf16[1024,256]{1,0:T(8,128)(2,1)S(1)} %bitcast.11), channel_id=1, source_target_pairs={{0,8},{1,9},{2,10},{3,11},{4,12},{5,13},{6,14},{7,15},{8,16},{9,17... | collective-permute-start | bytes 1572872 | tf_op jit(solution)/shard_map/ppermute | solution.py:319
  45.6 6.6 %collective-permute-start.1 = (bf16[1024,256]{1,0:T(8,128)(2,1)S(1)}, bf16[1024,256]{1,0:T(8,128)(2,1)S(1)}, u32[]{:S(2)}, u32[]{:S(2)}) collective-permute-start(bf16[1024,256]{1,0:T(8,128)(2,1)S(1)} %bitcast.12), channel_id=1, source_target_pairs={{8,0},{9,1},{10,2},{11,3},{12,4},{13,5},{14,6},{15,7},{16,8},{17,9... | collective-permute-start | bytes 1572872 | tf_op jit(solution)/shard_map/ppermute | solution.py:319
  52.2 1.0 copy-done.4
  53.3 1.0 copy-done.5
  54.3 1.1 join_heads.1
  55.4 3.6 %all-to-all-start.1 = ((bf16[8,256,256]{2,1,0:T(8,128)(2,1)}), bf16[8,256,256]{2,1,0:T(8,128)(2,1)S(1)}, u32[]{:S(2)}, u32[]{:S(2)}) async-start(bf16[8,256,256]{2,1,0:T(8,128)(2,1)} %join_heads.1), calls=%async_computation.1 | async-start | bytes 2097152 | tf_op jit(solution)/shard_map/all_to_all | solution.py:293
  59.1 13.9 %all-gather = bf16[256,1024]{1,0:T(8,128)(2,1)S(1)} all-gather(bf16[64,1024]{1,0:T(8,128)(2,1)S(1)} %pad_maximum_fusion), channel_id=2, replica_groups=mesh['x'=4,'zh'=2,'y'=8,'zl'=4,'c'=2] {'x'}, dimensions={0}, use_global_device_ids=true | all-gather | bytes 655360 | tf_op jit(solution)/shard_map/all_gather | solution.py:337
  75.4 1.2 behind.2.ok_ref
  76.6 8.9 %all-to-all-done.1.q_ref.v_ref = bf16[8,256,256]{2,1,0:T(8,128)(2,1)S(1)} async-done(((bf16[8,256,256]{2,1,0:T(8,128)(2,1)}), bf16[8,256,256]{2,1,0:T(8,128)(2,1)S(1)}, u32[]{:S(2)}, u32[]{:S(2)}) %all-to-all-start.1) | async-done | bytes 1048608 | tf_op jit(solution)/shard_map/all_to_all | solution.py:293
  85.6 1.9 %collective-permute-start.5 = (bf16[1024,128]{1,0:T(8,128)(2,1)S(1)}, bf16[1024,128]{1,0:T(8,128)(2,1)S(1)}, u32[]{:S(2)}, u32[]{:S(2)}) collective-permute-start(bf16[1024,128]{1,0:T(8,128)(2,1)S(1)} %bitcast.19), channel_id=1, source_target_pairs={{0,8},{1,9},{2,10},{3,11},{4,12},{5,13},{6,14},{7,15},{8,16},{9,17... | collective-permute-start | bytes 786440 | tf_op jit(solution)/shard_map/ppermute | solution.py:319
  87.6 8.1 %collective-permute-start.6 = (bf16[1024,128]{1,0:T(8,128)(2,1)S(1)}, bf16[1024,128]{1,0:T(8,128)(2,1)S(1)}, u32[]{:S(2)}, u32[]{:S(2)}) collective-permute-start(bf16[1024,128]{1,0:T(8,128)(2,1)S(1)} %bitcast.20), channel_id=1, source_target_pairs={{8,0},{9,1},{10,2},{11,3},{12,4},{13,5},{14,6},{15,7},{16,8},{17,9... | collective-permute-start | bytes 786440 | tf_op jit(solution)/shard_map/ppermute | solution.py:319
  95.7 1.9 %collective-permute-start.3 = (bf16[1024,128]{1,0:T(8,128)(2,1)S(1)}, bf16[1024,128]{1,0:T(8,128)(2,1)S(1)}, u32[]{:S(2)}, u32[]{:S(2)}) collective-permute-start(bf16[1024,128]{1,0:T(8,128)(2,1)S(1)} %bitcast.17), channel_id=1, source_target_pairs={{0,8},{1,9},{2,10},{3,11},{4,12},{5,13},{6,14},{7,15},{8,16},{9,17... | collective-permute-start | bytes 786440 | tf_op jit(solution)/shard_map/ppermute | solution.py:319
  97.6 8.1 %collective-permute-start.4 = (bf16[1024,128]{1,0:T(8,128)(2,1)S(1)}, bf16[1024,128]{1,0:T(8,128)(2,1)S(1)}, u32[]{:S(2)}, u32[]{:S(2)}) collective-permute-start(bf16[1024,128]{1,0:T(8,128)(2,1)S(1)} %bitcast.18), channel_id=1, source_target_pairs={{8,0},{9,1},{10,2},{11,3},{12,4},{13,5},{14,6},{15,7},{16,8},{17,9... | collective-permute-start | bytes 786440 | tf_op jit(solution)/shard_map/ppermute | solution.py:319
  105.8 1.0 copy-done.8
  106.8 1.0 copy-done.10
  108.5 11.1 %score.1 = (f32[2,128,1024]{2,1,0:T(8,128)S(1)}, f32[2,8,1024]{2,1,0:T(8,128)S(1)}, bf16[2,1024,1024]{2,1,0:T(8,128)(2,1)S(1)}, bf16[2,1024,1024]{2,1,0:T(8,128)(2,1)S(1)}) custom-call(s32[2]{0:T(128)S(1)} %copy-done.16, bf16[8,256,256]{2,1,0:T(8,128)(2,1)S(1)} %all-to-all-done.1.q_ref.v_ref, bf16[1024,256]{1,0:T(8,128)(2,1)S(1)} %bitcast.13, ...), custom_call_target="tpu_custom_call" | custom-call | flops 262144 | bytes 262144 | tf_op jit(solution)/shard_map/score/pallas_call | solution.py:72
  119.6 2.0 %mix.3 = bf16[8,128,128]{2,1,0:T(8,128)(2,1)} custom-call(s32[2]{0:T(128)S(1)} %copy-done.16, bf16[2,1024,1024]{2,1,0:T(8,128)(2,1)S(1)} %get-tuple-element.26.pp_ref, bf16[2,1024,1024]{2,1,0:T(8,128)(2,1)S(1)} %get-tuple-element.27.pn_ref, bf16[1024,128]{1,0:T(8,128)(2,1)S(1)} %collective-permute-done.5.vp_ref, ...), custom_call_target="tpu_custom_call" | custom-call | flops 536870912 | bytes 1835008 | tf_op jit(solution)/shard_map/mix/pallas_call | solution.py:115
  121.6 2.1 %copy-done = bf16[2,1024,1024]{2,1,0:T(8,128)(2,1)} copy-done((bf16[2,1024,1024]{2,1,0:T(8,128)(2,1)}, bf16[2,1024,1024]{2,1,0:T(8,128)(2,1)S(1)}, u32[]{:S(2)}) %copy-start) | copy-done | bytes 4194328
  123.7 2.1 %copy-done.2 = bf16[2,1024,1024]{2,1,0:T(8,128)(2,1)} copy-done((bf16[2,1024,1024]{2,1,0:T(8,128)(2,1)}, bf16[2,1024,1024]{2,1,0:T(8,128)(2,1)S(1)}, u32[]{:S(2)}) %copy-start.2) | copy-done | bytes 4194328
  125.7 4.5 %all-to-all-start.3 = ((bf16[8,128,128]{2,1,0:T(8,128)(2,1)}), bf16[8,128,128]{2,1,0:T(8,128)(2,1)S(1)}, u32[]{:S(2)}, u32[]{:S(2)}) async-start(bf16[8,128,128]{2,1,0:T(8,128)(2,1)} %mix.3), calls=%async_computation.3 | async-start | bytes 524288 | tf_op jit(solution)/shard_map/all_to_all | solution.py:293
  131.7 1.2 behind.3.ok_ref
  132.9 2.3 %copy-done.1 = bf16[2,1024,1024]{2,1,0:T(8,128)(2,1)S(1)} copy-done((bf16[2,1024,1024]{2,1,0:T(8,128)(2,1)S(1)}, bf16[2,1024,1024]{2,1,0:T(8,128)(2,1)}, u32[]{:S(2)}) %copy-start.1) | copy-done | bytes 4194328
  135.1 2.2 %copy-done.3 = bf16[2,1024,1024]{2,1,0:T(8,128)(2,1)S(1)} copy-done((bf16[2,1024,1024]{2,1,0:T(8,128)(2,1)S(1)}, bf16[2,1024,1024]{2,1,0:T(8,128)(2,1)}, u32[]{:S(2)}) %copy-start.3) | copy-done | bytes 4194328
  139.9 2.0 %mix.2 = bf16[8,128,128]{2,1,0:T(8,128)(2,1)} custom-call(s32[2]{0:T(128)S(1)} %copy-done.17, bf16[2,1024,1024]{2,1,0:T(8,128)(2,1)S(1)} %copy-done.1, bf16[2,1024,1024]{2,1,0:T(8,128)(2,1)S(1)} %copy-done.3, bf16[1024,128]{1,0:T(8,128)(2,1)S(1)} %copy-done.12, bf16[1024,128]{1,0:T(8,128)(2,1)S(1)} %copy-done.14, ...), custom_call_target="tpu_custom_call" | custom-call | flops 536870912 | bytes 1835008 | tf_op jit(solution)/shard_map/mix/pallas_call | solution.py:115
  141.9 5.1 %all-to-all-start.2 = ((bf16[8,128,128]{2,1,0:T(8,128)(2,1)}), bf16[8,128,128]{2,1,0:T(8,128)(2,1)S(1)}, u32[]{:S(2)}, u32[]{:S(2)}) async-start(bf16[8,128,128]{2,1,0:T(8,128)(2,1)} %mix.2), calls=%async_computation.2 | async-start | bytes 524288 | tf_op jit(solution)/shard_map/all_to_all | solution.py:293
  147.0 3.4 %project_first.1.first_ref = f32[8,200,128]{2,1,0:T(8,128)} custom-call(s32[1]{0:T(128)} %bitcast.mirror_ref, bf16[8,2,200,1024]{3,2,1,0:T(8,128)(2,1)} %bitcast.15, bf16[8,128,128]{2,1,0:T(8,128)(2,1)} %copy-done.18), custom_call_target="tpu_custom_call" | custom-call | flops 419430400 | bytes 3276800 | tf_op jit(solution)/shard_map/project_first/pallas_call | solution.py:183
  150.4 6.3 %all-to-all-done.2.ctx_ref = bf16[8,128,128]{2,1,0:T(8,128)(2,1)S(1)} async-done(((bf16[8,128,128]{2,1,0:T(8,128)(2,1)}), bf16[8,128,128]{2,1,0:T(8,128)(2,1)S(1)}, u32[]{:S(2)}, u32[]{:S(2)}) %all-to-all-start.2) | async-done | bytes 262176 | tf_op jit(solution)/shard_map/all_to_all | solution.py:293
  157.4 3.6 %project_last.1 = bf16[1600,128]{1,0:T(8,128)(2,1)} custom-call(s32[1]{0:T(128)} %bitcast.mirror_ref, bf16[8,2,200,1024]{3,2,1,0:T(8,128)(2,1)} %bitcast.16, bf16[8,128,128]{2,1,0:T(8,128)(2,1)} %copy-done.19, f32[8,200,128]{2,1,0:T(8,128)} %project_first.1.first_ref), custom_call_target="tpu_custom_call" | custom-call | flops 419430400 | bytes 3276800 | tf_op jit(solution)/shard_map/project_last/pallas_call | solution.py:191
  (49 shorter events, 10.2 us)
Async XLA Ops:
  6.5 1.0 copy-start.6
  7.6 0.7 copy-start.15
  9.2 24.0 %all-to-all-start = ((bf16[8,144,256]{2,1,0:T(8,128)(2,1)}), bf16[8,144,256]{2,1,0:T(8,128)(2,1)S(1)}, u32[]{:S(2)}, u32[]{:S(2)}) async-start(bf16[8,144,256]{2,1,0:T(8,128)(2,1)} %pack.1), calls=%async_computation | async-start | bytes 1179648 | tf_op jit(solution)/shard_map/all_to_all | solution.py:293
  33.3 25.8 %collective-permute-start.2 = (bf16[32,1024]{1,0:T(8,128)(2,1)S(1)}, bf16[32,1024]{1,0:T(8,128)(2,1)S(1)}, u32[]{:S(2)}, u32[]{:S(2)}) collective-permute-start(bf16[32,1024]{1,0:T(8,128)(2,1)S(1)} %get-tuple-element.21), channel_id=1, source_target_pairs={{0,64},{64,0},{1,65},{65,1},{2,66},{66,2},{3,67},{67,3},{4,68},{68... | collective-permute-start | bytes 196616 | tf_op jit(solution)/shard_map/ppermute | solution.py:335
  42.1 31.7 %collective-permute-start = (bf16[1024,256]{1,0:T(8,128)(2,1)S(1)}, bf16[1024,256]{1,0:T(8,128)(2,1)S(1)}, u32[]{:S(2)}, u32[]{:S(2)}) collective-permute-start(bf16[1024,256]{1,0:T(8,128)(2,1)S(1)} %bitcast.11), channel_id=1, source_target_pairs={{0,8},{1,9},{2,10},{3,11},{4,12},{5,13},{6,14},{7,15},{8,16},{9,17... | collective-permute-start | bytes 1572872 | tf_op jit(solution)/shard_map/ppermute | solution.py:319
  45.6 28.2 %collective-permute-start.1 = (bf16[1024,256]{1,0:T(8,128)(2,1)S(1)}, bf16[1024,256]{1,0:T(8,128)(2,1)S(1)}, u32[]{:S(2)}, u32[]{:S(2)}) collective-permute-start(bf16[1024,256]{1,0:T(8,128)(2,1)S(1)} %bitcast.12), channel_id=1, source_target_pairs={{8,0},{9,1},{10,2},{11,3},{12,4},{13,5},{14,6},{15,7},{16,8},{17,9... | collective-permute-start | bytes 1572872 | tf_op jit(solution)/shard_map/ppermute | solution.py:319
  52.2 1.0 copy-start.4
  53.3 1.0 copy-start.5
  55.4 30.1 %all-to-all-start.1 = ((bf16[8,256,256]{2,1,0:T(8,128)(2,1)}), bf16[8,256,256]{2,1,0:T(8,128)(2,1)S(1)}, u32[]{:S(2)}, u32[]{:S(2)}) async-start(bf16[8,256,256]{2,1,0:T(8,128)(2,1)} %join_heads.1), calls=%async_computation.1 | async-start | bytes 2097152 | tf_op jit(solution)/shard_map/all_to_all | solution.py:293
  59.0 88.0 %all-gather.4.cloned.1.call-start = ((), (), s32[]{:S(2)}) async-start(), calls=%async_computation.4 | async-start | bytes 6963200 | tf_op jit(solution)/shard_map/all_gather | solution.py:344
  73.8 0.8 copy-start.7
  74.6 0.8 copy-start.9
  85.6 33.9 %collective-permute-start.5 = (bf16[1024,128]{1,0:T(8,128)(2,1)S(1)}, bf16[1024,128]{1,0:T(8,128)(2,1)S(1)}, u32[]{:S(2)}, u32[]{:S(2)}) collective-permute-start(bf16[1024,128]{1,0:T(8,128)(2,1)S(1)} %bitcast.19), channel_id=1, source_target_pairs={{0,8},{1,9},{2,10},{3,11},{4,12},{5,13},{6,14},{7,15},{8,16},{9,17... | collective-permute-start | bytes 786440 | tf_op jit(solution)/shard_map/ppermute | solution.py:319
  87.6 32.0 %collective-permute-start.6 = (bf16[1024,128]{1,0:T(8,128)(2,1)S(1)}, bf16[1024,128]{1,0:T(8,128)(2,1)S(1)}, u32[]{:S(2)}, u32[]{:S(2)}) collective-permute-start(bf16[1024,128]{1,0:T(8,128)(2,1)S(1)} %bitcast.20), channel_id=1, source_target_pairs={{8,0},{9,1},{10,2},{11,3},{12,4},{13,5},{14,6},{15,7},{16,8},{17,9... | collective-permute-start | bytes 786440 | tf_op jit(solution)/shard_map/ppermute | solution.py:319
  95.7 34.6 %collective-permute-start.3 = (bf16[1024,128]{1,0:T(8,128)(2,1)S(1)}, bf16[1024,128]{1,0:T(8,128)(2,1)S(1)}, u32[]{:S(2)}, u32[]{:S(2)}) collective-permute-start(bf16[1024,128]{1,0:T(8,128)(2,1)S(1)} %bitcast.17), channel_id=1, source_target_pairs={{0,8},{1,9},{2,10},{3,11},{4,12},{5,13},{6,14},{7,15},{8,16},{9,17... | collective-permute-start | bytes 786440 | tf_op jit(solution)/shard_map/ppermute | solution.py:319
  97.6 32.7 %collective-permute-start.4 = (bf16[1024,128]{1,0:T(8,128)(2,1)S(1)}, bf16[1024,128]{1,0:T(8,128)(2,1)S(1)}, u32[]{:S(2)}, u32[]{:S(2)}) collective-permute-start(bf16[1024,128]{1,0:T(8,128)(2,1)S(1)} %bitcast.18), channel_id=1, source_target_pairs={{8,0},{9,1},{10,2},{11,3},{12,4},{13,5},{14,6},{15,7},{16,8},{17,9... | collective-permute-start | bytes 786440 | tf_op jit(solution)/shard_map/ppermute | solution.py:319
  105.8 1.0 copy-start.8
  106.8 1.0 copy-start.10
  107.9 0.6 copy-start.16
  121.6 2.1 %copy-start = (bf16[2,1024,1024]{2,1,0:T(8,128)(2,1)}, bf16[2,1024,1024]{2,1,0:T(8,128)(2,1)S(1)}, u32[]{:S(2)}) copy-start(bf16[2,1024,1024]{2,1,0:T(8,128)(2,1)S(1)} %get-tuple-element.26.pp_ref) | copy-start | bytes 12582916
  123.7 2.1 %copy-start.2 = (bf16[2,1024,1024]{2,1,0:T(8,128)(2,1)}, bf16[2,1024,1024]{2,1,0:T(8,128)(2,1)S(1)}, u32[]{:S(2)}) copy-start(bf16[2,1024,1024]{2,1,0:T(8,128)(2,1)S(1)} %get-tuple-element.27.pn_ref) | copy-start | bytes 12582916
  125.7 16.1 %all-to-all-start.3 = ((bf16[8,128,128]{2,1,0:T(8,128)(2,1)}), bf16[8,128,128]{2,1,0:T(8,128)(2,1)S(1)}, u32[]{:S(2)}, u32[]{:S(2)}) async-start(bf16[8,128,128]{2,1,0:T(8,128)(2,1)} %mix.3), calls=%async_computation.3 | async-start | bytes 524288 | tf_op jit(solution)/shard_map/all_to_all | solution.py:293
  130.3 0.7 copy-start.11
  131.0 0.7 copy-start.13
  132.9 2.3 %copy-start.1 = (bf16[2,1024,1024]{2,1,0:T(8,128)(2,1)S(1)}, bf16[2,1024,1024]{2,1,0:T(8,128)(2,1)}, u32[]{:S(2)}) copy-start(bf16[2,1024,1024]{2,1,0:T(8,128)(2,1)} %copy-done) | copy-start | bytes 12582916
  135.1 2.2 %copy-start.3 = (bf16[2,1024,1024]{2,1,0:T(8,128)(2,1)S(1)}, bf16[2,1024,1024]{2,1,0:T(8,128)(2,1)}, u32[]{:S(2)}) copy-start(bf16[2,1024,1024]{2,1,0:T(8,128)(2,1)} %copy-done.2) | copy-start | bytes 12582916
  137.4 1.0 copy-start.12
  138.3 0.9 copy-start.14
  139.3 0.6 copy-start.17
  141.9 5.1 %copy-start.18 = (bf16[8,128,128]{2,1,0:T(8,128)(2,1)}, bf16[8,128,128]{2,1,0:T(8,128)(2,1)S(1)}, u32[]{:S(2)}) copy-start(bf16[8,128,128]{2,1,0:T(8,128)(2,1)S(1)} %all-to-all-done.3.ctx_ref) | copy-start | bytes 786436
  141.9 14.8 %all-to-all-start.2 = ((bf16[8,128,128]{2,1,0:T(8,128)(2,1)}), bf16[8,128,128]{2,1,0:T(8,128)(2,1)S(1)}, u32[]{:S(2)}, u32[]{:S(2)}) async-start(bf16[8,128,128]{2,1,0:T(8,128)(2,1)} %mix.2), calls=%async_computation.2 | async-start | bytes 524288 | tf_op jit(solution)/shard_map/all_to_all | solution.py:293
  156.7 0.7 copy-start.19
Sparse Core Ops, SparseCore 0:
  85.6 52.9 all-gather.3

commit v12 on v10

--- a/solution.py
+++ b/solution.py
@@ -307,12 +307,13 @@
     ok = jnp.stack([here > 0, here < N_BLK - 1]).astype(jnp.int32)
     first = lax.axis_index("zh") == 0
     mirror = jnp.where(first, 0, 6).astype(jnp.int32)[None]
+    joined = join_heads(mirror, values, queries)
     k, w_rows = unpack(to_heads(pack(mirror, keys, w_out.T)))
     k = k.reshape(8 * tok, -1)
 
     kp, kn = to_block(k, 1), to_block(k, -1)
-    values, k = lax.optimization_barrier((values, k))
-    vq = to_heads(join_heads(mirror, values, queries))
+    vq, k = lax.optimization_barrier((joined, k))
+    vq = to_heads(vq)
     other = lax.ppermute(w_rows, "zh", [(0, 1), (1, 0)])
     pair = jnp.concatenate([jnp.where(first, w_rows, other), jnp.where(first, other, w_rows)])
     line = tighten(lax.all_gather(pair, "x"), cols)

time: 152 us -> 150 us (0.987)
  waiting for transfers between devices: 34.7 us -> 31.1 us
  blocking collectives: 32.3 us -> 33.9 us
    all_to_all x2, waiting for transfers between devices: 25.7 us -> 21.1 us  [to_heads(): return lax.all_to_all(chunks, HEAD, split_axis=0, concat_axis=0)]
    all_to_all x1, blocking collectives: 18.4 us -> 20.1 us  [to_heads(): return lax.all_to_all(chunks, HEAD, split_axis=0, concat_axis=0)]
  transfers between devices with their start and end apart: 8 -> 8, of which waited for: 4 -> 5; matrix products, arithmetic and copies ran while one was open for 0% -> 0% of each run, Pallas kernels for 11% -> 11%
where the time goes in v12:
time: 150 us; the launch traced here: 149 us
  starting transfers between devices  39.2 us (26%)
  blocking collectives  33.9 us (23%)
  waiting for transfers between devices  31.1 us (21%)
  Pallas kernels  21.9 us (15%)
  between operations  13.5 us (9%)
  local copies, waits for them, and re-layouts  8.2 us (5%)
    all_to_all x2, waiting for transfers between devices, to_heads(): return lax.all_to_all(chunks, HEAD, split_axis=0, concat_axis=0)  21.1 us
    ppermute x4, starting transfers between devices, to_block(): return lax.ppermute(value, AXES, pairs)  20.1 us
    all_to_all x1, blocking collectives, to_heads(): return lax.all_to_all(chunks, HEAD, split_axis=0, concat_axis=0)  20.1 us
    all_gather x1, blocking collectives, local(): line = tighten(lax.all_gather(pair, 'x'), cols)  13.8 us
    pallas_call x1, Pallas kernels, score(): pl.pallas_call(score_kernel, grid=(heads,), in_specs=[pl.BlockSpec(memory...  11.1 us
    all_to_all x2, starting transfers between devices, to_heads(): return lax.all_to_all(chunks, HEAD, split_axis=0, concat_axis=0)  10.8 us
    ppermute x4, waiting for transfers between devices, to_block(): return lax.ppermute(value, AXES, pairs)  10 us
    ppermute x1, starting transfers between devices, local(): other = lax.ppermute(w_rows, 'zh', [(0, 1), (1, 0)])  8.22 us
  transfers between devices with their start and end apart: 8, of which 5 were waited for; matrix products, arithmetic and copies ran while one was open for 0% of the time, Pallas kernels for 11%

profile of v12, /device:TPU:6, one launch (start us, length us, event | category | flops | bytes accessed | tf_op | source)
XLA Modules:
  0.0 148.5 jit_solution(8827755574291121219)
XLA Ops:
  6.5 1.0 copy-done.2
  7.6 0.7 copy-done.7
  8.3 0.9 pack.1
  9.2 7.3 %all-to-all-start = ((bf16[8,144,256]{2,1,0:T(8,128)(2,1)}), bf16[8,144,256]{2,1,0:T(8,128)(2,1)S(1)}, u32[]{:S(2)}, u32[]{:S(2)}) async-start(bf16[8,144,256]{2,1,0:T(8,128)(2,1)} %pack.1), calls=%async_computation | async-start | bytes 1179648 | tf_op jit(solution)/shard_map/all_to_all | solution.py:274
  16.5 1.0 copy-done
  17.5 1.0 copy-done.1
  18.6 1.1 join_heads.1
  19.7 13.5 %all-to-all-done.in_ref = bf16[8,144,256]{2,1,0:T(8,128)(2,1)S(1)} async-done(((bf16[8,144,256]{2,1,0:T(8,128)(2,1)}), bf16[8,144,256]{2,1,0:T(8,128)(2,1)S(1)}, u32[]{:S(2)}, u32[]{:S(2)}) %all-to-all-start) | async-done | bytes 589856 | tf_op jit(solution)/shard_map/all_to_all | solution.py:274
  33.3 8.2 %collective-permute-start.2 = (bf16[32,1024]{1,0:T(8,128)(2,1)S(1)}, bf16[32,1024]{1,0:T(8,128)(2,1)S(1)}, u32[]{:S(2)}, u32[]{:S(2)}) collective-permute-start(bf16[32,1024]{1,0:T(8,128)(2,1)S(1)} %get-tuple-element.21), channel_id=1, source_target_pairs={{0,64},{64,0},{1,65},{65,1},{2,66},{66,2},{3,67},{67,3},{4,68},{68... | collective-permute-start | bytes 196616 | tf_op jit(solution)/shard_map/ppermute | solution.py:317
  41.5 0.6 add_convert_fusion.ok_ref
  42.1 3.5 %collective-permute-start = (bf16[1024,256]{1,0:T(8,128)(2,1)S(1)}, bf16[1024,256]{1,0:T(8,128)(2,1)S(1)}, u32[]{:S(2)}, u32[]{:S(2)}) collective-permute-start(bf16[1024,256]{1,0:T(8,128)(2,1)S(1)} %bitcast.10), channel_id=1, source_target_pairs={{0,8},{1,9},{2,10},{3,11},{4,12},{5,13},{6,14},{7,15},{8,16},{9,17... | collective-permute-start | bytes 1572872 | tf_op jit(solution)/shard_map/ppermute | solution.py:300
  45.6 6.6 %collective-permute-start.1 = (bf16[1024,256]{1,0:T(8,128)(2,1)S(1)}, bf16[1024,256]{1,0:T(8,128)(2,1)S(1)}, u32[]{:S(2)}, u32[]{:S(2)}) collective-permute-start(bf16[1024,256]{1,0:T(8,128)(2,1)S(1)} %bitcast.11), channel_id=1, source_target_pairs={{8,0},{9,1},{10,2},{11,3},{12,4},{13,5},{14,6},{15,7},{16,8},{17,9... | collective-permute-start | bytes 1572872 | tf_op jit(solution)/shard_map/ppermute | solution.py:300
  52.2 3.6 %all-to-all-start.1 = ((bf16[8,256,256]{2,1,0:T(8,128)(2,1)}), bf16[8,256,256]{2,1,0:T(8,128)(2,1)S(1)}, u32[]{:S(2)}, u32[]{:S(2)}) async-start(bf16[8,256,256]{2,1,0:T(8,128)(2,1)} %join_heads.1), calls=%async_computation.1 | async-start | bytes 2097152 | tf_op jit(solution)/shard_map/all_to_all | solution.py:274
  55.8 0.0 all-gather.4.cloned.1.call-start
  55.9 13.8 %all-gather = bf16[256,1024]{1,0:T(8,128)(2,1)S(1)} all-gather(bf16[64,1024]{1,0:T(8,128)(2,1)S(1)} %pad_maximum_fusion), channel_id=2, replica_groups=mesh['x'=4,'zh'=2,'y'=8,'zl'=4,'c'=2] {'x'}, dimensions={0}, use_global_device_ids=true | all-gather | bytes 655360 | tf_op jit(solution)/shard_map/all_gather | solution.py:319
  69.7 0.9 tighten.1
  70.5 1.4 collective-permute-done.kp_ref
  72.0 0.8 copy-done.3
  72.8 0.8 copy-done.5
  73.5 1.2 behind.1.ok_ref
  74.7 7.6 %all-to-all-done.1.q_ref.v_ref = bf16[8,256,256]{2,1,0:T(8,128)(2,1)S(1)} async-done(((bf16[8,256,256]{2,1,0:T(8,128)(2,1)}), bf16[8,256,256]{2,1,0:T(8,128)(2,1)S(1)}, u32[]{:S(2)}, u32[]{:S(2)}) %all-to-all-start.1) | async-done | bytes 1048608 | tf_op jit(solution)/shard_map/all_to_all | solution.py:274
  82.3 1.9 %collective-permute-start.3 = (bf16[1024,256]{1,0:T(8,128)(2,1)S(1)}, bf16[1024,256]{1,0:T(8,128)(2,1)S(1)}, u32[]{:S(2)}, u32[]{:S(2)}) collective-permute-start(bf16[1024,256]{1,0:T(8,128)(2,1)S(1)} %bitcast.15), channel_id=1, source_target_pairs={{0,8},{1,9},{2,10},{3,11},{4,12},{5,13},{6,14},{7,15},{8,16},{9,17... | collective-permute-start | bytes 1572872 | tf_op jit(solution)/shard_map/ppermute | solution.py:300
  84.3 8.1 %collective-permute-start.4 = (bf16[1024,256]{1,0:T(8,128)(2,1)S(1)}, bf16[1024,256]{1,0:T(8,128)(2,1)S(1)}, u32[]{:S(2)}, u32[]{:S(2)}) collective-permute-start(bf16[1024,256]{1,0:T(8,128)(2,1)S(1)} %bitcast.16), channel_id=1, source_target_pairs={{8,0},{9,1},{10,2},{11,3},{12,4},{13,5},{14,6},{15,7},{16,8},{17,9... | collective-permute-start | bytes 1572872 | tf_op jit(solution)/shard_map/ppermute | solution.py:300
  92.4 1.0 copy-done.4
  93.5 1.0 copy-done.6
  94.5 0.7 copy-done.8
  95.2 11.1 %score.1 = (f32[2,128,1024]{2,1,0:T(8,128)S(1)}, f32[2,8,1024]{2,1,0:T(8,128)S(1)}, bf16[2,1024,1024]{2,1,0:T(8,128)(2,1)S(1)}, bf16[2,1024,1024]{2,1,0:T(8,128)(2,1)S(1)}) custom-call(s32[2]{0:T(128)S(1)} %copy-done.8, bf16[8,256,256]{2,1,0:T(8,128)(2,1)S(1)} %all-to-all-done.1.q_ref.v_ref, bf16[1024,256]{1,0:T(8,128)(2,1)S(1)} %bitcast.12, ...), custom_call_target="tpu_custom_call" | custom-call | flops 262144 | bytes 262144 | tf_op jit(solution)/shard_map/score/pallas_call | solution.py:71
  106.3 5.9 %collective-permute-done.3.vp_ref = bf16[1024,256]{1,0:T(8,128)(2,1)S(1)} collective-permute-done((bf16[1024,256]{1,0:T(8,128)(2,1)S(1)}, bf16[1024,256]{1,0:T(8,128)(2,1)S(1)}, u32[]{:S(2)}, u32[]{:S(2)}) %collective-permute-start.3) | collective-permute-done | bytes 524320 | tf_op jit(solution)/shard_map/ppermute | solution.py:300
  112.2 2.7 %collective-permute-done.4.vn_ref = bf16[1024,256]{1,0:T(8,128)(2,1)S(1)} collective-permute-done((bf16[1024,256]{1,0:T(8,128)(2,1)S(1)}, bf16[1024,256]{1,0:T(8,128)(2,1)S(1)}, u32[]{:S(2)}, u32[]{:S(2)}) %collective-permute-start.4) | collective-permute-done | bytes 524320 | tf_op jit(solution)/shard_map/ppermute | solution.py:300
  114.9 1.8 %mix.1 = bf16[8,256,128]{2,1,0:T(8,128)(2,1)S(1)} custom-call(bf16[2,1024,1024]{2,1,0:T(8,128)(2,1)S(1)} %get-tuple-element.26.pp_ref, bf16[2,1024,1024]{2,1,0:T(8,128)(2,1)S(1)} %get-tuple-element.27.pn_ref, bf16[1024,256]{1,0:T(8,128)(2,1)S(1)} %collective-permute-done.3.vp_ref, bf16[1024,256]{1,0:T(8,128)(2,1)S(1)} %collective-permute-done.4.vn_ref, ...), custom_call_target="tpu_custom_call" | custom-call | flops 1073741824 | bytes 3670016 | tf_op jit(solution)/shard_map/mix/pallas_call | solution.py:116
  116.6 20.1 %all_to_all.15.ctx_ref = bf16[8,256,128]{2,1,0:T(8,128)(2,1)} all-to-all(bf16[8,256,128]{2,1,0:T(8,128)(2,1)S(1)} %mix.1), channel_id=1, replica_groups=mesh['x'=4,'zh'=2,'y'=8,'zl'=4,'c'=2] {'zl','c'}, dimensions={0} | all-to-all | bytes 1048576 | tf_op jit(solution)/shard_map/all_to_all | solution.py:274
  136.7 5.0 %project.1 = bf16[1600,128]{1,0:T(8,128)(2,1)} custom-call(s32[1]{0:T(128)} %bitcast.mirror_ref, bf16[8,2,200,1024]{3,2,1,0:T(8,128)(2,1)} %bitcast.14, bf16[8,256,128]{2,1,0:T(8,128)(2,1)} %all_to_all.15.ctx_ref), custom_call_target="tpu_custom_call" | custom-call | flops 838860800 | bytes 6553600 | tf_op jit(solution)/shard_map/project/pallas_call | solution.py:164
  (17 shorter events, 0.1 us)
Async XLA Ops:
  6.5 1.0 copy-start.2
  7.6 0.7 copy-start.7
  9.2 24.0 %all-to-all-start = ((bf16[8,144,256]{2,1,0:T(8,128)(2,1)}), bf16[8,144,256]{2,1,0:T(8,128)(2,1)S(1)}, u32[]{:S(2)}, u32[]{:S(2)}) async-start(bf16[8,144,256]{2,1,0:T(8,128)(2,1)} %pack.1), calls=%async_computation | async-start | bytes 1179648 | tf_op jit(solution)/shard_map/all_to_all | solution.py:274
  16.5 1.0 copy-start
  17.5 1.0 copy-start.1
  33.3 22.5 %collective-permute-start.2 = (bf16[32,1024]{1,0:T(8,128)(2,1)S(1)}, bf16[32,1024]{1,0:T(8,128)(2,1)S(1)}, u32[]{:S(2)}, u32[]{:S(2)}) collective-permute-start(bf16[32,1024]{1,0:T(8,128)(2,1)S(1)} %get-tuple-element.21), channel_id=1, source_target_pairs={{0,64},{64,0},{1,65},{65,1},{2,66},{66,2},{3,67},{67,3},{4,68},{68... | collective-permute-start | bytes 196616 | tf_op jit(solution)/shard_map/ppermute | solution.py:317
  42.1 29.8 %collective-permute-start = (bf16[1024,256]{1,0:T(8,128)(2,1)S(1)}, bf16[1024,256]{1,0:T(8,128)(2,1)S(1)}, u32[]{:S(2)}, u32[]{:S(2)}) collective-permute-start(bf16[1024,256]{1,0:T(8,128)(2,1)S(1)} %bitcast.10), channel_id=1, source_target_pairs={{0,8},{1,9},{2,10},{3,11},{4,12},{5,13},{6,14},{7,15},{8,16},{9,17... | collective-permute-start | bytes 1572872 | tf_op jit(solution)/shard_map/ppermute | solution.py:300
  45.6 26.4 %collective-permute-start.1 = (bf16[1024,256]{1,0:T(8,128)(2,1)S(1)}, bf16[1024,256]{1,0:T(8,128)(2,1)S(1)}, u32[]{:S(2)}, u32[]{:S(2)}) collective-permute-start(bf16[1024,256]{1,0:T(8,128)(2,1)S(1)} %bitcast.11), channel_id=1, source_target_pairs={{8,0},{9,1},{10,2},{11,3},{12,4},{13,5},{14,6},{15,7},{16,8},{17,9... | collective-permute-start | bytes 1572872 | tf_op jit(solution)/shard_map/ppermute | solution.py:300
  52.2 30.1 %all-to-all-start.1 = ((bf16[8,256,256]{2,1,0:T(8,128)(2,1)}), bf16[8,256,256]{2,1,0:T(8,128)(2,1)S(1)}, u32[]{:S(2)}, u32[]{:S(2)}) async-start(bf16[8,256,256]{2,1,0:T(8,128)(2,1)} %join_heads.1), calls=%async_computation.1 | async-start | bytes 2097152 | tf_op jit(solution)/shard_map/all_to_all | solution.py:274
  55.8 80.9 %all-gather.4.cloned.1.call-start = ((), (), s32[]{:S(2)}) async-start(), calls=%async_computation.3 | async-start | bytes 6963200 | tf_op jit(solution)/shard_map/all_gather | solution.py:325
  72.0 0.8 copy-start.3
  72.8 0.8 copy-start.5
  82.3 29.8 %collective-permute-start.3 = (bf16[1024,256]{1,0:T(8,128)(2,1)S(1)}, bf16[1024,256]{1,0:T(8,128)(2,1)S(1)}, u32[]{:S(2)}, u32[]{:S(2)}) collective-permute-start(bf16[1024,256]{1,0:T(8,128)(2,1)S(1)} %bitcast.15), channel_id=1, source_target_pairs={{0,8},{1,9},{2,10},{3,11},{4,12},{5,13},{6,14},{7,15},{8,16},{9,17... | collective-permute-start | bytes 1572872 | tf_op jit(solution)/shard_map/ppermute | solution.py:300
  84.3 30.6 %collective-permute-start.4 = (bf16[1024,256]{1,0:T(8,128)(2,1)S(1)}, bf16[1024,256]{1,0:T(8,128)(2,1)S(1)}, u32[]{:S(2)}, u32[]{:S(2)}) collective-permute-start(bf16[1024,256]{1,0:T(8,128)(2,1)S(1)} %bitcast.16), channel_id=1, source_target_pairs={{8,0},{9,1},{10,2},{11,3},{12,4},{13,5},{14,6},{15,7},{16,8},{17,9... | collective-permute-start | bytes 1572872 | tf_op jit(solution)/shard_map/ppermute | solution.py:300
  92.4 1.0 copy-start.4
  93.5 1.0 copy-start.6
  94.5 0.7 copy-start.8
Sparse Core Ops, SparseCore 0:
  82.4 53.7 all-gather.3

commit v13 on v12

--- a/solution.py
+++ b/solution.py
@@ -184,27 +184,41 @@
     return pl.ds(pl.multiple_of((chunk ^ mirror_ref[0]) * width, width), width)
 
 
-def pack_kernel(mirror_ref, k_ref, w_ref, out_ref):
+def pack_kernel(mirror_ref, k_ref, w_ref, out_ref, sems):
     groups, _, width = out_ref.shape
     tok = k_ref.shape[0]
     half = width // 2
     cols = w_ref.shape[0]
+    copies = []
     for g in range(groups):
-        out_ref[g, :tok, :] = k_ref[:, columns(mirror_ref, g, width)]
+        copies.append(
+            pltpu.make_async_copy(
+                k_ref.at[:, columns(mirror_ref, g, width)], out_ref.at[g, pl.ds(0, tok), :], sems.at[g]
+            )
+        )
+        copies[g].start()
+    for g in range(groups):
         part = w_ref[:, (g % 2) * half : (g % 2 + 1) * half]
         out_ref[g, tok:, :half] = part[:EXTRA]
         out_ref[g, tok:, half:] = jnp.concatenate(
             [part[EXTRA:], jnp.zeros((2 * EXTRA - cols, half), part.dtype)], axis=0
         )
+    for copy in copies:
+        copy.wait()
 
 
 def pack(mirror, k, wt):
     tok, width = k.shape[0], wt.shape[1]
     return pl.pallas_call(
         pack_kernel,
-        in_specs=[pl.BlockSpec(memory_space=pltpu.SMEM)] + [pl.BlockSpec(memory_space=pltpu.VMEM)] * 2,
+        in_specs=[
+            pl.BlockSpec(memory_space=pltpu.SMEM),
+            pl.BlockSpec(memory_space=pltpu.HBM),
+            pl.BlockSpec(memory_space=pltpu.VMEM),
+        ],
+        scratch_shapes=[pltpu.SemaphoreType.DMA((8,))],
         out_shape=jax.ShapeDtypeStruct((8, tok + EXTRA, width), k.dtype),
-        compiler_params=pltpu.CompilerParams(vmem_limit_bytes=VMEM),
+        compiler_params=pltpu.CompilerParams(vmem_limit_bytes=60 * 1024 * 1024),
         name="pack",
     )(mirror, k, wt)
 

time: 150 us -> 150 us (level)
  Pallas kernels: 21.9 us -> 23.7 us
  local copies, waits for them, and re-layouts: 8.2 us -> 6.42 us
    pallas_call x1, Pallas kernels: 0.91 us -> 2.69 us  [pack(): pl.pallas_call(pack_kernel, in_specs=[pl.BlockSpec(memory_space=pltpu.SME...]
    unnamed x18 -> x14, local copies, waits for them, and re-layouts: 8.16 us -> 6.39 us
where the time goes in v13:
time: 150 us; the launch traced here: 148 us
  starting transfers between devices  39.2 us (26%)
  blocking collectives  33.9 us (23%)
  waiting for transfers between devices  31.1 us (21%)
  Pallas kernels  23.7 us (16%)
  between operations  13.5 us (9%)
  local copies, waits for them, and re-layouts  6.42 us (4%)
    all_to_all x2, waiting for transfers between devices, to_heads(): return lax.all_to_all(chunks, HEAD, split_axis=0, concat_axis=0)  21.1 us
    ppermute x4, starting transfers between devices, to_block(): return lax.ppermute(value, AXES, pairs)  20.1 us
    all_to_all x1, blocking collectives, to_heads(): return lax.all_to_all(chunks, HEAD, split_axis=0, concat_axis=0)  20.1 us
    all_gather x1, blocking collectives, local(): line = tighten(lax.all_gather(pair, 'x'), cols)  13.8 us
    pallas_call x1, Pallas kernels, score(): pl.pallas_call(score_kernel, grid=(heads,), in_specs=[pl.BlockSpec(memory...  11.1 us
    all_to_all x2, starting transfers between devices, to_heads(): return lax.all_to_all(chunks, HEAD, split_axis=0, concat_axis=0)  10.8 us
    ppermute x4, waiting for transfers between devices, to_block(): return lax.ppermute(value, AXES, pairs)  9.98 us
    ppermute x1, starting transfers between devices, local(): other = lax.ppermute(w_rows, 'zh', [(0, 1), (1, 0)])  8.22 us
  transfers between devices with their start and end apart: 8, of which 5 were waited for; matrix products, arithmetic and copies ran while one was open for 0% of the time, Pallas kernels for 11%

profile of v13, /device:TPU:6, one launch (start us, length us, event | category | flops | bytes accessed | tf_op | source)
XLA Modules:
  0.0 148.5 jit_solution(4849143733949097989)
XLA Ops:
  6.5 2.7 %pack.1 = bf16[8,144,256]{2,1,0:T(8,128)(2,1)} custom-call(s32[1]{0:T(128)} %bitcast.mirror_ref, bf16[128,2048]{1,0:T(8,128)(2,1)} %k_ref.1, bf16[25,256]{1,0:T(8,128)(2,1)} %bitcast.16), custom_call_target="tpu_custom_call" | custom-call | tf_op jit(solution)/shard_map/pack/pallas_call | solution.py:212
  9.2 7.3 %all-to-all-start = ((bf16[8,144,256]{2,1,0:T(8,128)(2,1)}), bf16[8,144,256]{2,1,0:T(8,128)(2,1)S(1)}, u32[]{:S(2)}, u32[]{:S(2)}) async-start(bf16[8,144,256]{2,1,0:T(8,128)(2,1)} %pack.1), calls=%async_computation | async-start | bytes 1179648 | tf_op jit(solution)/shard_map/all_to_all | solution.py:288
  16.5 1.0 copy-done
  17.6 1.0 copy-done.1
  18.6 1.1 join_heads.1
  19.7 13.6 %all-to-all-done.in_ref = bf16[8,144,256]{2,1,0:T(8,128)(2,1)S(1)} async-done(((bf16[8,144,256]{2,1,0:T(8,128)(2,1)}), bf16[8,144,256]{2,1,0:T(8,128)(2,1)S(1)}, u32[]{:S(2)}, u32[]{:S(2)}) %all-to-all-start) | async-done | bytes 589856 | tf_op jit(solution)/shard_map/all_to_all | solution.py:288
  33.3 8.2 %collective-permute-start.2 = (bf16[32,1024]{1,0:T(8,128)(2,1)S(1)}, bf16[32,1024]{1,0:T(8,128)(2,1)S(1)}, u32[]{:S(2)}, u32[]{:S(2)}) collective-permute-start(bf16[32,1024]{1,0:T(8,128)(2,1)S(1)} %get-tuple-element.21), channel_id=1, source_target_pairs={{0,64},{64,0},{1,65},{65,1},{2,66},{66,2},{3,67},{67,3},{4,68},{68... | collective-permute-start | bytes 196616 | tf_op jit(solution)/shard_map/ppermute | solution.py:331
  41.6 0.6 add_convert_fusion.ok_ref
  42.1 3.5 %collective-permute-start = (bf16[1024,256]{1,0:T(8,128)(2,1)S(1)}, bf16[1024,256]{1,0:T(8,128)(2,1)S(1)}, u32[]{:S(2)}, u32[]{:S(2)}) collective-permute-start(bf16[1024,256]{1,0:T(8,128)(2,1)S(1)} %bitcast.10), channel_id=1, source_target_pairs={{0,8},{1,9},{2,10},{3,11},{4,12},{5,13},{6,14},{7,15},{8,16},{9,17... | collective-permute-start | bytes 1572872 | tf_op jit(solution)/shard_map/ppermute | solution.py:314
  45.6 6.6 %collective-permute-start.1 = (bf16[1024,256]{1,0:T(8,128)(2,1)S(1)}, bf16[1024,256]{1,0:T(8,128)(2,1)S(1)}, u32[]{:S(2)}, u32[]{:S(2)}) collective-permute-start(bf16[1024,256]{1,0:T(8,128)(2,1)S(1)} %bitcast.11), channel_id=1, source_target_pairs={{8,0},{9,1},{10,2},{11,3},{12,4},{13,5},{14,6},{15,7},{16,8},{17,9... | collective-permute-start | bytes 1572872 | tf_op jit(solution)/shard_map/ppermute | solution.py:314
  52.2 3.6 %all-to-all-start.1 = ((bf16[8,256,256]{2,1,0:T(8,128)(2,1)}), bf16[8,256,256]{2,1,0:T(8,128)(2,1)S(1)}, u32[]{:S(2)}, u32[]{:S(2)}) async-start(bf16[8,256,256]{2,1,0:T(8,128)(2,1)} %join_heads.1), calls=%async_computation.1 | async-start | bytes 2097152 | tf_op jit(solution)/shard_map/all_to_all | solution.py:288
  55.7 0.0 all-gather.4.cloned.1.call-start
  55.8 0.0 collective-permute-done.2
  55.9 13.8 %all-gather = bf16[256,1024]{1,0:T(8,128)(2,1)S(1)} all-gather(bf16[64,1024]{1,0:T(8,128)(2,1)S(1)} %pad_maximum_fusion), channel_id=2, replica_groups=mesh['x'=4,'zh'=2,'y'=8,'zl'=4,'c'=2] {'x'}, dimensions={0}, use_global_device_ids=true | all-gather | bytes 655360 | tf_op jit(solution)/shard_map/all_gather | solution.py:333
  69.7 0.9 tighten.1
  70.5 1.4 collective-permute-done.kp_ref
  71.9 0.8 copy-done.2
  72.7 0.8 copy-done.4
  73.5 1.2 behind.1.ok_ref
  74.7 7.6 %all-to-all-done.1.q_ref.v_ref = bf16[8,256,256]{2,1,0:T(8,128)(2,1)S(1)} async-done(((bf16[8,256,256]{2,1,0:T(8,128)(2,1)}), bf16[8,256,256]{2,1,0:T(8,128)(2,1)S(1)}, u32[]{:S(2)}, u32[]{:S(2)}) %all-to-all-start.1) | async-done | bytes 1048608 | tf_op jit(solution)/shard_map/all_to_all | solution.py:288
  82.3 0.0 all-gather.4.cloned.1.call-update
  82.3 1.9 %collective-permute-start.3 = (bf16[1024,256]{1,0:T(8,128)(2,1)S(1)}, bf16[1024,256]{1,0:T(8,128)(2,1)S(1)}, u32[]{:S(2)}, u32[]{:S(2)}) collective-permute-start(bf16[1024,256]{1,0:T(8,128)(2,1)S(1)} %bitcast.14), channel_id=1, source_target_pairs={{0,8},{1,9},{2,10},{3,11},{4,12},{5,13},{6,14},{7,15},{8,16},{9,17... | collective-permute-start | bytes 1572872 | tf_op jit(solution)/shard_map/ppermute | solution.py:314
  84.3 8.1 %collective-permute-start.4 = (bf16[1024,256]{1,0:T(8,128)(2,1)S(1)}, bf16[1024,256]{1,0:T(8,128)(2,1)S(1)}, u32[]{:S(2)}, u32[]{:S(2)}) collective-permute-start(bf16[1024,256]{1,0:T(8,128)(2,1)S(1)} %bitcast.15), channel_id=1, source_target_pairs={{8,0},{9,1},{10,2},{11,3},{12,4},{13,5},{14,6},{15,7},{16,8},{17,9... | collective-permute-start | bytes 1572872 | tf_op jit(solution)/shard_map/ppermute | solution.py:314
  92.4 1.0 copy-done.3
  93.5 1.0 copy-done.5
  94.5 0.7 copy-done.6
  95.2 11.1 %score.1 = (f32[2,128,1024]{2,1,0:T(8,128)S(1)}, f32[2,8,1024]{2,1,0:T(8,128)S(1)}, bf16[2,1024,1024]{2,1,0:T(8,128)(2,1)S(1)}, bf16[2,1024,1024]{2,1,0:T(8,128)(2,1)S(1)}) custom-call(s32[2]{0:T(128)S(1)} %copy-done.6, bf16[8,256,256]{2,1,0:T(8,128)(2,1)S(1)} %all-to-all-done.1.q_ref.v_ref, bf16[1024,256]{1,0:T(8,128)(2,1)S(1)} %bitcast.12, ...), custom_call_target="tpu_custom_call" | custom-call | flops 262144 | bytes 262144 | tf_op jit(solution)/shard_map/score/pallas_call | solution.py:71
  106.3 5.9 %collective-permute-done.3.vp_ref = bf16[1024,256]{1,0:T(8,128)(2,1)S(1)} collective-permute-done((bf16[1024,256]{1,0:T(8,128)(2,1)S(1)}, bf16[1024,256]{1,0:T(8,128)(2,1)S(1)}, u32[]{:S(2)}, u32[]{:S(2)}) %collective-permute-start.3) | collective-permute-done | bytes 524320 | tf_op jit(solution)/shard_map/ppermute | solution.py:314
  112.1 2.7 %collective-permute-done.4.vn_ref = bf16[1024,256]{1,0:T(8,128)(2,1)S(1)} collective-permute-done((bf16[1024,256]{1,0:T(8,128)(2,1)S(1)}, bf16[1024,256]{1,0:T(8,128)(2,1)S(1)}, u32[]{:S(2)}, u32[]{:S(2)}) %collective-permute-start.4) | collective-permute-done | bytes 524320 | tf_op jit(solution)/shard_map/ppermute | solution.py:314
  114.8 1.8 %mix.1 = bf16[8,256,128]{2,1,0:T(8,128)(2,1)S(1)} custom-call(bf16[2,1024,1024]{2,1,0:T(8,128)(2,1)S(1)} %get-tuple-element.26.pp_ref, bf16[2,1024,1024]{2,1,0:T(8,128)(2,1)S(1)} %get-tuple-element.27.pn_ref, bf16[1024,256]{1,0:T(8,128)(2,1)S(1)} %collective-permute-done.3.vp_ref, bf16[1024,256]{1,0:T(8,128)(2,1)S(1)} %collective-permute-done.4.vn_ref, ...), custom_call_target="tpu_custom_call" | custom-call | flops 1073741824 | bytes 3670016 | tf_op jit(solution)/shard_map/mix/pallas_call | solution.py:116
  116.6 20.1 %all_to_all.15.ctx_ref = bf16[8,256,128]{2,1,0:T(8,128)(2,1)} all-to-all(bf16[8,256,128]{2,1,0:T(8,128)(2,1)S(1)} %mix.1), channel_id=1, replica_groups=mesh['x'=4,'zh'=2,'y'=8,'zl'=4,'c'=2] {'zl','c'}, dimensions={0} | all-to-all | bytes 1048576 | tf_op jit(solution)/shard_map/all_to_all | solution.py:288
  136.7 5.0 %project.1 = bf16[1600,128]{1,0:T(8,128)(2,1)} custom-call(s32[1]{0:T(128)} %bitcast.mirror_ref, bf16[8,2,200,1024]{3,2,1,0:T(8,128)(2,1)} %bitcast.13, bf16[8,256,128]{2,1,0:T(8,128)(2,1)} %all_to_all.15.ctx_ref), custom_call_target="tpu_custom_call" | custom-call | flops 838860800 | bytes 6553600 | tf_op jit(solution)/shard_map/project/pallas_call | solution.py:164
  (13 shorter events, 0.1 us)
Async XLA Ops:
  9.2 24.0 %all-to-all-start = ((bf16[8,144,256]{2,1,0:T(8,128)(2,1)}), bf16[8,144,256]{2,1,0:T(8,128)(2,1)S(1)}, u32[]{:S(2)}, u32[]{:S(2)}) async-start(bf16[8,144,256]{2,1,0:T(8,128)(2,1)} %pack.1), calls=%async_computation | async-start | bytes 1179648 | tf_op jit(solution)/shard_map/all_to_all | solution.py:288
  16.5 1.0 copy-start
  17.6 1.0 copy-start.1
  33.3 22.5 %collective-permute-start.2 = (bf16[32,1024]{1,0:T(8,128)(2,1)S(1)}, bf16[32,1024]{1,0:T(8,128)(2,1)S(1)}, u32[]{:S(2)}, u32[]{:S(2)}) collective-permute-start(bf16[32,1024]{1,0:T(8,128)(2,1)S(1)} %get-tuple-element.21), channel_id=1, source_target_pairs={{0,64},{64,0},{1,65},{65,1},{2,66},{66,2},{3,67},{67,3},{4,68},{68... | collective-permute-start | bytes 196616 | tf_op jit(solution)/shard_map/ppermute | solution.py:331
  42.1 29.8 %collective-permute-start = (bf16[1024,256]{1,0:T(8,128)(2,1)S(1)}, bf16[1024,256]{1,0:T(8,128)(2,1)S(1)}, u32[]{:S(2)}, u32[]{:S(2)}) collective-permute-start(bf16[1024,256]{1,0:T(8,128)(2,1)S(1)} %bitcast.10), channel_id=1, source_target_pairs={{0,8},{1,9},{2,10},{3,11},{4,12},{5,13},{6,14},{7,15},{8,16},{9,17... | collective-permute-start | bytes 1572872 | tf_op jit(solution)/shard_map/ppermute | solution.py:314
  45.6 26.4 %collective-permute-start.1 = (bf16[1024,256]{1,0:T(8,128)(2,1)S(1)}, bf16[1024,256]{1,0:T(8,128)(2,1)S(1)}, u32[]{:S(2)}, u32[]{:S(2)}) collective-permute-start(bf16[1024,256]{1,0:T(8,128)(2,1)S(1)} %bitcast.11), channel_id=1, source_target_pairs={{8,0},{9,1},{10,2},{11,3},{12,4},{13,5},{14,6},{15,7},{16,8},{17,9... | collective-permute-start | bytes 1572872 | tf_op jit(solution)/shard_map/ppermute | solution.py:314
  52.2 30.1 %all-to-all-start.1 = ((bf16[8,256,256]{2,1,0:T(8,128)(2,1)}), bf16[8,256,256]{2,1,0:T(8,128)(2,1)S(1)}, u32[]{:S(2)}, u32[]{:S(2)}) async-start(bf16[8,256,256]{2,1,0:T(8,128)(2,1)} %join_heads.1), calls=%async_computation.1 | async-start | bytes 2097152 | tf_op jit(solution)/shard_map/all_to_all | solution.py:288
  55.7 80.9 %all-gather.4.cloned.1.call-start = ((), (), s32[]{:S(2)}) async-start(), calls=%async_computation.3 | async-start | bytes 6963200 | tf_op jit(solution)/shard_map/all_gather | solution.py:339
  71.9 0.8 copy-start.2
  72.7 0.8 copy-start.4
  82.3 29.8 %collective-permute-start.3 = (bf16[1024,256]{1,0:T(8,128)(2,1)S(1)}, bf16[1024,256]{1,0:T(8,128)(2,1)S(1)}, u32[]{:S(2)}, u32[]{:S(2)}) collective-permute-start(bf16[1024,256]{1,0:T(8,128)(2,1)S(1)} %bitcast.14), channel_id=1, source_target_pairs={{0,8},{1,9},{2,10},{3,11},{4,12},{5,13},{6,14},{7,15},{8,16},{9,17... | collective-permute-start | bytes 1572872 | tf_op jit(solution)/shard_map/ppermute | solution.py:314
  84.3 30.6 %collective-permute-start.4 = (bf16[1024,256]{1,0:T(8,128)(2,1)S(1)}, bf16[1024,256]{1,0:T(8,128)(2,1)S(1)}, u32[]{:S(2)}, u32[]{:S(2)}) collective-permute-start(bf16[1024,256]{1,0:T(8,128)(2,1)S(1)} %bitcast.15), channel_id=1, source_target_pairs={{8,0},{9,1},{10,2},{11,3},{12,4},{13,5},{14,6},{15,7},{16,8},{17,9... | collective-permute-start | bytes 1572872 | tf_op jit(solution)/shard_map/ppermute | solution.py:314
  92.4 1.0 copy-start.3
  93.5 1.0 copy-start.5
  94.5 0.7 copy-start.6
Sparse Core Ops, SparseCore 0:
  82.4 53.7 all-gather.3

commit v14 on v12

--- a/solution.py
+++ b/solution.py
@@ -19,7 +19,7 @@
 MIX_TILE = 1024
 CHUNK = 256
 PROJECT_STEP = 4
-HINT = 28_750_000_000
+HINT = 4_600_000_000
 PROJECT_VMEM = 56 * 1024 * 1024
 DIMS_NT = (((1,), (1,)), ((), ()))
 DIMS_TN = (((0,), (0,)), ((), ()))
@@ -312,9 +312,9 @@
     k = k.reshape(8 * tok, -1)
 
     kp, kn = to_block(k, 1), to_block(k, -1)
-    vq, k = lax.optimization_barrier((joined, k))
+    other = lax.ppermute(w_rows, "zh", [(0, 1), (1, 0)])
+    vq, other = lax.optimization_barrier((joined, other))
     vq = to_heads(vq)
-    other = lax.ppermute(w_rows, "zh", [(0, 1), (1, 0)])
     pair = jnp.concatenate([jnp.where(first, w_rows, other), jnp.where(first, other, w_rows)])
     line = tighten(lax.all_gather(pair, "x"), cols)
     ok = behind(ok, kp, kn)

time: 150 us -> 152 us (1.013)
  blocking collectives: 33.9 us -> 60.4 us
  waiting for transfers between devices: 31.1 us -> 11.8 us
  starting transfers between devices: 39.2 us -> 34.2 us
    all_to_all x1 -> x2, blocking collectives: 20.1 us -> 46.5 us  [to_heads(): return lax.all_to_all(chunks, HEAD, split_axis=0, concat_axis=0)]
    all_to_all x2 -> x1, waiting for transfers between devices: 21.1 us -> 0.01 us  [to_heads(): return lax.all_to_all(chunks, HEAD, split_axis=0, concat_axis=0)]
    all_to_all x2 -> x1, starting transfers between devices: 10.8 us -> 3.56 us  [to_heads(): return lax.all_to_all(chunks, HEAD, split_axis=0, concat_axis=0)]
    ppermute x4, starting transfers between devices: 20.1 us -> 22.4 us  [to_block(): return lax.ppermute(value, AXES, pairs)]
    ppermute x4, waiting for transfers between devices: 10 us -> 11.7 us  [to_block(): return lax.ppermute(value, AXES, pairs)]
  transfers between devices with their start and end apart: 8 -> 7, of which waited for: 5 -> 3; matrix products, arithmetic and copies ran while one was open for 0% -> 0% of each run, Pallas kernels for 11% -> 11%
where the time goes in v14:
time: 152 us; the launch traced here: 150 us
  blocking collectives  60.4 us (40%)
  starting transfers between devices  34.2 us (23%)
  Pallas kernels  21.1 us (14%)
  between operations  13.6 us (9%)
  waiting for transfers between devices  11.8 us (8%)
  local copies, waits for them, and re-layouts  8.18 us (5%)
    all_to_all x2, blocking collectives, to_heads(): return lax.all_to_all(chunks, HEAD, split_axis=0, concat_axis=0)  46.5 us
    ppermute x4, starting transfers between devices, to_block(): return lax.ppermute(value, AXES, pairs)  22.4 us
    all_gather x1, blocking collectives, local(): line = tighten(lax.all_gather(pair, 'x'), cols)  13.8 us
    ppermute x4, waiting for transfers between devices, to_block(): return lax.ppermute(value, AXES, pairs)  11.7 us
    pallas_call x1, Pallas kernels, score(): pl.pallas_call(score_kernel, grid=(heads,), in_specs=[pl.BlockSpec(memory...  11.1 us
    ppermute x1, starting transfers between devices, local(): other = lax.ppermute(w_rows, 'zh', [(0, 1), (1, 0)])  8.22 us
    unnamed x18, local copies, waits for them, and re-layouts  8.15 us
    pallas_call x1, Pallas kernels, project(): pl.pallas_call(functools.partial(project_kernel, cols), grid=(count // st...  4.96 us
  transfers between devices with their start and end apart: 7, of which 3 were waited for; matrix products, arithmetic and copies ran while one was open for 0% of the time, Pallas kernels for 11%

profile of v14, /device:TPU:6, one launch (start us, length us, event | category | flops | bytes accessed | tf_op | source)
XLA Modules:
  0.0 149.8 jit_solution(17725520253269262093)
XLA Ops:
  6.5 1.0 copy-done.2
  7.6 0.7 copy-done.7
  8.3 0.1 pack.1
  8.4 23.8 %all_to_all.15.in_ref = bf16[8,144,256]{2,1,0:T(8,128)(2,1)S(1)} all-to-all(bf16[8,144,256]{2,1,0:T(8,128)(2,1)S(1)} %pack.1), channel_id=1, replica_groups=mesh['x'=4,'zh'=2,'y'=8,'zl'=4,'c'=2] {'zl','c'}, dimensions={0} | all-to-all | bytes 1179648 | tf_op jit(solution)/shard_map/all_to_all | solution.py:274
  32.2 8.2 %collective-permute-start.2 = (bf16[32,1024]{1,0:T(8,128)(2,1)S(1)}, bf16[32,1024]{1,0:T(8,128)(2,1)S(1)}, u32[]{:S(2)}, u32[]{:S(2)}) collective-permute-start(bf16[32,1024]{1,0:T(8,128)(2,1)S(1)} %get-tuple-element.20), channel_id=1, source_target_pairs={{0,64},{64,0},{1,65},{65,1},{2,66},{66,2},{3,67},{67,3},{4,68},{68... | collective-permute-start | bytes 196616 | tf_op jit(solution)/shard_map/ppermute | solution.py:315
  40.5 0.0 copy-start
  40.5 1.0 copy-done
  41.5 1.0 copy-done.1
  42.6 1.1 join_heads.1
  43.7 3.6 %all-to-all-start.1 = ((bf16[8,256,256]{2,1,0:T(8,128)(2,1)}), bf16[8,256,256]{2,1,0:T(8,128)(2,1)S(1)}, u32[]{:S(2)}, u32[]{:S(2)}) async-start(bf16[8,256,256]{2,1,0:T(8,128)(2,1)} %join_heads.1), calls=%async_computation.1 | async-start | bytes 2097152 | tf_op jit(solution)/shard_map/all_to_all | solution.py:274
  47.3 0.0 all-gather.4.cloned.1.call-start
  47.3 0.6 add_convert_fusion.ok_ref
  47.9 3.5 %collective-permute-start = (bf16[1024,256]{1,0:T(8,128)(2,1)S(1)}, bf16[1024,256]{1,0:T(8,128)(2,1)S(1)}, u32[]{:S(2)}, u32[]{:S(2)}) collective-permute-start(bf16[1024,256]{1,0:T(8,128)(2,1)S(1)} %bitcast.10), channel_id=1, source_target_pairs={{0,8},{1,9},{2,10},{3,11},{4,12},{5,13},{6,14},{7,15},{8,16},{9,17... | collective-permute-start | bytes 1572872 | tf_op jit(solution)/shard_map/ppermute | solution.py:300
  51.4 8.9 %collective-permute-start.1 = (bf16[1024,256]{1,0:T(8,128)(2,1)S(1)}, bf16[1024,256]{1,0:T(8,128)(2,1)S(1)}, u32[]{:S(2)}, u32[]{:S(2)}) collective-permute-start(bf16[1024,256]{1,0:T(8,128)(2,1)S(1)} %bitcast.11), channel_id=1, source_target_pairs={{8,0},{9,1},{10,2},{11,3},{12,4},{13,5},{14,6},{15,7},{16,8},{17,9... | collective-permute-start | bytes 1572872 | tf_op jit(solution)/shard_map/ppermute | solution.py:300
  60.3 13.8 %all-gather = bf16[256,1024]{1,0:T(8,128)(2,1)S(1)} all-gather(bf16[64,1024]{1,0:T(8,128)(2,1)S(1)} %pad_maximum_fusion), channel_id=2, replica_groups=mesh['x'=4,'zh'=2,'y'=8,'zl'=4,'c'=2] {'x'}, dimensions={0}, use_global_device_ids=true | all-gather | bytes 655360 | tf_op jit(solution)/shard_map/all_gather | solution.py:319
  74.1 0.9 tighten.1
  75.0 6.1 %collective-permute-done.kp_ref = bf16[1024,256]{1,0:T(8,128)(2,1)S(1)} collective-permute-done((bf16[1024,256]{1,0:T(8,128)(2,1)S(1)}, bf16[1024,256]{1,0:T(8,128)(2,1)S(1)}, u32[]{:S(2)}, u32[]{:S(2)}) %collective-permute-start) | collective-permute-done | bytes 524320 | tf_op jit(solution)/shard_map/ppermute | solution.py:300
  81.1 0.8 copy-done.3
  81.9 0.8 copy-done.5
  82.7 1.2 behind.1.ok_ref
  83.9 0.0 all-gather.4.cloned.1.call-update
  83.9 1.9 %collective-permute-start.3 = (bf16[1024,256]{1,0:T(8,128)(2,1)S(1)}, bf16[1024,256]{1,0:T(8,128)(2,1)S(1)}, u32[]{:S(2)}, u32[]{:S(2)}) collective-permute-start(bf16[1024,256]{1,0:T(8,128)(2,1)S(1)} %bitcast.15), channel_id=1, source_target_pairs={{0,8},{1,9},{2,10},{3,11},{4,12},{5,13},{6,14},{7,15},{8,16},{9,17... | collective-permute-start | bytes 1572872 | tf_op jit(solution)/shard_map/ppermute | solution.py:300
  85.9 8.1 %collective-permute-start.4 = (bf16[1024,256]{1,0:T(8,128)(2,1)S(1)}, bf16[1024,256]{1,0:T(8,128)(2,1)S(1)}, u32[]{:S(2)}, u32[]{:S(2)}) collective-permute-start(bf16[1024,256]{1,0:T(8,128)(2,1)S(1)} %bitcast.16), channel_id=1, source_target_pairs={{8,0},{9,1},{10,2},{11,3},{12,4},{13,5},{14,6},{15,7},{16,8},{17,9... | collective-permute-start | bytes 1572872 | tf_op jit(solution)/shard_map/ppermute | solution.py:300
  94.0 1.0 copy-done.4
  95.1 1.0 copy-done.6
  96.1 0.7 copy-done.8
  96.8 11.1 %score.1 = (f32[2,128,1024]{2,1,0:T(8,128)S(1)}, f32[2,8,1024]{2,1,0:T(8,128)S(1)}, bf16[2,1024,1024]{2,1,0:T(8,128)(2,1)S(1)}, bf16[2,1024,1024]{2,1,0:T(8,128)(2,1)S(1)}) custom-call(s32[2]{0:T(128)S(1)} %copy-done.8, bf16[8,256,256]{2,1,0:T(8,128)(2,1)S(1)} %all-to-all-done.1.q_ref.v_ref, bf16[1024,256]{1,0:T(8,128)(2,1)S(1)} %bitcast.12, ...), custom_call_target="tpu_custom_call" | custom-call | flops 262144 | bytes 262144 | tf_op jit(solution)/shard_map/score/pallas_call | solution.py:71
  107.8 4.1 %collective-permute-done.3.vp_ref = bf16[1024,256]{1,0:T(8,128)(2,1)S(1)} collective-permute-done((bf16[1024,256]{1,0:T(8,128)(2,1)S(1)}, bf16[1024,256]{1,0:T(8,128)(2,1)S(1)}, u32[]{:S(2)}, u32[]{:S(2)}) %collective-permute-start.3) | collective-permute-done | bytes 524320 | tf_op jit(solution)/shard_map/ppermute | solution.py:300
  112.0 1.5 collective-permute-done.4.vn_ref
  113.5 1.8 %mix.1 = bf16[8,256,128]{2,1,0:T(8,128)(2,1)S(1)} custom-call(bf16[2,1024,1024]{2,1,0:T(8,128)(2,1)S(1)} %get-tuple-element.26.pp_ref, bf16[2,1024,1024]{2,1,0:T(8,128)(2,1)S(1)} %get-tuple-element.27.pn_ref, bf16[1024,256]{1,0:T(8,128)(2,1)S(1)} %collective-permute-done.3.vp_ref, bf16[1024,256]{1,0:T(8,128)(2,1)S(1)} %collective-permute-done.4.vn_ref, ...), custom_call_target="tpu_custom_call" | custom-call | flops 1073741824 | bytes 3670016 | tf_op jit(solution)/shard_map/mix/pallas_call | solution.py:116
  115.3 22.7 %all_to_all.16.ctx_ref = bf16[8,256,128]{2,1,0:T(8,128)(2,1)} all-to-all(bf16[8,256,128]{2,1,0:T(8,128)(2,1)S(1)} %mix.1), channel_id=1, replica_groups=mesh['x'=4,'zh'=2,'y'=8,'zl'=4,'c'=2] {'zl','c'}, dimensions={0} | all-to-all | bytes 1048576 | tf_op jit(solution)/shard_map/all_to_all | solution.py:274
  138.0 5.0 %project.1 = bf16[1600,128]{1,0:T(8,128)(2,1)} custom-call(s32[1]{0:T(128)} %bitcast.mirror_ref, bf16[8,2,200,1024]{3,2,1,0:T(8,128)(2,1)} %bitcast.14, bf16[8,256,128]{2,1,0:T(8,128)(2,1)} %all_to_all.16.ctx_ref), custom_call_target="tpu_custom_call" | custom-call | flops 838860800 | bytes 6553600 | tf_op jit(solution)/shard_map/project/pallas_call | solution.py:164
  (16 shorter events, 0.1 us)
Async XLA Ops:
  6.5 1.0 copy-start.2
  7.6 0.7 copy-start.7
  32.2 11.4 %collective-permute-start.2 = (bf16[32,1024]{1,0:T(8,128)(2,1)S(1)}, bf16[32,1024]{1,0:T(8,128)(2,1)S(1)}, u32[]{:S(2)}, u32[]{:S(2)}) collective-permute-start(bf16[32,1024]{1,0:T(8,128)(2,1)S(1)} %get-tuple-element.20), channel_id=1, source_target_pairs={{0,64},{64,0},{1,65},{65,1},{2,66},{66,2},{3,67},{67,3},{4,68},{68... | collective-permute-start | bytes 196616 | tf_op jit(solution)/shard_map/ppermute | solution.py:315
  40.5 1.0 copy-start
  41.5 1.0 copy-start.1
  43.7 40.2 %all-to-all-start.1 = ((bf16[8,256,256]{2,1,0:T(8,128)(2,1)}), bf16[8,256,256]{2,1,0:T(8,128)(2,1)S(1)}, u32[]{:S(2)}, u32[]{:S(2)}) async-start(bf16[8,256,256]{2,1,0:T(8,128)(2,1)} %join_heads.1), calls=%async_computation.1 | async-start | bytes 2097152 | tf_op jit(solution)/shard_map/all_to_all | solution.py:274
  47.3 90.7 %all-gather.4.cloned.1.call-start = ((), (), s32[]{:S(2)}) async-start(), calls=%async_computation.3 | async-start | bytes 6963200 | tf_op jit(solution)/shard_map/all_gather | solution.py:325
  47.9 33.2 %collective-permute-start = (bf16[1024,256]{1,0:T(8,128)(2,1)S(1)}, bf16[1024,256]{1,0:T(8,128)(2,1)S(1)}, u32[]{:S(2)}, u32[]{:S(2)}) collective-permute-start(bf16[1024,256]{1,0:T(8,128)(2,1)S(1)} %bitcast.10), channel_id=1, source_target_pairs={{0,8},{1,9},{2,10},{3,11},{4,12},{5,13},{6,14},{7,15},{8,16},{9,17... | collective-permute-start | bytes 1572872 | tf_op jit(solution)/shard_map/ppermute | solution.py:300
  51.4 29.7 %collective-permute-start.1 = (bf16[1024,256]{1,0:T(8,128)(2,1)S(1)}, bf16[1024,256]{1,0:T(8,128)(2,1)S(1)}, u32[]{:S(2)}, u32[]{:S(2)}) collective-permute-start(bf16[1024,256]{1,0:T(8,128)(2,1)S(1)} %bitcast.11), channel_id=1, source_target_pairs={{8,0},{9,1},{10,2},{11,3},{12,4},{13,5},{14,6},{15,7},{16,8},{17,9... | collective-permute-start | bytes 1572872 | tf_op jit(solution)/shard_map/ppermute | solution.py:300
  81.1 0.8 copy-start.3
  81.9 0.8 copy-start.5
  83.9 28.1 %collective-permute-start.3 = (bf16[1024,256]{1,0:T(8,128)(2,1)S(1)}, bf16[1024,256]{1,0:T(8,128)(2,1)S(1)}, u32[]{:S(2)}, u32[]{:S(2)}) collective-permute-start(bf16[1024,256]{1,0:T(8,128)(2,1)S(1)} %bitcast.15), channel_id=1, source_target_pairs={{0,8},{1,9},{2,10},{3,11},{4,12},{5,13},{6,14},{7,15},{8,16},{9,17... | collective-permute-start | bytes 1572872 | tf_op jit(solution)/shard_map/ppermute | solution.py:300
  85.9 27.6 %collective-permute-start.4 = (bf16[1024,256]{1,0:T(8,128)(2,1)S(1)}, bf16[1024,256]{1,0:T(8,128)(2,1)S(1)}, u32[]{:S(2)}, u32[]{:S(2)}) collective-permute-start(bf16[1024,256]{1,0:T(8,128)(2,1)S(1)} %bitcast.16), channel_id=1, source_target_pairs={{8,0},{9,1},{10,2},{11,3},{12,4},{13,5},{14,6},{15,7},{16,8},{17,9... | collective-permute-start | bytes 1572872 | tf_op jit(solution)/shard_map/ppermute | solution.py:300
  94.0 1.0 copy-start.4
  95.0 1.0 copy-start.6
  96.1 0.7 copy-start.8
Sparse Core Ops, SparseCore 0:
  84.0 52.9 all-gather.3
